TPU v7x, 512 devices: a whole 4x8x8 slice. The times are simulated.
512 devices in a mesh: space: 32 (over y, z_lo), mode: 16 (over x, z_hi, core).
Axes of the slice: x: 4, y: 8, z: 8 (z_hi: 2, z_lo: 4; z = z_hi * 4 + z_lo), core: 2. Of those that a mesh axis runs over, the one named last changes fastest.
Arguments:
- old_modes: bfloat16 [512, 64, 4096], P('mode', None, 'space'), as said below
- new_modes: bfloat16 [512, 64, 4096], P('mode', None, 'space'), as said below
- material: int32 [64, 4096], P(None, 'space'), may hold values from 0 to 11
- density: float32 [12], replicated, may hold values from 0.5 to 2
- memb_x: bfloat16 [12], replicated, may hold values from 1 to 4
- memb_y: bfloat16 [12], replicated, may hold values from 1 to 4
- bend_table: float32 [12], replicated, may hold values from 0.02 to 0.1
Outputs:
- cross_mass: float32 [512, 512], P(None, 'mode')
- cross_membrane: float32 [512, 512], P(None, 'mode')
- cross_bending: float32 [512, 512], P(None, 'mode')
- mass_image: bfloat16 [512, 64, 4096], P('mode', None, 'space')
- stiff_image: bfloat16 [512, 64, 4096], P('mode', None, 'space')
Inputs may be any that keep to these rules, and one draw needn't show every extreme that they name: `old_modes`: A value of one mode shape at one cell. `new_modes`: A value of one mode shape at one cell.
All inputs are finite; a program needn't handle non-finite values.
Results may differ from a plain program's by a relative error of at most 0.0015.
Values may be sent and summed in bfloat16 or wider, within the bound.
No kernel may reach another device: no remote copies, remote signals or barrier semaphores. Data moves between devices by JAX's collectives and lax.ppermute only.
A program may use at most 64 MiB of HBM per device.

v0:
```python
import jax
import jax.numpy as jnp
from jax import lax
from jax.sharding import PartitionSpec as P


def extended(shard, sides, width):
    for axis, dim in sides:
        devices, length = (lax.axis_size(axis), shard.shape[dim])
        up = [(i, (i + 1) % devices) for i in range(devices - 1)]
        down = [(j, i) for i, j in up]
        last = lax.slice_in_dim(shard, length - width, length, axis=dim)
        initial = lax.slice_in_dim(shard, 0, width, axis=dim)
        before = lax.ppermute(last, axis, up)
        after = lax.ppermute(initial, axis, down)
        shard = jnp.concatenate([before, shard, after], axis=dim)
    return shard


def passed_along(value, axis, steps):
    count = lax.axis_size(axis)
    pairs = [(source, (source + steps) % count) for source in range(count)]
    return lax.ppermute(value, axis, pairs)


def lookup(material, table):
    levels = jnp.arange(table.shape[0], dtype=jnp.int32)
    picks = (material[None, :, :] == levels[:, None, None]).astype(jnp.float32)
    return jnp.sum(picks * table.astype(jnp.float32)[:, None, None], axis=0)


def operators(padded, kxp, kyp, density_field, bend_field, rows, cols):

    def moved(a, b):
        return padded[:, 2 + a : 2 + a + rows, 2 + b : 2 + b + cols]

    center = moved(0, 0)
    east = moved(1, 0)
    west = moved(-1, 0)
    north = moved(0, 1)
    south = moved(0, -1)
    nearest = east + west + north + south
    mass = density_field * (2.0 / 3.0 * center + nearest / 12.0)
    face_e = 0.5 * (kxp[1:-1, 1:-1] + kxp[2:, 1:-1])
    face_w = 0.5 * (kxp[1:-1, 1:-1] + kxp[:-2, 1:-1])
    face_n = 0.5 * (kyp[1:-1, 1:-1] + kyp[1:-1, 2:])
    face_s = 0.5 * (kyp[1:-1, 1:-1] + kyp[1:-1, :-2])
    membrane = (
        face_e * (center - east)
        + face_w * (center - west)
        + face_n * (center - north)
        + face_s * (center - south)
    )
    diagonals = moved(1, 1) + moved(1, -1) + moved(-1, 1) + moved(-1, -1)
    distant = moved(2, 0) + moved(-2, 0) + moved(0, 2) + moved(0, -2)
    bending = bend_field * (20.0 * center - 8.0 * nearest + 2.0 * diagonals + distant)
    return (mass, membrane, bending)


def local(old_modes, new_modes, material, density, memb_x, memb_y, bend_table):
    panel_size, rows, cols = new_modes.shape
    density_field = lookup(material, density)
    kxp = jnp.pad(lookup(material, memb_x), 1)
    ky_field = lookup(material, memb_y).astype(jnp.bfloat16)
    bend_field = lookup(material, bend_table)
    stacked = jnp.concatenate([new_modes, ky_field[None]], axis=0)
    rimmed = extended(stacked, (("space", 2),), 2)
    rimmed = jnp.pad(rimmed, ((0, 0), (2, 2), (0, 0)))
    padded = rimmed[:panel_size].astype(jnp.float32)
    kyp = rimmed[panel_size, 1:-1, 1:-1].astype(jnp.float32)
    mass, membrane, bending = operators(padded, kxp, kyp, density_field, bend_field, rows, cols)
    mass_image = mass.astype(jnp.bfloat16)
    stiff_image = (membrane + bending).astype(jnp.bfloat16)
    images = jnp.concatenate([mass, membrane, bending], axis=0).reshape(3 * panel_size, rows * cols)
    index = lax.axis_index("mode")
    loop_size = lax.axis_size("mode")
    area = 1.0 / (rows * cols * lax.axis_size("space"))

    def place(grams, panel, owner):
        block = lax.dot_general(
            panel.reshape(panel_size, rows * cols).astype(jnp.float32),
            images,
            (((1,), (1,)), ((), ())),
            precision=lax.Precision.HIGHEST,
            preferred_element_type=jnp.float32,
        )
        start = jnp.mod(owner, loop_size) * panel_size
        return lax.dynamic_update_slice(grams, block, (start, jnp.int32(0)))

    grams = jnp.zeros((loop_size * panel_size, 3 * panel_size), jnp.float32)
    grams = place(grams, old_modes, index)

    def turn(step, carry):
        panel, totals = carry
        panel = passed_along(panel, "mode", 1)
        return (panel, place(totals, panel, index - step))

    last, grams = lax.fori_loop(1, loop_size, turn, (old_modes, grams))
    total = lax.psum(grams, "space")
    cross_mass = total[:, :panel_size] * area
    cross_membrane = total[:, panel_size : 2 * panel_size] * area
    cross_bending = total[:, 2 * panel_size :] * area
    return (cross_mass, cross_membrane, cross_bending, mass_image, stiff_image)


def solution(mesh):
    in_specs = (
        P("mode", None, "space"),
        P("mode", None, "space"),
        P(None, "space"),
        P(),
        P(),
        P(),
        P(),
    )
    out_specs = (
        P(None, "mode"),
        P(None, "mode"),
        P(None, "mode"),
        P("mode", None, "space"),
        P("mode", None, "space"),
    )
    return jax.shard_map(local, mesh=mesh, in_specs=in_specs, out_specs=out_specs, check_vma=False)
```

profile of v0, /device:TPU:6, one launch (start us, length us, event | category | flops | bytes accessed | tf_op | source)
XLA Modules:
  0.0 738.0 jit_solution(993492930398526759)
XLA Ops:
  13.9 4.9 collective-permute-start.1
  24.7 7.6 %add_convert_fusion = (bf16[32,64,128]{1,0,2:T(8,128)(2,1)}, f32[32,64,128]{1,0,2:T(8,128)S(1)}, f32[32,64,128]{1,0,2:T(8,128)S(1)}, f32[32,64,128]{1,0,2:T(8,128)S(1)}) fusion(f32[32,68,132]{1,0,2:T(8,128)S(1)} %slice_convert_fusion, f32[64,128]{0,1:T(8,128)S(1)} %copy.93, f32[64,128]{0,1:T(8,128)S(1)} %copy.91, f32[64,128]{0,1:T(8,128)S(1)} %copy.88, ...), kind=kLoop, calls=%fused_computation.18 | loop fusion | flops 7602176 | bytes 17465344 | tf_op jit(solution)/shard_map/convert_element_type | solution.py:73
  39.2 6.8 copy.97
  46.0 4.3 copy.112
  50.3 5.5 fusion.12
  55.8 335.7 %while.17 = (s32[]{:T(128)}, bf16[32,64,128]{2,1,0:T(8,128)(2,1)}, f32[512,96]{1,0:T(8,128)S(1)}, f32[96,8192]{1,0:T(8,128)S(1)}, s32[]{:T(128)}, /*index=5*/s32...) while((s32[]{:T(128)}, bf16[32,64,128]{2,1,0:T(8,128)(2,1)}, ...), condition=%wide.region_5.6_spmd, body=%wide.region_4.5_spmd.sunk | while | flops 301989920 | bytes 6832448 | solution.py:98
  57.8 15.0 %collective-permute-done = bf16[32,64,128]{2,1,0:T(8,128)(2,1)} collective-permute-done((bf16[32,64,128]{2,1,0:T(8,128)(2,1)}, bf16[32,64,128]{2,1,0:T(8,128)(2,1)}, u32[]{:S(2)}, u32[]{:S(2)}) %collective-permute-start) | collective-permute-done | bytes 524320 | tf_op jit(solution)/shard_map/while/body/eval_jaxpr/ppermute | solution.py:23
  77.5 5.6 collective-permute-start
  83.1 10.0 %collective-permute-done = bf16[32,64,128]{2,1,0:T(8,128)(2,1)} collective-permute-done((bf16[32,64,128]{2,1,0:T(8,128)(2,1)}, bf16[32,64,128]{2,1,0:T(8,128)(2,1)}, u32[]{:S(2)}, u32[]{:S(2)}) %collective-permute-start) | collective-permute-done | bytes 524320 | tf_op jit(solution)/shard_map/while/body/eval_jaxpr/ppermute | solution.py:23
  97.7 5.0 collective-permute-start
  102.7 10.6 %collective-permute-done = bf16[32,64,128]{2,1,0:T(8,128)(2,1)} collective-permute-done((bf16[32,64,128]{2,1,0:T(8,128)(2,1)}, bf16[32,64,128]{2,1,0:T(8,128)(2,1)}, u32[]{:S(2)}, u32[]{:S(2)}) %collective-permute-start) | collective-permute-done | bytes 524320 | tf_op jit(solution)/shard_map/while/body/eval_jaxpr/ppermute | solution.py:23
  122.0 11.6 %collective-permute-done = bf16[32,64,128]{2,1,0:T(8,128)(2,1)} collective-permute-done((bf16[32,64,128]{2,1,0:T(8,128)(2,1)}, bf16[32,64,128]{2,1,0:T(8,128)(2,1)}, u32[]{:S(2)}, u32[]{:S(2)}) %collective-permute-start) | collective-permute-done | bytes 524320 | tf_op jit(solution)/shard_map/while/body/eval_jaxpr/ppermute | solution.py:23
  141.5 12.4 %collective-permute-done = bf16[32,64,128]{2,1,0:T(8,128)(2,1)} collective-permute-done((bf16[32,64,128]{2,1,0:T(8,128)(2,1)}, bf16[32,64,128]{2,1,0:T(8,128)(2,1)}, u32[]{:S(2)}, u32[]{:S(2)}) %collective-permute-start) | collective-permute-done | bytes 524320 | tf_op jit(solution)/shard_map/while/body/eval_jaxpr/ppermute | solution.py:23
  160.8 13.3 %collective-permute-done = bf16[32,64,128]{2,1,0:T(8,128)(2,1)} collective-permute-done((bf16[32,64,128]{2,1,0:T(8,128)(2,1)}, bf16[32,64,128]{2,1,0:T(8,128)(2,1)}, u32[]{:S(2)}, u32[]{:S(2)}) %collective-permute-start) | collective-permute-done | bytes 524320 | tf_op jit(solution)/shard_map/while/body/eval_jaxpr/ppermute | solution.py:23
  178.8 5.7 collective-permute-start
  184.5 15.6 %collective-permute-done = bf16[32,64,128]{2,1,0:T(8,128)(2,1)} collective-permute-done((bf16[32,64,128]{2,1,0:T(8,128)(2,1)}, bf16[32,64,128]{2,1,0:T(8,128)(2,1)}, u32[]{:S(2)}, u32[]{:S(2)}) %collective-permute-start) | collective-permute-done | bytes 524320 | tf_op jit(solution)/shard_map/while/body/eval_jaxpr/ppermute | solution.py:23
  204.7 4.8 collective-permute-start
  209.6 15.2 %collective-permute-done = bf16[32,64,128]{2,1,0:T(8,128)(2,1)} collective-permute-done((bf16[32,64,128]{2,1,0:T(8,128)(2,1)}, bf16[32,64,128]{2,1,0:T(8,128)(2,1)}, u32[]{:S(2)}, u32[]{:S(2)}) %collective-permute-start) | collective-permute-done | bytes 524320 | tf_op jit(solution)/shard_map/while/body/eval_jaxpr/ppermute | solution.py:23
  229.4 5.1 collective-permute-start
  234.5 10.6 %collective-permute-done = bf16[32,64,128]{2,1,0:T(8,128)(2,1)} collective-permute-done((bf16[32,64,128]{2,1,0:T(8,128)(2,1)}, bf16[32,64,128]{2,1,0:T(8,128)(2,1)}, u32[]{:S(2)}, u32[]{:S(2)}) %collective-permute-start) | collective-permute-done | bytes 524320 | tf_op jit(solution)/shard_map/while/body/eval_jaxpr/ppermute | solution.py:23
  249.8 9.5 %collective-permute-start = (bf16[32,64,128]{2,1,0:T(8,128)(2,1)}, bf16[32,64,128]{2,1,0:T(8,128)(2,1)}, u32[]{:S(2)}, u32[]{:S(2)}) collective-permute-start(bf16[32,64,128]{2,1,0:T(8,128)(2,1)} %get-tuple-element.241), channel_id=1, source_target_pairs={{0,1},{1,2},{2,3},{3,4},{4,5},{5,6},{6,7},{7,8},{8,9},{9,10},{10,1... | collective-permute-start | bytes 1572872 | tf_op jit(solution)/shard_map/while/body/eval_jaxpr/ppermute | solution.py:23
  259.3 6.1 collective-permute-done
  270.0 14.3 %collective-permute-start = (bf16[32,64,128]{2,1,0:T(8,128)(2,1)}, bf16[32,64,128]{2,1,0:T(8,128)(2,1)}, u32[]{:S(2)}, u32[]{:S(2)}) collective-permute-start(bf16[32,64,128]{2,1,0:T(8,128)(2,1)} %get-tuple-element.241), channel_id=1, source_target_pairs={{0,1},{1,2},{2,3},{3,4},{4,5},{5,6},{6,7},{7,8},{8,9},{9,10},{10,1... | collective-permute-start | bytes 1572872 | tf_op jit(solution)/shard_map/while/body/eval_jaxpr/ppermute | solution.py:23
  284.3 4.2 collective-permute-done
  293.2 16.0 %collective-permute-start = (bf16[32,64,128]{2,1,0:T(8,128)(2,1)}, bf16[32,64,128]{2,1,0:T(8,128)(2,1)}, u32[]{:S(2)}, u32[]{:S(2)}) collective-permute-start(bf16[32,64,128]{2,1,0:T(8,128)(2,1)} %get-tuple-element.241), channel_id=1, source_target_pairs={{0,1},{1,2},{2,3},{3,4},{4,5},{5,6},{6,7},{7,8},{8,9},{9,10},{10,1... | collective-permute-start | bytes 1572872 | tf_op jit(solution)/shard_map/while/body/eval_jaxpr/ppermute | solution.py:23
  309.3 4.4 collective-permute-done
  318.3 15.9 %collective-permute-start = (bf16[32,64,128]{2,1,0:T(8,128)(2,1)}, bf16[32,64,128]{2,1,0:T(8,128)(2,1)}, u32[]{:S(2)}, u32[]{:S(2)}) collective-permute-start(bf16[32,64,128]{2,1,0:T(8,128)(2,1)} %get-tuple-element.241), channel_id=1, source_target_pairs={{0,1},{1,2},{2,3},{3,4},{4,5},{5,6},{6,7},{7,8},{8,9},{9,10},{10,1... | collective-permute-start | bytes 1572872 | tf_op jit(solution)/shard_map/while/body/eval_jaxpr/ppermute | solution.py:23
  334.2 5.0 collective-permute-done
  343.9 15.4 %collective-permute-start = (bf16[32,64,128]{2,1,0:T(8,128)(2,1)}, bf16[32,64,128]{2,1,0:T(8,128)(2,1)}, u32[]{:S(2)}, u32[]{:S(2)}) collective-permute-start(bf16[32,64,128]{2,1,0:T(8,128)(2,1)} %get-tuple-element.241), channel_id=1, source_target_pairs={{0,1},{1,2},{2,3},{3,4},{4,5},{5,6},{6,7},{7,8},{8,9},{9,10},{10,1... | collective-permute-start | bytes 1572872 | tf_op jit(solution)/shard_map/while/body/eval_jaxpr/ppermute | solution.py:23
  359.3 4.3 collective-permute-done
  368.2 15.8 %collective-permute-start = (bf16[32,64,128]{2,1,0:T(8,128)(2,1)}, bf16[32,64,128]{2,1,0:T(8,128)(2,1)}, u32[]{:S(2)}, u32[]{:S(2)}) collective-permute-start(bf16[32,64,128]{2,1,0:T(8,128)(2,1)} %get-tuple-element.241), channel_id=1, source_target_pairs={{0,1},{1,2},{2,3},{3,4},{4,5},{5,6},{6,7},{7,8},{8,9},{9,10},{10,1... | collective-permute-start | bytes 1572872 | tf_op jit(solution)/shard_map/while/body/eval_jaxpr/ppermute | solution.py:23
  397.3 332.3 %all-reduce.4.cloned.1.call-done = f32[512,96]{0,1:T(8,128)} async-done(((f32[512,96]{0,1:T(8,128)}), f32[512,96]{0,1:T(8,128)}) %all-reduce.4.cloned.1.call-update) | async-done | bytes 196624 | tf_op jit(solution)/shard_map/psum | solution.py:99
  (89 shorter events, 110.4 us)
Async XLA Ops:
  7.2 11.7 %copy-start.7 = (bf16[32,64,128]{2,1,0:T(8,128)(2,1)S(1)}, bf16[32,64,128]{2,1,0:T(8,128)(2,1)}, u32[]{:S(2)}) copy-start(bf16[32,64,128]{2,1,0:T(8,128)(2,1)} %param.10) | copy-start | bytes 1572868
  7.2 722.4 %all-reduce.4.cloned.1.call-start = ((), (), s32[]{:S(2)}) async-start(), calls=%async_computation | async-start | bytes 393216 | tf_op jit(solution)/shard_map/psum | solution.py:99
  8.3 12.2 %copy-start.8 = (bf16[32,64,128]{2,1,0:T(8,128)(2,1)}, bf16[32,64,128]{2,1,0:T(8,128)(2,1)S(1)}, u32[]{:S(2)}) copy-start(bf16[32,64,128]{2,1,0:T(8,128)(2,1)S(1)} %copy.128) | copy-start | bytes 1572868
  12.3 10.8 %collective-permute-start.2 = (bf16[33,64,2]{1,2,0:T(2,128)(2,1)S(1)}, bf16[33,64,2]{1,2,0:T(2,128)(2,1)S(1)}, u32[]{:S(2)}, u32[]{:S(2)}) collective-permute-start(bf16[33,64,2]{1,2,0:T(2,128)(2,1)S(1)} %copy.104), channel_id=1, source_target_pairs={{16,0},{32,16},{48,32},{64,48},{80,64},{96,80},{112,96},{128,112},... | collective-permute-start | bytes 25352 | tf_op jit(solution)/shard_map/ppermute | solution.py:15
  13.9 9.2 %collective-permute-start.1 = (bf16[33,64,2]{1,2,0:T(2,128)(2,1)S(1)}, bf16[33,64,2]{1,2,0:T(2,128)(2,1)S(1)}, u32[]{:S(2)}, u32[]{:S(2)}) collective-permute-start(bf16[33,64,2]{1,2,0:T(2,128)(2,1)S(1)} %copy.103), channel_id=1, source_target_pairs={{0,16},{16,32},{32,48},{48,64},{64,80},{80,96},{96,112},{112,128},... | collective-permute-start | bytes 25352 | tf_op jit(solution)/shard_map/ppermute | solution.py:14
  32.3 2.2 copy-start
  32.3 2.4 copy-start.2
  34.6 1.3 copy-start.4
  46.0 4.3 copy-start.1
  46.0 4.3 copy-start.3
  46.0 4.3 copy-start.5
  55.8 17.0 %collective-permute-start = (bf16[32,64,128]{2,1,0:T(8,128)(2,1)}, bf16[32,64,128]{2,1,0:T(8,128)(2,1)}, u32[]{:S(2)}, u32[]{:S(2)}) collective-permute-start(bf16[32,64,128]{2,1,0:T(8,128)(2,1)} %get-tuple-element.241), channel_id=1, source_target_pairs={{0,1},{1,2},{2,3},{3,4},{4,5},{5,6},{6,7},{7,8},{8,9},{9,10},{10,1... | collective-permute-start | bytes 1572872 | tf_op jit(solution)/shard_map/while/body/eval_jaxpr/ppermute | solution.py:23
  77.5 15.6 %collective-permute-start = (bf16[32,64,128]{2,1,0:T(8,128)(2,1)}, bf16[32,64,128]{2,1,0:T(8,128)(2,1)}, u32[]{:S(2)}, u32[]{:S(2)}) collective-permute-start(bf16[32,64,128]{2,1,0:T(8,128)(2,1)} %get-tuple-element.241), channel_id=1, source_target_pairs={{0,1},{1,2},{2,3},{3,4},{4,5},{5,6},{6,7},{7,8},{8,9},{9,10},{10,1... | collective-permute-start | bytes 1572872 | tf_op jit(solution)/shard_map/while/body/eval_jaxpr/ppermute | solution.py:23
  97.7 15.6 %collective-permute-start = (bf16[32,64,128]{2,1,0:T(8,128)(2,1)}, bf16[32,64,128]{2,1,0:T(8,128)(2,1)}, u32[]{:S(2)}, u32[]{:S(2)}) collective-permute-start(bf16[32,64,128]{2,1,0:T(8,128)(2,1)} %get-tuple-element.241), channel_id=1, source_target_pairs={{0,1},{1,2},{2,3},{3,4},{4,5},{5,6},{6,7},{7,8},{8,9},{9,10},{10,1... | collective-permute-start | bytes 1572872 | tf_op jit(solution)/shard_map/while/body/eval_jaxpr/ppermute | solution.py:23
  118.0 15.6 %collective-permute-start = (bf16[32,64,128]{2,1,0:T(8,128)(2,1)}, bf16[32,64,128]{2,1,0:T(8,128)(2,1)}, u32[]{:S(2)}, u32[]{:S(2)}) collective-permute-start(bf16[32,64,128]{2,1,0:T(8,128)(2,1)} %get-tuple-element.241), channel_id=1, source_target_pairs={{0,1},{1,2},{2,3},{3,4},{4,5},{5,6},{6,7},{7,8},{8,9},{9,10},{10,1... | collective-permute-start | bytes 1572872 | tf_op jit(solution)/shard_map/while/body/eval_jaxpr/ppermute | solution.py:23
  138.2 15.6 %collective-permute-start = (bf16[32,64,128]{2,1,0:T(8,128)(2,1)}, bf16[32,64,128]{2,1,0:T(8,128)(2,1)}, u32[]{:S(2)}, u32[]{:S(2)}) collective-permute-start(bf16[32,64,128]{2,1,0:T(8,128)(2,1)} %get-tuple-element.241), channel_id=1, source_target_pairs={{0,1},{1,2},{2,3},{3,4},{4,5},{5,6},{6,7},{7,8},{8,9},{9,10},{10,1... | collective-permute-start | bytes 1572872 | tf_op jit(solution)/shard_map/while/body/eval_jaxpr/ppermute | solution.py:23
  158.5 15.6 %collective-permute-start = (bf16[32,64,128]{2,1,0:T(8,128)(2,1)}, bf16[32,64,128]{2,1,0:T(8,128)(2,1)}, u32[]{:S(2)}, u32[]{:S(2)}) collective-permute-start(bf16[32,64,128]{2,1,0:T(8,128)(2,1)} %get-tuple-element.241), channel_id=1, source_target_pairs={{0,1},{1,2},{2,3},{3,4},{4,5},{5,6},{6,7},{7,8},{8,9},{9,10},{10,1... | collective-permute-start | bytes 1572872 | tf_op jit(solution)/shard_map/while/body/eval_jaxpr/ppermute | solution.py:23
  178.8 21.3 %collective-permute-start = (bf16[32,64,128]{2,1,0:T(8,128)(2,1)}, bf16[32,64,128]{2,1,0:T(8,128)(2,1)}, u32[]{:S(2)}, u32[]{:S(2)}) collective-permute-start(bf16[32,64,128]{2,1,0:T(8,128)(2,1)} %get-tuple-element.241), channel_id=1, source_target_pairs={{0,1},{1,2},{2,3},{3,4},{4,5},{5,6},{6,7},{7,8},{8,9},{9,10},{10,1... | collective-permute-start | bytes 1572872 | tf_op jit(solution)/shard_map/while/body/eval_jaxpr/ppermute | solution.py:23
  204.7 20.0 %collective-permute-start = (bf16[32,64,128]{2,1,0:T(8,128)(2,1)}, bf16[32,64,128]{2,1,0:T(8,128)(2,1)}, u32[]{:S(2)}, u32[]{:S(2)}) collective-permute-start(bf16[32,64,128]{2,1,0:T(8,128)(2,1)} %get-tuple-element.241), channel_id=1, source_target_pairs={{0,1},{1,2},{2,3},{3,4},{4,5},{5,6},{6,7},{7,8},{8,9},{9,10},{10,1... | collective-permute-start | bytes 1572872 | tf_op jit(solution)/shard_map/while/body/eval_jaxpr/ppermute | solution.py:23
  229.4 15.7 %collective-permute-start = (bf16[32,64,128]{2,1,0:T(8,128)(2,1)}, bf16[32,64,128]{2,1,0:T(8,128)(2,1)}, u32[]{:S(2)}, u32[]{:S(2)}) collective-permute-start(bf16[32,64,128]{2,1,0:T(8,128)(2,1)} %get-tuple-element.241), channel_id=1, source_target_pairs={{0,1},{1,2},{2,3},{3,4},{4,5},{5,6},{6,7},{7,8},{8,9},{9,10},{10,1... | collective-permute-start | bytes 1572872 | tf_op jit(solution)/shard_map/while/body/eval_jaxpr/ppermute | solution.py:23
  249.8 15.6 %collective-permute-start = (bf16[32,64,128]{2,1,0:T(8,128)(2,1)}, bf16[32,64,128]{2,1,0:T(8,128)(2,1)}, u32[]{:S(2)}, u32[]{:S(2)}) collective-permute-start(bf16[32,64,128]{2,1,0:T(8,128)(2,1)} %get-tuple-element.241), channel_id=1, source_target_pairs={{0,1},{1,2},{2,3},{3,4},{4,5},{5,6},{6,7},{7,8},{8,9},{9,10},{10,1... | collective-permute-start | bytes 1572872 | tf_op jit(solution)/shard_map/while/body/eval_jaxpr/ppermute | solution.py:23
  270.0 18.5 %collective-permute-start = (bf16[32,64,128]{2,1,0:T(8,128)(2,1)}, bf16[32,64,128]{2,1,0:T(8,128)(2,1)}, u32[]{:S(2)}, u32[]{:S(2)}) collective-permute-start(bf16[32,64,128]{2,1,0:T(8,128)(2,1)} %get-tuple-element.241), channel_id=1, source_target_pairs={{0,1},{1,2},{2,3},{3,4},{4,5},{5,6},{6,7},{7,8},{8,9},{9,10},{10,1... | collective-permute-start | bytes 1572872 | tf_op jit(solution)/shard_map/while/body/eval_jaxpr/ppermute | solution.py:23
  293.2 20.4 %collective-permute-start = (bf16[32,64,128]{2,1,0:T(8,128)(2,1)}, bf16[32,64,128]{2,1,0:T(8,128)(2,1)}, u32[]{:S(2)}, u32[]{:S(2)}) collective-permute-start(bf16[32,64,128]{2,1,0:T(8,128)(2,1)} %get-tuple-element.241), channel_id=1, source_target_pairs={{0,1},{1,2},{2,3},{3,4},{4,5},{5,6},{6,7},{7,8},{8,9},{9,10},{10,1... | collective-permute-start | bytes 1572872 | tf_op jit(solution)/shard_map/while/body/eval_jaxpr/ppermute | solution.py:23
  318.3 20.9 %collective-permute-start = (bf16[32,64,128]{2,1,0:T(8,128)(2,1)}, bf16[32,64,128]{2,1,0:T(8,128)(2,1)}, u32[]{:S(2)}, u32[]{:S(2)}) collective-permute-start(bf16[32,64,128]{2,1,0:T(8,128)(2,1)} %get-tuple-element.241), channel_id=1, source_target_pairs={{0,1},{1,2},{2,3},{3,4},{4,5},{5,6},{6,7},{7,8},{8,9},{9,10},{10,1... | collective-permute-start | bytes 1572872 | tf_op jit(solution)/shard_map/while/body/eval_jaxpr/ppermute | solution.py:23
  343.9 19.7 %collective-permute-start = (bf16[32,64,128]{2,1,0:T(8,128)(2,1)}, bf16[32,64,128]{2,1,0:T(8,128)(2,1)}, u32[]{:S(2)}, u32[]{:S(2)}) collective-permute-start(bf16[32,64,128]{2,1,0:T(8,128)(2,1)} %get-tuple-element.241), channel_id=1, source_target_pairs={{0,1},{1,2},{2,3},{3,4},{4,5},{5,6},{6,7},{7,8},{8,9},{9,10},{10,1... | collective-permute-start | bytes 1572872 | tf_op jit(solution)/shard_map/while/body/eval_jaxpr/ppermute | solution.py:23
  368.2 18.7 %collective-permute-start = (bf16[32,64,128]{2,1,0:T(8,128)(2,1)}, bf16[32,64,128]{2,1,0:T(8,128)(2,1)}, u32[]{:S(2)}, u32[]{:S(2)}) collective-permute-start(bf16[32,64,128]{2,1,0:T(8,128)(2,1)} %get-tuple-element.241), channel_id=1, source_target_pairs={{0,1},{1,2},{2,3},{3,4},{4,5},{5,6},{6,7},{7,8},{8,9},{9,10},{10,1... | collective-permute-start | bytes 1572872 | tf_op jit(solution)/shard_map/while/body/eval_jaxpr/ppermute | solution.py:23
  391.6 3.8 copy-start.6
Sparse Core Ops, SparseCore 0:
  392.5 337.0 all-reduce.3
where the time goes:
time: 740 us; the launch traced here: 738 us
  waiting for transfers between devices  473 us (64%)
  starting transfers between devices  131 us (18%)
  local copies, waits for them, and re-layouts  52.2 us (7%)
  matrix products  47 us (6%)
  other arithmetic  19.8 us (3%)
  between operations  14.3 us (2%)
    psum x1, waiting for transfers between devices, local(): total = lax.psum(grams, 'space')  332 us
    ppermute x15, waiting for transfers between devices, passed_along(): return lax.ppermute(value, axis, pairs)  141 us
    ppermute x15, starting transfers between devices, passed_along(): return lax.ppermute(value, axis, pairs)  124 us
    dot_general x16, matrix products, place(): lax.dot_general(panel.reshape(panel_size, rows * cols).astype(jnp.float32...  47 us
    while x15, local copies, waits for them, and re-layouts  28 us
  transfers between devices with their start and end apart: 18, of which 16 were waited for; matrix products, arithmetic and copies ran while one was open for 1% of the time, Pallas kernels for 0%

commit v1 on v0

v1 whole, which is shorter than its diff:
```python
import jax
import jax.numpy as jnp
from jax import lax
from jax.experimental import pallas as pl
from jax.experimental.pallas import tpu as pltpu
from jax.sharding import Mesh, PartitionSpec as P

SPACE = ("y", "zl")
MODE = ("x", "zh", "c")
R, M, C = 64, 32, 128
F32, BF16 = jnp.float32, jnp.bfloat16
VM = pl.BlockSpec(memory_space=pltpu.VMEM)
SM = pl.BlockSpec(memory_space=pltpu.SMEM)


def shifted(value, axis, step):
    n = lax.axis_size(axis)
    return lax.ppermute(value, axis, [(i, (i + step) % n) for i in range(n)])


def select_table(material, table_ref):
    value = jnp.zeros(material.shape, F32)
    for level in range(table_ref.shape[0]):
        value = jnp.where(material == level, table_ref[level].astype(F32), value)
    return value


def edges_kernel(u_ref, mat_ref, my_ref, out_ref, ky):
    ky[...] = select_table(mat_ref[...], my_ref)
    lane = lax.broadcasted_iota(jnp.int32, (1, C), 1)

    def row(r, carry):
        first, last, kfirst, klast = carry
        here = lane // 2 == r
        u = u_ref[r].astype(F32)
        k = jnp.broadcast_to(ky[pl.ds(r, 1), :], (8, C))
        first = jnp.where(here, pltpu.roll(u, 2 * r, 1), first)
        last = jnp.where(here, pltpu.roll(u, (2 * r + 2) % C, 1), last)
        kfirst = jnp.where(here, pltpu.roll(k, 2 * r, 1), kfirst)
        klast = jnp.where(here, pltpu.roll(k, (2 * r + 2) % C, 1), klast)
        return first, last, kfirst, klast

    zu, zk = jnp.zeros((M, C), F32), jnp.zeros((8, C), F32)
    first, last, kfirst, klast = lax.fori_loop(0, R, row, (zu, zu, zk, zk))
    out_ref[0] = jnp.concatenate([first, kfirst], axis=0).astype(BF16)
    out_ref[1] = jnp.concatenate([last, klast], axis=0).astype(BF16)


def edges(u, material, memb_y):
    return pl.pallas_call(
        edges_kernel,
        out_shape=jax.ShapeDtypeStruct((2, M + 8, C), BF16),
        in_specs=[VM, VM, SM],
        out_specs=VM,
        scratch_shapes=[pltpu.VMEM((R, C), F32)],
        cost_estimate=pl.CostEstimate(flops=10**6, bytes_accessed=10**6, transcendentals=0),
    )(u, material, memb_y)


def fields_kernel(mat_ref, left_ref, right_ref, rho_ref, mx_ref, my_ref, dd_ref, f_ref, kx, ky, rho, dd):
    material = mat_ref[...]
    kx[...] = jnp.zeros(kx.shape, F32)
    kx[8 : 8 + R, :] = select_table(material, mx_ref)
    ky[...] = select_table(material, my_ref)
    rho[...] = select_table(material, rho_ref)
    dd[...] = select_table(material, dd_ref)
    lane = lax.broadcasted_iota(jnp.int32, (1, C), 1)
    left = left_ref[M : M + 8, :].astype(F32)
    right = right_ref[M : M + 8, :].astype(F32)

    def row(r, _):
        k = ky[pl.ds(r, 1), :]
        kl = pltpu.roll(left, C - 1 - 2 * r, 1)[0:1]
        kr = pltpu.roll(right, C - 1 - 2 * r, 1)[0:1]
        k8 = jnp.broadcast_to(k, (8, C))
        south = jnp.where(lane == 0, kl, pltpu.roll(k8, 1, 1)[0:1])
        north = jnp.where(lane == C - 1, kr, pltpu.roll(k8, C - 1, 1)[0:1])
        kc = kx[pl.ds(r + 8, 1), :]
        fe = 0.5 * (kc + kx[pl.ds(r + 9, 1), :])
        fw = 0.5 * (kc + kx[pl.ds(r + 7, 1), :])
        fn = 0.5 * (k + north)
        fs = 0.5 * (k + south)
        rr = rho[pl.ds(r, 1), :]
        rows = [rr * (2.0 / 3.0), rr * (1.0 / 12.0), fe + fw + fn + fs, fe, fw, fn, fs, dd[pl.ds(r, 1), :]]
        f_ref[r] = jnp.concatenate(rows, axis=0)
        return 0

    lax.fori_loop(0, R, row, 0)


def fields(material, left, right, density, memb_x, memb_y, bend_table):
    return pl.pallas_call(
        fields_kernel,
        out_shape=jax.ShapeDtypeStruct((R, 8, C), F32),
        in_specs=[VM, VM, VM, SM, SM, SM, SM],
        out_specs=VM,
        scratch_shapes=[pltpu.VMEM((R + 16, C), F32)] + [pltpu.VMEM((R, C), F32)] * 3,
        cost_estimate=pl.CostEstimate(flops=10**6, bytes_accessed=10**6, transcendentals=0),
    )(material, left, right, density, memb_x, memb_y, bend_table)


def stencil_kernel(with_images, u_ref, halo_ref, f_ref, *rest):
    if with_images:
        hi_ref, lo_ref, mass_ref, stiff_ref, us, s1, s2, q = rest
    else:
        hi_ref, lo_ref, us, s1, s2, q = rest
    zero = jnp.zeros((M, C), F32)
    for r in (0, 1, R + 2, R + 3):
        us[r] = zero
    s1[0] = zero
    s1[R + 1] = zero
    lane = lax.broadcasted_iota(jnp.int32, (1, C), 1)
    left = halo_ref[0].astype(F32)[0:M]
    right = halo_ref[1].astype(F32)[0:M]

    def spread(r, _):
        u = u_ref[r].astype(F32)
        south = jnp.where(lane == 0, pltpu.roll(left, C - 1 - 2 * r, 1), pltpu.roll(u, 1, 1))
        south2 = jnp.where(lane < 2, pltpu.roll(left, (C - 2 * r) % C, 1), pltpu.roll(u, 2, 1))
        north = jnp.where(lane == C - 1, pltpu.roll(right, C - 1 - 2 * r, 1), pltpu.roll(u, C - 1, 1))
        north2 = jnp.where(lane >= C - 2, pltpu.roll(right, C - 2 - 2 * r, 1), pltpu.roll(u, C - 2, 1))
        us[r + 2] = u
        s1[r + 1] = south + north
        s2[r] = south2 + north2
        q[r] = f_ref[r, 5:6, :] * north + f_ref[r, 6:7, :] * south
        return 0

    lax.fori_loop(0, R, spread, 0, unroll=4)

    def row(r, _):
        u, east, west = us[r + 2], us[r + 3], us[r + 1]
        near = (east + west) + s1[r + 1]
        mass = f_ref[r, 0:1, :] * u + f_ref[r, 1:2, :] * near
        membrane = f_ref[r, 2:3, :] * u - f_ref[r, 3:4, :] * east - f_ref[r, 4:5, :] * west - q[r]
        far = (us[r + 4] + us[r]) + s2[r]
        diagonal = s1[r] + s1[r + 2]
        bending = f_ref[r, 7:8, :] * (20.0 * u - 8.0 * near + 2.0 * diagonal + far)
        for i, v in enumerate((mass, membrane, bending)):
            hi = v.astype(BF16)
            hi_ref[r, M * i : M * i + M, :] = hi
            lo_ref[r, M * i : M * i + M, :] = (v - hi.astype(F32)).astype(BF16)
        if with_images:
            mass_ref[r] = mass.astype(BF16)
            stiff_ref[r] = (membrane + bending).astype(BF16)
        return 0

    lax.fori_loop(0, R, row, 0, unroll=4)


def stencil(u, halo, f, with_images):
    terms = [jax.ShapeDtypeStruct((R, 3 * M, C), BF16)] * 2
    images = [jax.ShapeDtypeStruct((R, M, C), BF16)] * (2 if with_images else 0)
    return pl.pallas_call(
        lambda *refs: stencil_kernel(with_images, *refs),
        out_shape=terms + images,
        in_specs=[VM] * 3,
        out_specs=[VM] * (len(terms) + len(images)),
        scratch_shapes=[
            pltpu.VMEM((R + 4, M, C), F32),
            pltpu.VMEM((R + 2, M, C), F32),
            pltpu.VMEM((R, M, C), F32),
            pltpu.VMEM((R, M, C), F32),
        ],
        compiler_params=pltpu.CompilerParams(vmem_limit_bytes=24 * 2**20),
        cost_estimate=pl.CostEstimate(flops=10**7, bytes_accessed=4 * 10**6, transcendentals=0),
    )(u, halo, f)


STEP = 8


def gram_kernel(*refs):
    terms, olds, out_ref, acc = refs[:8], refs[8:12], refs[12], refs[13]
    step = pl.program_id(0)

    def wide(ref):
        return jnp.concatenate([ref[r] for r in range(STEP)], axis=1)

    old = jnp.concatenate([wide(o) for o in olds], axis=0)

    @pl.when(step == 0)
    def _():
        acc[...] = jnp.zeros(acc.shape, F32)

    dims = (((1,), (1,)), ((), ()))
    for d in range(4):
        part = lax.dot_general(wide(terms[2 * d]), old, dims, preferred_element_type=F32)
        part += lax.dot_general(wide(terms[2 * d + 1]), old, dims, preferred_element_type=F32)
        acc[d] += part

    @pl.when(step == R // STEP - 1)
    def _():
        x, zh, c = lax.axis_index("x"), lax.axis_index("zh"), lax.axis_index("c")
        lane = lax.broadcasted_iota(jnp.int32, (1, 4 * M), 1)
        for d in range(4):
            v = pltpu.roll(acc[d], zh * 64, 1)
            swapped = jnp.where(lane % 64 < 32, pltpu.roll(v, 96, 1), pltpu.roll(v, 32, 1))
            v = jnp.where(c == 1, swapped, v)
            place = lax.rem(x + d, 4)
            for i in range(8):
                out_ref[i, place] = v[12 * i : 12 * i + 12]


def gram(terms, olds):
    return pl.pallas_call(
        gram_kernel,
        grid=(R // STEP,),
        out_shape=jax.ShapeDtypeStruct((8, 4, 12, 4 * M), F32),
        in_specs=[pl.BlockSpec((STEP, 3 * M, C), lambda i: (i, 0, 0))] * 8
        + [pl.BlockSpec((STEP, M, C), lambda i: (i, 0, 0))] * 4,
        out_specs=pl.BlockSpec((8, 4, 12, 4 * M), lambda i: (0, 0, 0, 0)),
        scratch_shapes=[pltpu.VMEM((4, 3 * M, 4 * M), F32)],
        compiler_params=pltpu.CompilerParams(vmem_limit_bytes=24 * 2**20),
        cost_estimate=pl.CostEstimate(flops=2 * 10**9, bytes_accessed=14 * 10**6, transcendentals=0),
    )(*terms, *olds)


def local(old_modes, new_modes, material, density, memb_x, memb_y, bend_table):
    old = old_modes.transpose(1, 0, 2)
    new = new_modes.transpose(1, 0, 2)
    other = shifted(old, "zh", 1)
    packet = edges(new, material, memb_y.astype(F32))
    n = 32
    up = [(i, i + 1) for i in range(n - 1)]
    down = [(i + 1, i) for i in range(n - 1)]
    left = lax.ppermute(packet[1], SPACE, up)
    right = lax.ppermute(packet[0], SPACE, down)
    panels = [new] + [shifted(new, "x", -d) for d in (1, 2, 3)]
    halo = jnp.stack([left, right])
    halos = lax.all_to_all(jnp.broadcast_to(halo[None], (4, *halo.shape)), "x", 0, 0)
    x = lax.axis_index("x")
    old_core = shifted(old, "c", 1)
    other_core = shifted(other, "c", 1)
    f = fields(material, left, right, density, memb_x.astype(F32), memb_y.astype(F32), bend_table)
    hi0, lo0, mass, stiff = stencil(new, halo, f, True)
    terms = [hi0, lo0]
    return finish(terms, panels, halos, x, f, (old, old_core, other, other_core), mass, stiff)


def field_terms(panel, halos, x, d, f):
    return stencil(panel, lax.dynamic_index_in_dim(halos, lax.rem(x + d, 4), 0, keepdims=False), f, False)


def finish(terms, panels, halos, x, f, olds, mass, stiff):
    for d in (1, 2, 3):
        terms = terms + list(field_terms(panels[d], halos, x, d, f))
    part = gram(terms, olds)
    part = jnp.sum(lax.all_to_all(part, "y", 0, 0), axis=0)
    part = jnp.broadcast_to(part[:, None], (4, 4, 12, 4 * M)).reshape(16, 12, 4 * M)
    part = lax.all_to_all(part, ("x", "zl"), 0, 0).reshape(4, 4, 12, 4 * M)
    part = jnp.sum(part, axis=1)
    part = lax.all_to_all(jnp.broadcast_to(part[None], (8, 4, 12, 4 * M)), "y", 0, 0)
    area = 1.0 / (R * C * 32)
    total = part.transpose(0, 2, 1, 3).reshape(3, M, 16 * M) * area
    crosses = [total[i].T for i in range(3)]
    return (*crosses, mass.transpose(1, 0, 2), stiff.transpose(1, 0, 2))


def solution(mesh):
    fine = Mesh(mesh.devices.reshape(8, 4, 4, 2, 2), ("y", "zl", "x", "zh", "c"))
    in_specs = (
        P(MODE, None, SPACE),
        P(MODE, None, SPACE),
        P(None, SPACE),
        P(),
        P(),
        P(),
        P(),
    )
    out_specs = (
        P(None, MODE),
        P(None, MODE),
        P(None, MODE),
        P(MODE, None, SPACE),
        P(MODE, None, SPACE),
    )
    return jax.shard_map(local, mesh=fine, in_specs=in_specs, out_specs=out_specs, check_vma=False)
```

time: 740 us -> 134 us (0.18)
  waiting for transfers between devices: 473 us -> 10 us
  starting transfers between devices: 131 us -> 36.9 us
  matrix products: 47 us -> 0 us
  local copies, waits for them, and re-layouts: 52.2 us -> 13.2 us
  Pallas kernels: 0 us -> 38.4 us
  blocking collectives: 0 us -> 31.9 us
  other arithmetic: 19.8 us -> 1.13 us
  between operations: 14.3 us -> 0.94 us
    psum x1 -> x0, waiting for transfers between devices: 332 us -> none  [local(): total = lax.psum(grams, 'space')]
    ppermute x17 -> x8, waiting for transfers between devices: 141 us -> 2.33 us  [the longest x1 2.31 us: local(): left = lax.ppermute(packet[1], SPACE, up)]
    ppermute x17 -> x8, starting transfers between devices: 131 us -> 28 us  [the longest x6 23.4 us: shifted(): return lax.ppermute(value, axis, [(i, (i + step) % n) for i in range(n)])]
    dot_general x16 -> x0, matrix products: 47 us -> none  [place(): lax.dot_general(panel.reshape(panel_size, rows * cols).astype(jnp.float32...]
    pallas_call x0 -> x7, Pallas kernels: none -> 38.4 us  [the longest x4 16.9 us: stencil(): pl.pallas_call(lambda *refs: stencil_kernel(with_images, *refs), out_shap...]
    all_to_all x0 -> x2, blocking collectives: none -> 31.9 us  [the longest x1 20.6 us: finish(): part = jnp.sum(lax.all_to_all(part, 'y', 0, 0), axis=0)]
    while x16 -> x0, local copies, waits for them, and re-layouts: 28.8 us -> none
    convert_element_type x6 -> x2, other arithmetic: 11.6 us -> 1.03 us  [the longest x1 0.51 us: local(): packet = edges(new, material, memb_y.astype(F32))]
  transfers between devices with their start and end apart: 18 -> 10, of which waited for: 16 -> 2; matrix products, arithmetic and copies ran while one was open for 1% -> 5% of each run, Pallas kernels for 0% -> 23%
where the time goes in v1:
time: 134 us; the launch traced here: 132 us
  Pallas kernels  38.4 us (29%)
  starting transfers between devices  36.9 us (28%)
  blocking collectives  31.9 us (24%)
  local copies, waits for them, and re-layouts  13.2 us (10%)
  waiting for transfers between devices  10 us (7%)
    ppermute x6, starting transfers between devices, shifted(): return lax.ppermute(value, axis, [(i, (i + step) % n) for i in range(n)])  23.4 us
    all_to_all x1, blocking collectives, finish(): part = jnp.sum(lax.all_to_all(part, 'y', 0, 0), axis=0)  20.6 us
    pallas_call x4, Pallas kernels, stencil(): pl.pallas_call(lambda *refs: stencil_kernel(with_images, *refs), out_shap...  16.9 us
    all_to_all x1, blocking collectives, finish(): part = lax.all_to_all(part, ('x', 'zl'), 0, 0).reshape(4, 4, 12, 4 * M)  11.4 us
    unnamed x30, local copies, waits for them, and re-layouts  10.3 us
    pallas_call x1, Pallas kernels, gram(): pl.pallas_call(gram_kernel, grid=(R // STEP,), out_shape=jax.ShapeDtypeSt...  7.97 us
    all_to_all x1, waiting for transfers between devices, finish(): lax.all_to_all(jnp.broadcast_to(part[None], (8, 4, 12, 4 * M)), 'y', 0, 0)  7.67 us
    pallas_call x1, Pallas kernels, fields(): pl.pallas_call(fields_kernel, out_shape=jax.ShapeDtypeStruct((R, 8, C), F...  6.79 us
  transfers between devices with their start and end apart: 10, of which 2 were waited for; matrix products, arithmetic and copies ran while one was open for 5% of the time, Pallas kernels for 23%

profile of v1, /device:TPU:6, one launch (start us, length us, event | category | flops | bytes accessed | tf_op | source)
XLA Modules:
  0.0 132.5 jit_solution(13883240804134487167)
XLA Ops:
  0.7 1.4 %copy.55 = bf16[32,64,128]{2,0,1:T(8,128)(2,1)S(1)} copy(bf16[32,64,128]{2,1,0:T(8,128)(2,1)} %param.7) | data formatting | bytes 1048576 | tf_op args[0]
  2.0 10.9 %collective-permute-start.6 = (bf16[64,32,128]{2,1,0:T(8,128)(2,1)S(1)}, bf16[64,32,128]{2,1,0:T(8,128)(2,1)S(1)}, u32[]{:S(2)}, u32[]{:S(2)}) collective-permute-start(bf16[64,32,128]{2,1,0:T(8,128)(2,1)S(1)} %bitcast.42), channel_id=1, source_target_pairs={{0,2},{2,0},{1,3},{3,1},{4,6},{6,4},{5,7},{7,5},{8,10},{10,8},{9,1... | collective-permute-start | bytes 1572872 | tf_op jit(solution)/shard_map/ppermute | solution.py:18
  13.0 2.2 %copy.56 = bf16[32,64,128]{2,0,1:T(8,128)(2,1)} copy(bf16[32,64,128]{2,1,0:T(8,128)(2,1)} %param.8) | data formatting | bytes 1048576 | tf_op args[1]
  15.7 6.7 %shard_map.110 = bf16[2,40,128]{2,1,0:T(8,128)(2,1)} custom-call(bf16[64,32,128]{2,1,0:T(8,128)(2,1)} %bitcast.37, s32[64,128]{1,0:T(8,128)} %mat_ref.3, f32[12]{0:T(128)} %convert_element_type.7.my_ref), custom_call_target="tpu_custom_call" | custom-call | flops 1000000 | bytes 1000000 | tf_op jit(solution)/shard_map/pallas_call | solution.py:50
  22.4 0.7 slice_bitcast_fusion.4
  23.1 3.4 %collective-permute-start = (bf16[40,128]{1,0:T(8,128)(2,1)S(1)}, bf16[40,128]{1,0:T(8,128)(2,1)S(1)}, u32[]{:S(2)}, u32[]{:S(2)}) collective-permute-start(bf16[40,128]{1,0:T(8,128)(2,1)S(1)} %get-tuple-element.61), channel_id=1, source_target_pairs={{0,16},{16,32},{32,48},{48,64},{64,80},{80,96},{96,112},{112,128},... | collective-permute-start | bytes 30728 | tf_op jit(solution)/shard_map/ppermute | solution.py:226
  26.5 1.3 collective-permute-start.1
  27.8 2.7 %collective-permute-start.2 = (bf16[64,32,128]{2,1,0:T(8,128)(2,1)}, bf16[64,32,128]{2,1,0:T(8,128)(2,1)}, u32[]{:S(2)}, u32[]{:S(2)}) collective-permute-start(bf16[64,32,128]{2,1,0:T(8,128)(2,1)} %bitcast.38), channel_id=1, source_target_pairs={{0,12},{4,0},{8,4},{12,8},{1,13},{5,1},{9,5},{13,9},{2,14},{6,2},{... | collective-permute-start | bytes 1572872 | tf_op jit(solution)/shard_map/ppermute | solution.py:18
  30.5 3.0 %collective-permute-start.3 = (bf16[64,32,128]{2,1,0:T(8,128)(2,1)}, bf16[64,32,128]{2,1,0:T(8,128)(2,1)}, u32[]{:S(2)}, u32[]{:S(2)}) collective-permute-start(bf16[64,32,128]{2,1,0:T(8,128)(2,1)} %bitcast.39), channel_id=1, source_target_pairs={{0,8},{4,12},{8,0},{12,4},{1,9},{5,13},{9,1},{13,5},{2,10},{6,14},... | collective-permute-start | bytes 1572872 | tf_op jit(solution)/shard_map/ppermute | solution.py:18
  33.6 2.3 %collective-permute-done.left_ref = bf16[40,128]{1,0:T(8,128)(2,1)S(1)} collective-permute-done((bf16[40,128]{1,0:T(8,128)(2,1)S(1)}, bf16[40,128]{1,0:T(8,128)(2,1)S(1)}, u32[]{:S(2)}, u32[]{:S(2)}) %collective-permute-start) | collective-permute-done | bytes 10272 | tf_op jit(solution)/shard_map/ppermute | solution.py:226
  35.9 2.4 %collective-permute-start.4 = (bf16[64,32,128]{2,1,0:T(8,128)(2,1)}, bf16[64,32,128]{2,1,0:T(8,128)(2,1)}, u32[]{:S(2)}, u32[]{:S(2)}) collective-permute-start(bf16[64,32,128]{2,1,0:T(8,128)(2,1)} %bitcast.40), channel_id=1, source_target_pairs={{0,4},{4,8},{8,12},{12,0},{1,5},{5,9},{9,13},{13,1},{2,6},{6,10},{... | collective-permute-start | bytes 1572872 | tf_op jit(solution)/shard_map/ppermute | solution.py:18
  38.3 1.9 %collective-permute-start.5 = (bf16[64,32,128]{2,1,0:T(8,128)(2,1)S(1)}, bf16[64,32,128]{2,1,0:T(8,128)(2,1)}, u32[]{:S(2)}, u32[]{:S(2)}) collective-permute-start(bf16[64,32,128]{2,1,0:T(8,128)(2,1)S(1)} %bitcast.43), channel_id=1, source_target_pairs={{0,1},{1,0},{2,3},{3,2},{4,5},{5,4},{6,7},{7,6},{8,9},{9,8},{10,11... | collective-permute-start | bytes 1572872 | tf_op jit(solution)/shard_map/ppermute | solution.py:18
  40.2 2.4 %collective-permute-start.7 = (bf16[64,32,128]{2,1,0:T(8,128)(2,1)S(1)}, bf16[64,32,128]{2,1,0:T(8,128)(2,1)}, u32[]{:S(2)}, u32[]{:S(2)}) collective-permute-start(bf16[64,32,128]{2,1,0:T(8,128)(2,1)S(1)} %collective-permute-done.6.refs_10_), channel_id=1, source_target_pairs={{0,1},{1,0},{2,3},{3,2},{4,5},{5,4},{6,7},{7,6},{8,9},{9,8},{10,11... | collective-permute-start | bytes 1572872 | tf_op jit(solution)/shard_map/ppermute | solution.py:18
  43.3 5.5 %all-to-all-start = ((bf16[4,2,40,128]{3,2,1,0:T(8,128)(2,1)}), bf16[4,2,40,128]{3,2,1,0:T(8,128)(2,1)S(1)}, u32[]{:S(2)}, u32[]{:S(2)}) async-start(bf16[4,2,40,128]{3,2,1,0:T(8,128)(2,1)} %broadcast_in_dim.6), calls=%async_computation | async-start | bytes 163840 | tf_op jit(solution)/shard_map/all_to_all | solution.py:230
  49.3 6.8 %shard_map.111.refs_2_ = f32[64,8,128]{2,1,0:T(8,128)} custom-call(s32[64,128]{1,0:T(8,128)} %mat_ref.3, bf16[40,128]{1,0:T(8,128)(2,1)} %copy-done.9, bf16[40,128]{1,0:T(8,128)(2,1)} %copy-done.10, f32[12]{0:T(128)} %rho_ref.1, f32[12]{0:T(128)} %convert_element_type.8.mx_ref, f32[12]{0:T(128)} %convert_element_type.7.my_ref, f32[12]{0:T(128)} %dd_ref.1), custom_call_target="tpu_custom_call" | custom-call | flops 1000000 | bytes 1000000 | tf_op jit(solution)/shard_map/pallas_call | solution.py:92
  56.1 0.9 copy-done
  57.0 3.4 %shard_map.112 = (bf16[64,96,128]{2,1,0:T(8,128)(2,1)S(1)}, bf16[64,96,128]{2,1,0:T(8,128)(2,1)S(1)}, bf16[64,32,128]{2,1,0:T(8,128)(2,1)S(1)}, bf16[64,32,128]{2,1,0:T(8,128)(2,1)S(1)}) custom-call(bf16[64,32,128]{2,1,0:T(8,128)(2,1)S(1)} %bitcast.41, bf16[2,40,128]{2,1,0:T(8,128)(2,1)S(1)} %pad_maximum_fusion.refs_1_, f32[64,8,128]{2,1,0:T(8,128)S(1)} %copy-done), custom_call_target="tpu_custom_call" | custom-call | flops 10000000 | bytes 4000000 | tf_op jit(solution)/shard_map/pallas_call | solution.py:153
  60.5 1.2 copy-done.3
  61.7 0.8 copy-done.5
  62.5 0.8 copy-done.7
  63.3 0.9 copy-done.1
  64.2 4.6 %shard_map.113 = (bf16[64,96,128]{2,1,0:T(8,128)(2,1)S(1)}, bf16[64,96,128]{2,1,0:T(8,128)(2,1)S(1)}) custom-call(bf16[64,32,128]{2,1,0:T(8,128)(2,1)} %collective-permute-done.2.refs_0_, bf16[2,40,128]{2,1,0:T(8,128)(2,1)S(1)} %get-tuple-element.60.refs_1_, f32[64,8,128]{2,1,0:T(8,128)S(1)} %copy-done.1), custom_call_target="tpu_custom_call" | custom-call | flops 10000000 | bytes 4000000 | tf_op jit(solution)/shard_map/pallas_call | solution.py:153
  68.8 4.4 %shard_map.114 = (bf16[64,96,128]{2,1,0:T(8,128)(2,1)S(1)}, bf16[64,96,128]{2,1,0:T(8,128)(2,1)S(1)}) custom-call(bf16[64,32,128]{2,1,0:T(8,128)(2,1)} %collective-permute-done.3.refs_0_, bf16[2,40,128]{2,1,0:T(8,128)(2,1)S(1)} %get-tuple-element.59.refs_1_, f32[64,8,128]{2,1,0:T(8,128)S(1)} %copy-done.1), custom_call_target="tpu_custom_call" | custom-call | flops 10000000 | bytes 4000000 | tf_op jit(solution)/shard_map/pallas_call | solution.py:153
  73.3 4.4 %shard_map.115 = (bf16[64,96,128]{2,1,0:T(8,128)(2,1)S(1)}, bf16[64,96,128]{2,1,0:T(8,128)(2,1)S(1)}) custom-call(bf16[64,32,128]{2,1,0:T(8,128)(2,1)} %collective-permute-done.4.refs_0_, bf16[2,40,128]{2,1,0:T(8,128)(2,1)S(1)} %get-tuple-element.58.refs_1_, f32[64,8,128]{2,1,0:T(8,128)S(1)} %copy-done.1), custom_call_target="tpu_custom_call" | custom-call | flops 10000000 | bytes 4000000 | tf_op jit(solution)/shard_map/pallas_call | solution.py:153
  77.8 8.0 %shard_map.116 = f32[8,4,12,128]{3,2,1,0:T(8,128)S(1)} custom-call(bf16[64,96,128]{2,1,0:T(8,128)(2,1)S(1)} %get-tuple-element.15.refs_0_, bf16[64,96,128]{2,1,0:T(8,128)(2,1)S(1)} %copy-done.4, bf16[64,96,128]{2,1,0:T(8,128)(2,1)S(1)} %get-tuple-element.17.refs_2_, bf16[64,96,128]{2,1,0:T(8,128)(2,1)S(1)} %get-tuple-element.18.refs_3_, ...), custom_call_target="tpu_custom_call" | custom-call | flops 2000000000 | bytes 14000000 | tf_op jit(solution)/shard_map/pallas_call | solution.py:205
  85.8 20.6 %all_to_all.20 = f32[8,4,12,128]{3,1,2,0:T(4,128)S(1)} all-to-all(f32[8,4,12,128]{3,1,2,0:T(4,128)S(1)} %copy.43), channel_id=1, replica_groups=mesh['y'=8,'zl'=4,'x'=4,'zh'=2,'c'=2] {'y'}, dimensions={0} | all-to-all | bytes 393216 | tf_op jit(solution)/shard_map/all_to_all | solution.py:248
  106.5 11.4 %all_to_all.21 = f32[16,12,128]{2,1,0:T(8,128)S(1)} all-to-all(f32[16,12,128]{2,1,0:T(8,128)S(1)} %bitcast.47), channel_id=1, replica_groups=mesh['y'=8,'zl'=4,'x'=4,'zh'=2,'c'=2] {'x','zl'}, dimensions={0} | all-to-all | bytes 196608 | tf_op jit(solution)/shard_map/all_to_all | solution.py:250
  117.9 0.7 broadcast_in_dim.8
  118.6 3.4 %all-to-all-start.3 = ((f32[8,4,12,128]{3,1,2,0:T(4,128)}), f32[8,4,12,128]{3,1,2,0:T(4,128)S(1)}, u32[]{:S(2)}, u32[]{:S(2)}) async-start(f32[8,4,12,128]{3,1,2,0:T(4,128)} %broadcast_in_dim.8), calls=%async_computation.3 | async-start | bytes 393216 | tf_op jit(solution)/shard_map/all_to_all | solution.py:252
  122.0 1.0 copy.48
  123.0 1.0 copy.49
  124.0 7.7 %all-to-all-done.3 = f32[8,4,12,128]{3,1,2,0:T(4,128)S(1)} async-done(((f32[8,4,12,128]{3,1,2,0:T(4,128)}), f32[8,4,12,128]{3,1,2,0:T(4,128)S(1)}, u32[]{:S(2)}, u32[]{:S(2)}) %all-to-all-start.3) | async-done | bytes 196640 | tf_op jit(solution)/shard_map/all_to_all | solution.py:252
  (43 shorter events, 2.7 us)
Async XLA Ops:
  0.6 14.5 %copy-start.11 = (bf16[12]{0:T(256)(128)(2,1)S(1)}, bf16[12]{0:T(256)(128)(2,1)}, u32[]{:S(2)}) copy-start(bf16[12]{0:T(256)(128)(2,1)} %param.12) | copy-start | bytes 76
  0.6 48.1 %copy-start.12 = (bf16[12]{0:T(256)(128)(2,1)S(1)}, bf16[12]{0:T(256)(128)(2,1)}, u32[]{:S(2)}) copy-start(bf16[12]{0:T(256)(128)(2,1)} %param.11) | copy-start | bytes 76
  2.0 38.2 %collective-permute-start.6 = (bf16[64,32,128]{2,1,0:T(8,128)(2,1)S(1)}, bf16[64,32,128]{2,1,0:T(8,128)(2,1)S(1)}, u32[]{:S(2)}, u32[]{:S(2)}) collective-permute-start(bf16[64,32,128]{2,1,0:T(8,128)(2,1)S(1)} %bitcast.42), channel_id=1, source_target_pairs={{0,2},{2,0},{1,3},{3,1},{4,6},{6,4},{5,7},{7,5},{8,10},{10,8},{9,1... | collective-permute-start | bytes 1572872 | tf_op jit(solution)/shard_map/ppermute | solution.py:18
  15.2 40.9 %copy-start.2 = (bf16[32,64,128]{2,0,1:T(8,128)(2,1)S(1)}, bf16[32,64,128]{2,0,1:T(8,128)(2,1)}, u32[]{:S(2)}) copy-start(bf16[32,64,128]{2,0,1:T(8,128)(2,1)} %copy.56) | copy-start | bytes 1572868
  23.1 12.8 %collective-permute-start = (bf16[40,128]{1,0:T(8,128)(2,1)S(1)}, bf16[40,128]{1,0:T(8,128)(2,1)S(1)}, u32[]{:S(2)}, u32[]{:S(2)}) collective-permute-start(bf16[40,128]{1,0:T(8,128)(2,1)S(1)} %get-tuple-element.61), channel_id=1, source_target_pairs={{0,16},{16,32},{32,48},{48,64},{64,80},{80,96},{96,112},{112,128},... | collective-permute-start | bytes 30728 | tf_op jit(solution)/shard_map/ppermute | solution.py:226
  26.5 11.8 %collective-permute-start.1 = (bf16[40,128]{1,0:T(8,128)(2,1)S(1)}, bf16[40,128]{1,0:T(8,128)(2,1)S(1)}, u32[]{:S(2)}, u32[]{:S(2)}) collective-permute-start(bf16[40,128]{1,0:T(8,128)(2,1)S(1)} %get-tuple-element.62), channel_id=1, source_target_pairs={{16,0},{32,16},{48,32},{64,48},{80,64},{96,80},{112,96},{128,112},... | collective-permute-start | bytes 30728 | tf_op jit(solution)/shard_map/ppermute | solution.py:227
  27.8 35.5 %collective-permute-start.2 = (bf16[64,32,128]{2,1,0:T(8,128)(2,1)}, bf16[64,32,128]{2,1,0:T(8,128)(2,1)}, u32[]{:S(2)}, u32[]{:S(2)}) collective-permute-start(bf16[64,32,128]{2,1,0:T(8,128)(2,1)} %bitcast.38), channel_id=1, source_target_pairs={{0,12},{4,0},{8,4},{12,8},{1,13},{5,1},{9,5},{13,9},{2,14},{6,2},{... | collective-permute-start | bytes 1572872 | tf_op jit(solution)/shard_map/ppermute | solution.py:18
  30.5 38.3 %collective-permute-start.3 = (bf16[64,32,128]{2,1,0:T(8,128)(2,1)}, bf16[64,32,128]{2,1,0:T(8,128)(2,1)}, u32[]{:S(2)}, u32[]{:S(2)}) collective-permute-start(bf16[64,32,128]{2,1,0:T(8,128)(2,1)} %bitcast.39), channel_id=1, source_target_pairs={{0,8},{4,12},{8,0},{12,4},{1,9},{5,13},{9,1},{13,5},{2,10},{6,14},... | collective-permute-start | bytes 1572872 | tf_op jit(solution)/shard_map/ppermute | solution.py:18
  35.9 13.4 %copy-start.9 = (bf16[40,128]{1,0:T(8,128)(2,1)}, bf16[40,128]{1,0:T(8,128)(2,1)S(1)}, u32[]{:S(2)}) copy-start(bf16[40,128]{1,0:T(8,128)(2,1)S(1)} %collective-permute-done.left_ref) | copy-start | bytes 30724
  35.9 37.4 %collective-permute-start.4 = (bf16[64,32,128]{2,1,0:T(8,128)(2,1)}, bf16[64,32,128]{2,1,0:T(8,128)(2,1)}, u32[]{:S(2)}, u32[]{:S(2)}) collective-permute-start(bf16[64,32,128]{2,1,0:T(8,128)(2,1)} %bitcast.40), channel_id=1, source_target_pairs={{0,4},{4,8},{8,12},{12,0},{1,5},{5,9},{9,13},{13,1},{2,6},{6,10},{... | collective-permute-start | bytes 1572872 | tf_op jit(solution)/shard_map/ppermute | solution.py:18
  38.3 11.0 %copy-start.10 = (bf16[40,128]{1,0:T(8,128)(2,1)}, bf16[40,128]{1,0:T(8,128)(2,1)S(1)}, u32[]{:S(2)}) copy-start(bf16[40,128]{1,0:T(8,128)(2,1)S(1)} %collective-permute-done.1.right_ref) | copy-start | bytes 30724
  38.3 39.5 %collective-permute-start.5 = (bf16[64,32,128]{2,1,0:T(8,128)(2,1)S(1)}, bf16[64,32,128]{2,1,0:T(8,128)(2,1)}, u32[]{:S(2)}, u32[]{:S(2)}) collective-permute-start(bf16[64,32,128]{2,1,0:T(8,128)(2,1)S(1)} %bitcast.43), channel_id=1, source_target_pairs={{0,1},{1,0},{2,3},{3,2},{4,5},{5,4},{6,7},{7,6},{8,9},{9,8},{10,11... | collective-permute-start | bytes 1572872 | tf_op jit(solution)/shard_map/ppermute | solution.py:18
  40.2 37.5 %collective-permute-start.7 = (bf16[64,32,128]{2,1,0:T(8,128)(2,1)S(1)}, bf16[64,32,128]{2,1,0:T(8,128)(2,1)}, u32[]{:S(2)}, u32[]{:S(2)}) collective-permute-start(bf16[64,32,128]{2,1,0:T(8,128)(2,1)S(1)} %collective-permute-done.6.refs_10_), channel_id=1, source_target_pairs={{0,1},{1,0},{2,3},{3,2},{4,5},{5,4},{6,7},{7,6},{8,9},{9,8},{10,11... | collective-permute-start | bytes 1572872 | tf_op jit(solution)/shard_map/ppermute | solution.py:18
  43.3 20.0 %all-to-all-start = ((bf16[4,2,40,128]{3,2,1,0:T(8,128)(2,1)}), bf16[4,2,40,128]{3,2,1,0:T(8,128)(2,1)S(1)}, u32[]{:S(2)}, u32[]{:S(2)}) async-start(bf16[4,2,40,128]{3,2,1,0:T(8,128)(2,1)} %broadcast_in_dim.6), calls=%async_computation | async-start | bytes 163840 | tf_op jit(solution)/shard_map/all_to_all | solution.py:230
  56.1 1.0 copy-start
  60.5 1.2 copy-start.3
  61.7 0.8 copy-start.5
  62.5 0.8 copy-start.7
  63.3 1.0 copy-start.1
  64.2 13.5 %copy-start.4 = (bf16[64,96,128]{2,1,0:T(8,128)(2,1)S(1)}, bf16[64,96,128]{2,1,0:T(8,128)(2,1)}, u32[]{:S(2)}) copy-start(bf16[64,96,128]{2,1,0:T(8,128)(2,1)} %copy-done.3) | copy-start | bytes 4718596
  85.7 36.2 %copy-start.8 = (bf16[64,32,128]{2,1,0:T(8,128)(2,1)S(1)}, bf16[64,32,128]{2,1,0:T(8,128)(2,1)}, u32[]{:S(2)}) copy-start(bf16[64,32,128]{2,1,0:T(8,128)(2,1)} %copy-done.7) | copy-start | bytes 1572868
  85.8 37.2 %copy-start.6 = (bf16[64,32,128]{2,1,0:T(8,128)(2,1)S(1)}, bf16[64,32,128]{2,1,0:T(8,128)(2,1)}, u32[]{:S(2)}) copy-start(bf16[64,32,128]{2,1,0:T(8,128)(2,1)} %copy-done.5) | copy-start | bytes 1572868
  118.6 13.1 %all-to-all-start.3 = ((f32[8,4,12,128]{3,1,2,0:T(4,128)}), f32[8,4,12,128]{3,1,2,0:T(4,128)S(1)}, u32[]{:S(2)}, u32[]{:S(2)}) async-start(f32[8,4,12,128]{3,1,2,0:T(4,128)} %broadcast_in_dim.8), calls=%async_computation.3 | async-start | bytes 393216 | tf_op jit(solution)/shard_map/all_to_all | solution.py:252

commit v2 on v1

v2 whole, which is shorter than its diff:
```python
import jax
import jax.numpy as jnp
from jax import lax
from jax.experimental import pallas as pl
from jax.experimental.pallas import tpu as pltpu
from jax.sharding import Mesh, PartitionSpec as P

SPACE = ("y", "zl")
MODE = ("x", "zh", "c")
R, M, C = 64, 32, 128
F32, BF16 = jnp.float32, jnp.bfloat16
VM = pl.BlockSpec(memory_space=pltpu.VMEM)
SM = pl.BlockSpec(memory_space=pltpu.SMEM)


def shifted(value, axis, step):
    n = lax.axis_size(axis)
    return lax.ppermute(value, axis, [(i, (i + step) % n) for i in range(n)])


def select_table(material, tables_ref, which):
    value = jnp.zeros(material.shape, F32)
    for level in range(tables_ref.shape[1]):
        value = jnp.where(material == level, tables_ref[which, level], value)
    return value


def edges_kernel(u_ref, mat_ref, tables_ref, first_ref, last_ref, ky):
    ky[...] = select_table(mat_ref[...], tables_ref, 2)
    pair = lax.broadcasted_iota(jnp.int32, (8, C), 1) // 2
    firsts, lasts = [], []
    for m in range(0, M + 8, 8):
        first = last = jnp.zeros((8, C), F32)
        for r in range(R):
            v = u_ref[r, m : m + 8, :].astype(F32) if m < M else jnp.broadcast_to(ky[r : r + 1, :], (8, C))
            first = jnp.where(pair == r, pltpu.roll(v, 2 * r, 1), first)
            last = jnp.where(pair == r, pltpu.roll(v, (2 * r + 2) % C, 1), last)
        firsts.append(first)
        lasts.append(last)
    first_ref[...] = jnp.concatenate(firsts, axis=0).astype(BF16)
    last_ref[...] = jnp.concatenate(lasts, axis=0).astype(BF16)


def edges(u, material, tables):
    return pl.pallas_call(
        edges_kernel,
        out_shape=[jax.ShapeDtypeStruct((M + 8, C), BF16)] * 2,
        in_specs=[VM, VM, SM],
        out_specs=[VM] * 2,
        scratch_shapes=[pltpu.VMEM((R, C), F32)],
        cost_estimate=pl.CostEstimate(flops=10**6, bytes_accessed=10**6, transcendentals=0),
    )(u, material, tables)


def fields_kernel(mat_ref, left_ref, right_ref, tables_ref, f_ref, kx, ky, rho, dd):
    material = mat_ref[...]
    kx[...] = jnp.zeros(kx.shape, F32)
    kx[8 : 8 + R, :] = select_table(material, tables_ref, 1)
    ky[...] = select_table(material, tables_ref, 2)
    rho[...] = select_table(material, tables_ref, 0)
    dd[...] = select_table(material, tables_ref, 3)
    lane = lax.broadcasted_iota(jnp.int32, (1, C), 1)
    left = left_ref[M : M + 8, :].astype(F32)
    right = right_ref[M : M + 8, :].astype(F32)

    for r in range(R):
        k = ky[r : r + 1, :]
        kl = pltpu.roll(left, C - 1 - 2 * r, 1)[0:1]
        kr = pltpu.roll(right, C - 1 - 2 * r, 1)[0:1]
        k8 = jnp.broadcast_to(k, (8, C))
        south = jnp.where(lane == 0, kl, pltpu.roll(k8, 1, 1)[0:1])
        north = jnp.where(lane == C - 1, kr, pltpu.roll(k8, C - 1, 1)[0:1])
        kc = kx[r + 8 : r + 9, :]
        fe = 0.5 * (kc + kx[r + 9 : r + 10, :])
        fw = 0.5 * (kc + kx[r + 7 : r + 8, :])
        fn = 0.5 * (k + north)
        fs = 0.5 * (k + south)
        rr = rho[r : r + 1, :]
        rows = [rr * (2.0 / 3.0), rr * (1.0 / 12.0), fe + fw + fn + fs, fe, fw, fn, fs, dd[r : r + 1, :]]
        f_ref[r] = jnp.concatenate(rows, axis=0)


def fields(material, left, right, tables):
    return pl.pallas_call(
        fields_kernel,
        out_shape=jax.ShapeDtypeStruct((R, 8, C), F32),
        in_specs=[VM, VM, VM, SM],
        out_specs=VM,
        scratch_shapes=[pltpu.VMEM((R + 16, C), F32)] + [pltpu.VMEM((R, C), F32)] * 3,
        cost_estimate=pl.CostEstimate(flops=10**6, bytes_accessed=10**6, transcendentals=0),
    )(material, left, right, tables)


PIECE = 3 * M // 8
ROWS = 8


def panel_kernel(with_images, appends, u_ref, halo_ref, f_ref, *rest):
    olds, rest = rest[:4], rest[4:]
    before_ref, rest = (rest[0], rest[1:]) if appends else (None, rest)
    if with_images:
        out_ref, mass_ref, stiff_ref, us, s1, s2, q, img, acc = rest
    else:
        out_ref, us, s1, s2, q, img, acc = rest
    zero = jnp.zeros((M, C), F32)
    for r in (0, 1, R + 2, R + 3):
        us[r] = zero
    s1[0] = zero
    s1[R + 1] = zero
    lane = lax.broadcasted_iota(jnp.int32, (1, C), 1)
    left = halo_ref[0].astype(F32)[0:M]
    right = halo_ref[1].astype(F32)[0:M]
    first = jnp.where(lane % 2 == 0, right, left)
    right = pltpu.roll(right, C - 2, 1)
    second = [jnp.where((lane // 2) % 2 == p, left, right) for p in (0, 1)]

    for r in range(R):
        u = u_ref[r].astype(F32)
        h1 = pltpu.roll(first, C - 1 - 2 * r, 1)
        h2 = pltpu.roll(second[r % 2], (C - 2 * r) % C, 1)
        south = jnp.where(lane == 0, h1, pltpu.roll(u, 1, 1))
        south2 = jnp.where(lane < 2, h2, pltpu.roll(u, 2, 1))
        north = jnp.where(lane == C - 1, h1, pltpu.roll(u, C - 1, 1))
        north2 = jnp.where(lane >= C - 2, h2, pltpu.roll(u, C - 2, 1))
        us[r + 2] = u
        s1[r + 1] = south + north
        s2[r] = south2 + north2
        q[r] = f_ref[r, 5:6, :] * north + f_ref[r, 6:7, :] * south

    acc[...] = jnp.zeros(acc.shape, F32)

    def rows(step, _):
        base = step * ROWS
        for j in range(ROWS):
            r = base + j
            u, east, west = us[r + 2], us[r + 3], us[r + 1]
            near = (east + west) + s1[r + 1]
            mass = f_ref[r, 0:1, :] * u + f_ref[r, 1:2, :] * near
            membrane = f_ref[r, 2:3, :] * u - f_ref[r, 3:4, :] * east - f_ref[r, 4:5, :] * west - q[r]
            far = (us[r + 4] + us[r]) + s2[r]
            diagonal = s1[r] + s1[r + 2]
            bending = f_ref[r, 7:8, :] * (20.0 * u - 8.0 * near + 2.0 * diagonal + far)
            for i, v in enumerate((mass, membrane, bending)):
                hi = v.astype(BF16)
                lo = (v - hi.astype(F32)).astype(BF16)
                img[step % 2, M * i : M * i + M, C * j : C * j + C] = hi
                img[step % 2, M * (i + 3) : M * (i + 3) + M, C * j : C * j + C] = lo
            if with_images:
                mass_ref[r] = mass.astype(BF16)
                stiff_ref[r] = (membrane + bending).astype(BF16)
        wide = [jnp.concatenate([o[base + j] for j in range(ROWS)], axis=1) for o in olds]
        acc[...] += lax.dot_general(
            img[step % 2], jnp.concatenate(wide, axis=0), (((1,), (1,)), ((), ())), preferred_element_type=F32
        )
        return 0

    for step in range(R // ROWS):
        rows(step, 0)
    zh, c = lax.axis_index("zh"), lax.axis_index("c")
    v = pltpu.roll(acc[0 : 3 * M] + acc[3 * M : 6 * M], zh * 64, 1)
    lane = lax.broadcasted_iota(jnp.int32, (1, 4 * M), 1)
    swapped = jnp.where(lane % 64 < 32, pltpu.roll(v, 96, 1), pltpu.roll(v, 32, 1))
    v = jnp.where(c == 1, swapped, v)
    for i in range(8):
        if appends:
            out_ref[i, 0:PIECE] = before_ref[i]
            out_ref[i, PIECE : 2 * PIECE] = v[PIECE * i : PIECE * i + PIECE]
        else:
            out_ref[i] = v[PIECE * i : PIECE * i + PIECE]


def panel(u, halo, f, olds, before, with_images):
    outs = [jax.ShapeDtypeStruct((8, PIECE if before is None else 2 * PIECE, 4 * M), F32)]
    outs += [jax.ShapeDtypeStruct((R, M, C), BF16)] * (2 if with_images else 0)
    operands = [u, halo, f, *olds] + ([] if before is None else [before])
    return pl.pallas_call(
        lambda *refs: panel_kernel(with_images, before is not None, *refs),
        out_shape=outs,
        in_specs=[VM] * len(operands),
        out_specs=[VM] * len(outs),
        scratch_shapes=[
            pltpu.VMEM((R + 4, M, C), F32),
            pltpu.VMEM((R + 2, M, C), F32),
            pltpu.VMEM((R, M, C), F32),
            pltpu.VMEM((R, M, C), F32),
            pltpu.VMEM((2, 6 * M, ROWS * C), BF16),
            pltpu.VMEM((6 * M, 4 * M), F32),
        ],
        compiler_params=pltpu.CompilerParams(vmem_limit_bytes=16 * 2**20),
        cost_estimate=pl.CostEstimate(flops=4 * 10**8, bytes_accessed=4 * 10**6, transcendentals=0),
    )(*operands)


def small(kernel, out_shape, *operands):
    return pl.pallas_call(
        kernel,
        out_shape=out_shape,
        in_specs=[VM] * len(operands),
        out_specs=jax.tree.map(lambda _: VM, out_shape),
        cost_estimate=pl.CostEstimate(flops=10**5, bytes_accessed=4 * 10**5, transcendentals=0),
    )(*operands)


def added(ref, axis_size, *at):
    total = ref[(0, *at)]
    for i in range(1, axis_size):
        total = total + ref[(i, *at)]
    return total


def to_chips_kernel(first_ref, second_ref, out_ref):
    x = lax.axis_index("x")
    first, second = added(first_ref, 8), added(second_ref, 8)
    for d, v in ((0, first[:PIECE]), (1, first[PIECE:]), (3, second[:PIECE]), (2, second[PIECE:])):
        place = lax.rem(x + d, 4) * 4
        for z in range(4):
            out_ref[place + z] = v


def to_y_kernel(in_ref, out_ref):
    for x in range(4):
        v = in_ref[4 * x] + in_ref[4 * x + 1] + in_ref[4 * x + 2] + in_ref[4 * x + 3]
        for y in range(8):
            out_ref[y, PIECE * x : PIECE * x + PIECE] = v


def crosses_kernel(in_ref, mass_ref, membrane_ref, bending_ref):
    area = 1.0 / (R * C * 32)
    for x in range(4):
        v = jnp.concatenate([in_ref[y, PIECE * x : PIECE * x + PIECE] for y in range(8)], axis=0) * area
        for i, ref in enumerate((mass_ref, membrane_ref, bending_ref)):
            ref[:, 4 * M * x : 4 * M * x + 4 * M] = v[M * i : M * i + M]


def local(old_modes, new_modes, material, density, memb_x, memb_y, bend_table):
    tables = jnp.stack([density, memb_x.astype(F32), memb_y.astype(F32), bend_table])
    old = old_modes.transpose(1, 0, 2)
    new = new_modes.transpose(1, 0, 2)
    other = shifted(old, "zh", 1)
    panels = [new] + [shifted(new, "x", -d) for d in (1, 2, 3)]
    first, last = edges(new, material, tables)
    n = 32
    left = lax.ppermute(last, SPACE, [(i, i + 1) for i in range(n - 1)])
    right = lax.ppermute(first, SPACE, [(i + 1, i) for i in range(n - 1)])
    halo = jnp.stack([left, right])
    halos = lax.all_to_all(jnp.broadcast_to(halo[None], (4, *halo.shape)), "x", 0, 0)
    x = lax.axis_index("x")
    beside = [halo] + [lax.dynamic_index_in_dim(halos, lax.rem(x + d, 4), 0, keepdims=False) for d in (1, 2, 3)]
    olds = (old, shifted(old, "c", 1), other, shifted(other, "c", 1))
    f = fields(material, left, right, tables)
    part, mass, stiff = panel(new, halo, f, olds, None, True)
    (part,) = panel(panels[1], beside[1], f, olds, part, False)
    early = lax.all_to_all(part, "y", 0, 0)
    (part,) = panel(panels[3], beside[3], f, olds, None, False)
    (part,) = panel(panels[2], beside[2], f, olds, part, False)
    late = lax.all_to_all(part, "y", 0, 0)
    part = small(to_chips_kernel, jax.ShapeDtypeStruct((16, PIECE, 4 * M), F32), early, late)
    part = lax.all_to_all(part, ("x", "zl"), 0, 0)
    part = small(to_y_kernel, jax.ShapeDtypeStruct((8, 4 * PIECE, 4 * M), F32), part)
    part = lax.all_to_all(part, "y", 0, 0)
    crosses = small(crosses_kernel, [jax.ShapeDtypeStruct((M, 16 * M), F32)] * 3, part)
    return (*[v.T for v in crosses], mass.transpose(1, 0, 2), stiff.transpose(1, 0, 2))


def solution(mesh):
    fine = Mesh(mesh.devices.reshape(8, 4, 4, 2, 2), ("y", "zl", "x", "zh", "c"))
    in_specs = (
        P(MODE, None, SPACE),
        P(MODE, None, SPACE),
        P(None, SPACE),
        P(),
        P(),
        P(),
        P(),
    )
    out_specs = (
        P(None, MODE),
        P(None, MODE),
        P(None, MODE),
        P(MODE, None, SPACE),
        P(MODE, None, SPACE),
    )
    return jax.shard_map(local, mesh=fine, in_specs=in_specs, out_specs=out_specs, check_vma=False)
```

time: 134 us -> 143 us (1.067)
  starting transfers between devices: 36.9 us -> 56.7 us
  Pallas kernels: 38.4 us -> 22.1 us
  waiting for transfers between devices: 10 us -> 24 us
  local copies, waits for them, and re-layouts: 13.2 us -> 7.54 us
  blocking collectives: 31.9 us -> 29.6 us
    pallas_call x6 -> x8, Pallas kernels: 31.6 us -> 20.2 us  [the longest x4 13.2 us: panel(): pl.pallas_call(lambda *refs: panel_kernel(with_images, before is not None...]
    ppermute x2, starting transfers between devices: 4.66 us -> 16 us  [the longest x1 14.7 us: local(): left = lax.ppermute(last, SPACE, [(i, i + 1) for i in range(n - 1)])]
    all_to_all x1 -> x2, starting transfers between devices: 3.39 us -> 10.6 us  [the longest x1 7.25 us: local(): late = lax.all_to_all(part, 'y', 0, 0)]
    all_to_all x1, waiting for transfers between devices: 0.01 us -> 5.5 us  [local(): lax.all_to_all(jnp.broadcast_to(halo[None], (4, *halo.shape)), 'x', 0, 0)]
    pallas_call x1, Pallas kernels: 6.79 us -> 1.91 us  [fields(): pl.pallas_call(fields_kernel, out_shape=jax.ShapeDtypeStruct((R, 8, C), F...]
    ppermute x2, waiting for transfers between devices: 2.31 us -> 6.33 us  [the longest x1 4.75 us: local(): right = lax.ppermute(first, SPACE, [(i + 1, i) for i in range(n - 1)])]
    unnamed x30 -> x34, local copies, waits for them, and re-layouts: 10.3 us -> 6.89 us
    ppermute x6, waiting for transfers between devices: 0.02 us -> 2.9 us  [shifted(): return lax.ppermute(value, axis, [(i, (i + step) % n) for i in range(n)])]
  transfers between devices with their start and end apart: 10 -> 11, of which waited for: 2 -> 6; matrix products, arithmetic and copies ran while one was open for 5% -> 3% of each run, Pallas kernels for 23% -> 12%
where the time goes in v2:
time: 143 us; the launch traced here: 141 us
  starting transfers between devices  56.7 us (40%)
  blocking collectives  29.6 us (21%)
  waiting for transfers between devices  24 us (17%)
  Pallas kernels  22.1 us (15%)
  local copies, waits for them, and re-layouts  7.54 us (5%)
    ppermute x6, starting transfers between devices, shifted(): return lax.ppermute(value, axis, [(i, (i + step) % n) for i in range(n)])  24.3 us
    all_to_all x1, blocking collectives, local(): part = lax.all_to_all(part, ('x', 'zl'), 0, 0)  15.3 us
    ppermute x1, starting transfers between devices, local(): left = lax.ppermute(last, SPACE, [(i, i + 1) for i in range(n - 1)])  14.7 us
    all_to_all x1, blocking collectives, local(): early = lax.all_to_all(part, 'y', 0, 0)  14.3 us
    pallas_call x4, Pallas kernels, panel(): pl.pallas_call(lambda *refs: panel_kernel(with_images, before is not None...  13.2 us
    all_to_all x1, waiting for transfers between devices, local(): part = lax.all_to_all(part, 'y', 0, 0)  7.68 us
    all_to_all x1, starting transfers between devices, local(): late = lax.all_to_all(part, 'y', 0, 0)  7.25 us
    unnamed x34, local copies, waits for them, and re-layouts  6.89 us
  transfers between devices with their start and end apart: 11, of which 6 were waited for; matrix products, arithmetic and copies ran while one was open for 3% of the time, Pallas kernels for 12%

profile of v2, /device:TPU:6, one launch (start us, length us, event | category | flops | bytes accessed | tf_op | source)
XLA Modules:
  0.0 141.4 jit_solution(16948166197581727621)
XLA Ops:
  0.6 1.4 %copy.18 = bf16[32,64,128]{2,0,1:T(8,128)(2,1)S(1)} copy(bf16[32,64,128]{2,1,0:T(8,128)(2,1)} %param.7) | data formatting | bytes 1048576 | tf_op args[0]
  2.1 10.9 %collective-permute-start.4 = (bf16[64,32,128]{2,1,0:T(8,128)(2,1)S(1)}, bf16[64,32,128]{2,1,0:T(8,128)(2,1)S(1)}, u32[]{:S(2)}, u32[]{:S(2)}) collective-permute-start(bf16[64,32,128]{2,1,0:T(8,128)(2,1)S(1)} %bitcast.27), channel_id=1, source_target_pairs={{0,2},{2,0},{1,3},{3,1},{4,6},{6,4},{5,7},{7,5},{8,10},{10,8},{9,1... | collective-permute-start | bytes 1572872 | tf_op jit(solution)/shard_map/ppermute | solution.py:18
  13.0 1.9 %collective-permute-start.3 = (bf16[64,32,128]{2,1,0:T(8,128)(2,1)S(1)}, bf16[64,32,128]{2,1,0:T(8,128)(2,1)S(1)}, u32[]{:S(2)}, u32[]{:S(2)}) collective-permute-start(bf16[64,32,128]{2,1,0:T(8,128)(2,1)S(1)} %bitcast.28), channel_id=1, source_target_pairs={{0,1},{1,0},{2,3},{3,2},{4,5},{5,4},{6,7},{7,6},{8,9},{9,8},{10,11... | collective-permute-start | bytes 1572872 | tf_op jit(solution)/shard_map/ppermute | solution.py:18
  15.3 2.5 %collective-permute-start.7 = (bf16[64,32,128]{2,1,0:T(8,128)(2,1)S(1)}, bf16[64,32,128]{2,1,0:T(8,128)(2,1)}, u32[]{:S(2)}, u32[]{:S(2)}) collective-permute-start(bf16[64,32,128]{2,1,0:T(8,128)(2,1)S(1)} %bitcast.33), channel_id=1, source_target_pairs={{0,4},{4,8},{8,12},{12,0},{1,5},{5,9},{9,13},{13,1},{2,6},{6,10},{... | collective-permute-start | bytes 1572872 | tf_op jit(solution)/shard_map/ppermute | solution.py:18
  17.9 4.3 %collective-permute-start.6 = (bf16[64,32,128]{2,1,0:T(8,128)(2,1)S(1)}, bf16[64,32,128]{2,1,0:T(8,128)(2,1)S(1)}, u32[]{:S(2)}, u32[]{:S(2)}) collective-permute-start(bf16[64,32,128]{2,1,0:T(8,128)(2,1)S(1)} %bitcast.34), channel_id=1, source_target_pairs={{0,8},{4,12},{8,0},{12,4},{1,9},{5,13},{9,1},{13,5},{2,10},{6,14},... | collective-permute-start | bytes 1572872 | tf_op jit(solution)/shard_map/ppermute | solution.py:18
  22.2 2.9 %collective-permute-done.4.refs_5_ = bf16[64,32,128]{2,1,0:T(8,128)(2,1)S(1)} collective-permute-done((bf16[64,32,128]{2,1,0:T(8,128)(2,1)S(1)}, bf16[64,32,128]{2,1,0:T(8,128)(2,1)S(1)}, u32[]{:S(2)}, u32[]{:S(2)}) %collective-permute-start.4) | collective-permute-done | bytes 524320 | tf_op jit(solution)/shard_map/ppermute | solution.py:18
  25.1 1.9 %collective-permute-start.5 = (bf16[64,32,128]{2,1,0:T(8,128)(2,1)S(1)}, bf16[64,32,128]{2,1,0:T(8,128)(2,1)S(1)}, u32[]{:S(2)}, u32[]{:S(2)}) collective-permute-start(bf16[64,32,128]{2,1,0:T(8,128)(2,1)S(1)} %collective-permute-done.4.refs_5_), channel_id=1, source_target_pairs={{0,1},{1,0},{2,3},{3,2},{4,5},{5,4},{6,7},{7,6},{8,9},{9,8},{10,11... | collective-permute-start | bytes 1572872 | tf_op jit(solution)/shard_map/ppermute | solution.py:18
  28.3 2.1 %shard_map.110 = (bf16[40,128]{1,0:T(8,128)(2,1)}, bf16[40,128]{1,0:T(8,128)(2,1)}) custom-call(bf16[64,32,128]{2,1,0:T(8,128)(2,1)} %bitcast.35, s32[64,128]{1,0:T(8,128)} %mat_ref.3, f32[4,12]{1,0:T(4,128)} %pad_maximum_fusion.1.tables_ref), custom_call_target="tpu_custom_call" | custom-call | flops 1000000 | bytes 1000000 | tf_op jit(solution)/shard_map/pallas_call | solution.py:45
  30.4 14.7 %collective-permute-start.1 = (bf16[40,128]{1,0:T(8,128)(2,1)}, bf16[40,128]{1,0:T(8,128)(2,1)S(1)}, u32[]{:S(2)}, u32[]{:S(2)}) collective-permute-start(bf16[40,128]{1,0:T(8,128)(2,1)} %get-tuple-element.13), channel_id=1, source_target_pairs={{0,16},{16,32},{32,48},{48,64},{64,80},{80,96},{96,112},{112,128},... | collective-permute-start | bytes 30728 | tf_op jit(solution)/shard_map/ppermute | solution.py:243
  45.1 1.6 %collective-permute-done.1.left_ref = bf16[40,128]{1,0:T(8,128)(2,1)S(1)} collective-permute-done((bf16[40,128]{1,0:T(8,128)(2,1)}, bf16[40,128]{1,0:T(8,128)(2,1)S(1)}, u32[]{:S(2)}, u32[]{:S(2)}) %collective-permute-start.1) | collective-permute-done | bytes 10272 | tf_op jit(solution)/shard_map/ppermute | solution.py:243
  46.7 1.3 collective-permute-start.2
  48.0 4.8 %collective-permute-done.2.right_ref = bf16[40,128]{1,0:T(8,128)(2,1)S(1)} collective-permute-done((bf16[40,128]{1,0:T(8,128)(2,1)}, bf16[40,128]{1,0:T(8,128)(2,1)S(1)}, u32[]{:S(2)}, u32[]{:S(2)}) %collective-permute-start.2) | collective-permute-done | bytes 10272 | tf_op jit(solution)/shard_map/ppermute | solution.py:244
  52.8 2.7 %collective-permute-start = (bf16[64,32,128]{2,1,0:T(8,128)(2,1)}, bf16[64,32,128]{2,1,0:T(8,128)(2,1)}, u32[]{:S(2)}, u32[]{:S(2)}) collective-permute-start(bf16[64,32,128]{2,1,0:T(8,128)(2,1)} %bitcast.36), channel_id=1, source_target_pairs={{0,12},{4,0},{8,4},{12,8},{1,13},{5,1},{9,5},{13,9},{2,14},{6,2},{... | collective-permute-start | bytes 1572872 | tf_op jit(solution)/shard_map/ppermute | solution.py:18
  56.2 5.7 %all-to-all-start = ((bf16[4,2,40,128]{3,2,1,0:T(8,128)(2,1)}), bf16[4,2,40,128]{3,2,1,0:T(8,128)(2,1)S(1)}, u32[]{:S(2)}, u32[]{:S(2)}) async-start(bf16[4,2,40,128]{3,2,1,0:T(8,128)(2,1)} %broadcast_in_dim.2), calls=%async_computation | async-start | bytes 163840 | tf_op jit(solution)/shard_map/all_to_all | solution.py:246
  61.8 1.9 %shard_map.111.refs_2_ = f32[64,8,128]{2,1,0:T(8,128)} custom-call(s32[64,128]{1,0:T(8,128)} %mat_ref.3, bf16[40,128]{1,0:T(8,128)(2,1)} %copy-done.9, bf16[40,128]{1,0:T(8,128)(2,1)} %copy-done.10, f32[4,12]{1,0:T(4,128)} %pad_maximum_fusion.1.tables_ref), custom_call_target="tpu_custom_call" | custom-call | flops 1000000 | bytes 1000000 | tf_op jit(solution)/shard_map/pallas_call | solution.py:84
  63.7 5.5 %all-to-all-done = bf16[4,2,40,128]{3,2,1,0:T(8,128)(2,1)S(1)} async-done(((bf16[4,2,40,128]{3,2,1,0:T(8,128)(2,1)}), bf16[4,2,40,128]{3,2,1,0:T(8,128)(2,1)S(1)}, u32[]{:S(2)}, u32[]{:S(2)}) %all-to-all-start) | async-done | bytes 81952 | tf_op jit(solution)/shard_map/all_to_all | solution.py:246
  69.3 0.9 copy-done
  70.2 3.6 %shard_map.114.refs_7_ = f32[8,12,128]{2,1,0:T(8,128)S(1)} custom-call(bf16[64,32,128]{2,1,0:T(8,128)(2,1)} %collective-permute-done.7.refs_0_, bf16[2,40,128]{2,1,0:T(8,128)(2,1)S(1)} %get-tuple-element.26.refs_1_, f32[64,8,128]{2,1,0:T(8,128)S(1)} %copy-done, bf16[64,32,128]{2,1,0:T(8,128)(2,1)S(1)} %bitcast.29, ...), custom_call_target="tpu_custom_call" | custom-call | flops 400000000 | bytes 4000000 | tf_op jit(solution)/shard_map/pallas_call | solution.py:176
  73.9 3.3 %shard_map.115 = f32[8,24,128]{2,1,0:T(8,128)} custom-call(bf16[64,32,128]{2,1,0:T(8,128)(2,1)S(1)} %collective-permute-done.6.refs_0_, bf16[2,40,128]{2,1,0:T(8,128)(2,1)S(1)} %get-tuple-element.27.refs_1_, f32[64,8,128]{2,1,0:T(8,128)S(1)} %copy-done, bf16[64,32,128]{2,1,0:T(8,128)(2,1)S(1)} %bitcast.30, ...), custom_call_target="tpu_custom_call" | custom-call | flops 400000000 | bytes 4000000 | tf_op jit(solution)/shard_map/pallas_call | solution.py:176
  77.2 7.2 %all-to-all-start.2 = ((f32[8,24,128]{2,1,0:T(8,128)}), f32[8,24,128]{2,1,0:T(8,128)S(1)}, u32[]{:S(2)}, u32[]{:S(2)}) async-start(f32[8,24,128]{2,1,0:T(8,128)} %shard_map.115), calls=%async_computation.2 | async-start | bytes 196608 | tf_op jit(solution)/shard_map/all_to_all | solution.py:256
  84.4 2.7 %shard_map.112 = (f32[8,12,128]{2,1,0:T(8,128)S(1)}, bf16[64,32,128]{2,1,0:T(8,128)(2,1)S(1)}, bf16[64,32,128]{2,1,0:T(8,128)(2,1)S(1)}) custom-call(bf16[64,32,128]{2,1,0:T(8,128)(2,1)S(1)} %bitcast.37, bf16[2,40,128]{2,1,0:T(8,128)(2,1)S(1)} %pad_maximum_fusion.refs_1_, f32[64,8,128]{2,1,0:T(8,128)S(1)} %copy-done.1, bf16[64,32,128]{2,1,0:T(8,128)(2,1)S(1)} %bitcast.31, ...), custom_call_target="tpu_custom_call" | custom-call | flops 400000000 | bytes 4000000 | tf_op jit(solution)/shard_map/pallas_call | solution.py:176
  87.9 3.7 %shard_map.113 = f32[8,24,128]{2,1,0:T(8,128)S(1)} custom-call(bf16[64,32,128]{2,1,0:T(8,128)(2,1)} %collective-permute-done.refs_0_, bf16[2,40,128]{2,1,0:T(8,128)(2,1)S(1)} %get-tuple-element.28.refs_1_, f32[64,8,128]{2,1,0:T(8,128)S(1)} %copy-done.1, bf16[64,32,128]{2,1,0:T(8,128)(2,1)S(1)} %bitcast.32, ...), custom_call_target="tpu_custom_call" | custom-call | flops 400000000 | bytes 4000000 | tf_op jit(solution)/shard_map/pallas_call | solution.py:176
  91.6 1.6 %all-to-all-done.2.second_ref = f32[8,24,128]{2,1,0:T(8,128)S(1)} async-done(((f32[8,24,128]{2,1,0:T(8,128)}), f32[8,24,128]{2,1,0:T(8,128)S(1)}, u32[]{:S(2)}, u32[]{:S(2)}) %all-to-all-start.2) | async-done | bytes 98336 | tf_op jit(solution)/shard_map/all_to_all | solution.py:256
  93.2 14.3 %all_to_all.25.first_ref = f32[8,24,128]{2,1,0:T(8,128)} all-to-all(f32[8,24,128]{2,1,0:T(8,128)S(1)} %shard_map.113), channel_id=1, replica_groups=mesh['y'=8,'zl'=4,'x'=4,'zh'=2,'c'=2] {'y'}, dimensions={0} | all-to-all | bytes 196608 | tf_op jit(solution)/shard_map/all_to_all | solution.py:253
  107.5 1.6 %shard_map.116 = f32[16,12,128]{2,1,0:T(8,128)} custom-call(f32[8,24,128]{2,1,0:T(8,128)} %all_to_all.25.first_ref, f32[8,24,128]{2,1,0:T(8,128)} %copy-done.8), custom_call_target="tpu_custom_call" | custom-call | flops 100000 | bytes 400000 | tf_op jit(solution)/shard_map/pallas_call | solution.py:195
  109.1 15.3 %all_to_all.26.in_ref = f32[16,12,128]{2,1,0:T(8,128)} all-to-all(f32[16,12,128]{2,1,0:T(8,128)} %shard_map.116), channel_id=1, replica_groups=mesh['y'=8,'zl'=4,'x'=4,'zh'=2,'c'=2] {'x','zl'}, dimensions={0} | all-to-all | bytes 196608 | tf_op jit(solution)/shard_map/all_to_all | solution.py:258
  124.4 1.6 %shard_map.117 = f32[8,48,128]{2,1,0:T(8,128)} custom-call(f32[16,12,128]{2,1,0:T(8,128)} %all_to_all.26.in_ref), custom_call_target="tpu_custom_call" | custom-call | flops 100000 | bytes 400000 | tf_op jit(solution)/shard_map/pallas_call | solution.py:195
  126.0 3.4 %all-to-all-start.4 = ((f32[8,48,128]{2,1,0:T(8,128)}), f32[8,48,128]{2,1,0:T(8,128)S(1)}, u32[]{:S(2)}, u32[]{:S(2)}) async-start(f32[8,48,128]{2,1,0:T(8,128)} %shard_map.117), calls=%async_computation.4 | async-start | bytes 393216 | tf_op jit(solution)/shard_map/all_to_all | solution.py:260
  129.4 1.0 copy.14
  130.4 1.0 copy.15
  131.4 7.7 %all-to-all-done.4.in_ref = f32[8,48,128]{2,1,0:T(8,128)S(1)} async-done(((f32[8,48,128]{2,1,0:T(8,128)}), f32[8,48,128]{2,1,0:T(8,128)S(1)}, u32[]{:S(2)}, u32[]{:S(2)}) %all-to-all-start.4) | async-done | bytes 196640 | tf_op jit(solution)/shard_map/all_to_all | solution.py:260
  139.7 1.6 %shard_map.118 = (f32[32,512]{1,0:T(8,128)}, f32[32,512]{1,0:T(8,128)}, f32[32,512]{1,0:T(8,128)}) custom-call(f32[8,48,128]{2,1,0:T(8,128)} %copy-done.6), custom_call_target="tpu_custom_call" | custom-call | flops 100000 | bytes 400000 | tf_op jit(solution)/shard_map/pallas_call | solution.py:195
  (40 shorter events, 3.8 us)
Async XLA Ops:
  0.6 14.3 %copy-start.7 = (bf16[32,64,128]{2,1,0:T(8,128)(2,1)S(1)}, bf16[32,64,128]{2,1,0:T(8,128)(2,1)}, u32[]{:S(2)}) copy-start(bf16[32,64,128]{2,1,0:T(8,128)(2,1)} %param.8) | copy-start | bytes 1572868
  2.1 23.0 %collective-permute-start.4 = (bf16[64,32,128]{2,1,0:T(8,128)(2,1)S(1)}, bf16[64,32,128]{2,1,0:T(8,128)(2,1)S(1)}, u32[]{:S(2)}, u32[]{:S(2)}) collective-permute-start(bf16[64,32,128]{2,1,0:T(8,128)(2,1)S(1)} %bitcast.27), channel_id=1, source_target_pairs={{0,2},{2,0},{1,3},{3,1},{4,6},{6,4},{5,7},{7,5},{8,10},{10,8},{9,1... | collective-permute-start | bytes 1572872 | tf_op jit(solution)/shard_map/ppermute | solution.py:18
  13.0 56.2 %collective-permute-start.3 = (bf16[64,32,128]{2,1,0:T(8,128)(2,1)S(1)}, bf16[64,32,128]{2,1,0:T(8,128)(2,1)S(1)}, u32[]{:S(2)}, u32[]{:S(2)}) collective-permute-start(bf16[64,32,128]{2,1,0:T(8,128)(2,1)S(1)} %bitcast.28), channel_id=1, source_target_pairs={{0,1},{1,0},{2,3},{3,2},{4,5},{5,4},{6,7},{7,6},{8,9},{9,8},{10,11... | collective-permute-start | bytes 1572872 | tf_op jit(solution)/shard_map/ppermute | solution.py:18
  15.3 13.0 %copy-start.2 = (bf16[32,64,128]{2,0,1:T(8,128)(2,1)}, bf16[32,64,128]{2,0,1:T(8,128)(2,1)S(1)}, u32[]{:S(2)}) copy-start(bf16[32,64,128]{2,0,1:T(8,128)(2,1)S(1)} %copy.19) | copy-start | bytes 1572868
  15.3 11.7 %copy-start.11 = (bf16[12]{0:T(256)(128)(2,1)S(1)}, bf16[12]{0:T(256)(128)(2,1)}, u32[]{:S(2)}) copy-start(bf16[12]{0:T(256)(128)(2,1)} %param.12) | copy-start | bytes 76
  15.3 11.7 %copy-start.12 = (bf16[12]{0:T(256)(128)(2,1)S(1)}, bf16[12]{0:T(256)(128)(2,1)}, u32[]{:S(2)}) copy-start(bf16[12]{0:T(256)(128)(2,1)} %param.11) | copy-start | bytes 76
  15.3 53.9 %collective-permute-start.7 = (bf16[64,32,128]{2,1,0:T(8,128)(2,1)S(1)}, bf16[64,32,128]{2,1,0:T(8,128)(2,1)}, u32[]{:S(2)}, u32[]{:S(2)}) collective-permute-start(bf16[64,32,128]{2,1,0:T(8,128)(2,1)S(1)} %bitcast.33), channel_id=1, source_target_pairs={{0,4},{4,8},{8,12},{12,0},{1,5},{5,9},{9,13},{13,1},{2,6},{6,10},{... | collective-permute-start | bytes 1572872 | tf_op jit(solution)/shard_map/ppermute | solution.py:18
  17.9 56.0 %collective-permute-start.6 = (bf16[64,32,128]{2,1,0:T(8,128)(2,1)S(1)}, bf16[64,32,128]{2,1,0:T(8,128)(2,1)S(1)}, u32[]{:S(2)}, u32[]{:S(2)}) collective-permute-start(bf16[64,32,128]{2,1,0:T(8,128)(2,1)S(1)} %bitcast.34), channel_id=1, source_target_pairs={{0,8},{4,12},{8,0},{12,4},{1,9},{5,13},{9,1},{13,5},{2,10},{6,14},... | collective-permute-start | bytes 1572872 | tf_op jit(solution)/shard_map/ppermute | solution.py:18
  25.1 44.2 %collective-permute-start.5 = (bf16[64,32,128]{2,1,0:T(8,128)(2,1)S(1)}, bf16[64,32,128]{2,1,0:T(8,128)(2,1)S(1)}, u32[]{:S(2)}, u32[]{:S(2)}) collective-permute-start(bf16[64,32,128]{2,1,0:T(8,128)(2,1)S(1)} %collective-permute-done.4.refs_5_), channel_id=1, source_target_pairs={{0,1},{1,0},{2,3},{3,2},{4,5},{5,4},{6,7},{7,6},{8,9},{9,8},{10,11... | collective-permute-start | bytes 1572872 | tf_op jit(solution)/shard_map/ppermute | solution.py:18
  27.0 0.7 copy-start.13
  27.0 0.7 copy-start.14
  30.4 16.3 %collective-permute-start.1 = (bf16[40,128]{1,0:T(8,128)(2,1)}, bf16[40,128]{1,0:T(8,128)(2,1)S(1)}, u32[]{:S(2)}, u32[]{:S(2)}) collective-permute-start(bf16[40,128]{1,0:T(8,128)(2,1)} %get-tuple-element.13), channel_id=1, source_target_pairs={{0,16},{16,32},{32,48},{48,64},{64,80},{80,96},{96,112},{112,128},... | collective-permute-start | bytes 30728 | tf_op jit(solution)/shard_map/ppermute | solution.py:243
  46.7 8.8 %copy-start.9 = (bf16[40,128]{1,0:T(8,128)(2,1)}, bf16[40,128]{1,0:T(8,128)(2,1)S(1)}, u32[]{:S(2)}) copy-start(bf16[40,128]{1,0:T(8,128)(2,1)S(1)} %collective-permute-done.1.left_ref) | copy-start | bytes 30724
  46.7 6.0 %collective-permute-start.2 = (bf16[40,128]{1,0:T(8,128)(2,1)}, bf16[40,128]{1,0:T(8,128)(2,1)S(1)}, u32[]{:S(2)}, u32[]{:S(2)}) collective-permute-start(bf16[40,128]{1,0:T(8,128)(2,1)} %get-tuple-element.14), channel_id=1, source_target_pairs={{16,0},{32,16},{48,32},{64,48},{80,64},{96,80},{112,96},{128,112},... | collective-permute-start | bytes 30728 | tf_op jit(solution)/shard_map/ppermute | solution.py:244
  52.8 2.8 %copy-start.10 = (bf16[40,128]{1,0:T(8,128)(2,1)}, bf16[40,128]{1,0:T(8,128)(2,1)S(1)}, u32[]{:S(2)}) copy-start(bf16[40,128]{1,0:T(8,128)(2,1)S(1)} %collective-permute-done.2.right_ref) | copy-start | bytes 30724
  52.8 35.2 %collective-permute-start = (bf16[64,32,128]{2,1,0:T(8,128)(2,1)}, bf16[64,32,128]{2,1,0:T(8,128)(2,1)}, u32[]{:S(2)}, u32[]{:S(2)}) collective-permute-start(bf16[64,32,128]{2,1,0:T(8,128)(2,1)} %bitcast.36), channel_id=1, source_target_pairs={{0,12},{4,0},{8,4},{12,8},{1,13},{5,1},{9,5},{13,9},{2,14},{6,2},{... | collective-permute-start | bytes 1572872 | tf_op jit(solution)/shard_map/ppermute | solution.py:18
  56.2 13.1 %all-to-all-start = ((bf16[4,2,40,128]{3,2,1,0:T(8,128)(2,1)}), bf16[4,2,40,128]{3,2,1,0:T(8,128)(2,1)S(1)}, u32[]{:S(2)}, u32[]{:S(2)}) async-start(bf16[4,2,40,128]{3,2,1,0:T(8,128)(2,1)} %broadcast_in_dim.2), calls=%async_computation | async-start | bytes 163840 | tf_op jit(solution)/shard_map/all_to_all | solution.py:246
  69.3 1.0 copy-start
  73.9 10.5 %copy-start.1 = (f32[64,8,128]{2,1,0:T(8,128)S(1)}, f32[64,8,128]{2,1,0:T(8,128)}, u32[]{:S(2)}) copy-start(f32[64,8,128]{2,1,0:T(8,128)} %shard_map.111.refs_2_) | copy-start | bytes 786436
  73.9 10.5 %copy-start.3 = (bf16[32,64,128]{2,0,1:T(8,128)(2,1)S(1)}, bf16[32,64,128]{2,0,1:T(8,128)(2,1)}, u32[]{:S(2)}) copy-start(bf16[32,64,128]{2,0,1:T(8,128)(2,1)} %copy-done.2) | copy-start | bytes 1572868
  77.2 16.0 %all-to-all-start.2 = ((f32[8,24,128]{2,1,0:T(8,128)}), f32[8,24,128]{2,1,0:T(8,128)S(1)}, u32[]{:S(2)}, u32[]{:S(2)}) async-start(f32[8,24,128]{2,1,0:T(8,128)} %shard_map.115), calls=%async_computation.2 | async-start | bytes 196608 | tf_op jit(solution)/shard_map/all_to_all | solution.py:256
  87.1 0.8 copy-start.4
  93.2 14.3 %copy-start.8 = (f32[8,24,128]{2,1,0:T(8,128)}, f32[8,24,128]{2,1,0:T(8,128)S(1)}, u32[]{:S(2)}) copy-start(f32[8,24,128]{2,1,0:T(8,128)S(1)} %all-to-all-done.2.second_ref) | copy-start | bytes 294916
  109.1 20.3 %copy-start.5 = (bf16[64,32,128]{2,1,0:T(8,128)(2,1)S(1)}, bf16[64,32,128]{2,1,0:T(8,128)(2,1)}, u32[]{:S(2)}) copy-start(bf16[64,32,128]{2,1,0:T(8,128)(2,1)} %copy-done.4) | copy-start | bytes 1572868
  126.0 13.1 %all-to-all-start.4 = ((f32[8,48,128]{2,1,0:T(8,128)}), f32[8,48,128]{2,1,0:T(8,128)S(1)}, u32[]{:S(2)}, u32[]{:S(2)}) async-start(f32[8,48,128]{2,1,0:T(8,128)} %shard_map.117), calls=%async_computation.4 | async-start | bytes 393216 | tf_op jit(solution)/shard_map/all_to_all | solution.py:260
  139.1 0.7 copy-start.6

commit v3 on v2

--- a/solution.py
+++ b/solution.py
@@ -95,9 +95,9 @@
 ROWS = 8
 
 
-def panel_kernel(with_images, appends, u_ref, halo_ref, f_ref, *rest):
-    olds, rest = rest[:4], rest[4:]
-    before_ref, rest = (rest[0], rest[1:]) if appends else (None, rest)
+def panel_kernel(d, u_ref, halo_ref, f_ref, *rest):
+    with_images = d == 0
+    olds, rest = rest[:4], rest[4 if d == 0 else 5 :]
     if with_images:
         out_ref, mass_ref, stiff_ref, us, s1, s2, q, img, acc = rest
     else:
@@ -161,23 +161,25 @@
     lane = lax.broadcasted_iota(jnp.int32, (1, 4 * M), 1)
     swapped = jnp.where(lane % 64 < 32, pltpu.roll(v, 96, 1), pltpu.roll(v, 32, 1))
     v = jnp.where(c == 1, swapped, v)
-    for i in range(8):
-        if appends:
-            out_ref[i, 0:PIECE] = before_ref[i]
-            out_ref[i, PIECE : 2 * PIECE] = v[PIECE * i : PIECE * i + PIECE]
-        else:
-            out_ref[i] = v[PIECE * i : PIECE * i + PIECE]
-
-
-def panel(u, halo, f, olds, before, with_images):
-    outs = [jax.ShapeDtypeStruct((8, PIECE if before is None else 2 * PIECE, 4 * M), F32)]
-    outs += [jax.ShapeDtypeStruct((R, M, C), BF16)] * (2 if with_images else 0)
-    operands = [u, halo, f, *olds] + ([] if before is None else [before])
+    chip = lax.rem(lax.axis_index("x") + d, 4)
+    for k in range(4):
+
+        @pl.when(chip == k)
+        def _():
+            for i in range(8):
+                out_ref[i, PIECE * k : PIECE * k + PIECE] = v[PIECE * i : PIECE * i + PIECE]
+
+
+def panel(d, u, halo, f, olds, parts):
+    outs = [jax.ShapeDtypeStruct((8, 4 * PIECE, 4 * M), F32)]
+    outs += [jax.ShapeDtypeStruct((R, M, C), BF16)] * (2 if d == 0 else 0)
+    operands = [u, halo, f, *olds] + ([] if d == 0 else [parts])
     return pl.pallas_call(
-        lambda *refs: panel_kernel(with_images, before is not None, *refs),
+        lambda *refs: panel_kernel(d, *refs),
         out_shape=outs,
-        in_specs=[VM] * len(operands),
+        in_specs=[VM] * 7 + ([] if d == 0 else [pl.BlockSpec(memory_space=pl.ANY)]),
         out_specs=[VM] * len(outs),
+        input_output_aliases={} if d == 0 else {7: 0},
         scratch_shapes=[
             pltpu.VMEM((R + 4, M, C), F32),
             pltpu.VMEM((R + 2, M, C), F32),
@@ -189,47 +191,6 @@
         compiler_params=pltpu.CompilerParams(vmem_limit_bytes=16 * 2**20),
         cost_estimate=pl.CostEstimate(flops=4 * 10**8, bytes_accessed=4 * 10**6, transcendentals=0),
     )(*operands)
-
-
-def small(kernel, out_shape, *operands):
-    return pl.pallas_call(
-        kernel,
-        out_shape=out_shape,
-        in_specs=[VM] * len(operands),
-        out_specs=jax.tree.map(lambda _: VM, out_shape),
-        cost_estimate=pl.CostEstimate(flops=10**5, bytes_accessed=4 * 10**5, transcendentals=0),
-    )(*operands)
-
-
-def added(ref, axis_size, *at):
-    total = ref[(0, *at)]
-    for i in range(1, axis_size):
-        total = total + ref[(i, *at)]
-    return total
-
-
-def to_chips_kernel(first_ref, second_ref, out_ref):
-    x = lax.axis_index("x")
-    first, second = added(first_ref, 8), added(second_ref, 8)
-    for d, v in ((0, first[:PIECE]), (1, first[PIECE:]), (3, second[:PIECE]), (2, second[PIECE:])):
-        place = lax.rem(x + d, 4) * 4
-        for z in range(4):
-            out_ref[place + z] = v
-
-
-def to_y_kernel(in_ref, out_ref):
-    for x in range(4):
-        v = in_ref[4 * x] + in_ref[4 * x + 1] + in_ref[4 * x + 2] + in_ref[4 * x + 3]
-        for y in range(8):
-            out_ref[y, PIECE * x : PIECE * x + PIECE] = v
-
-
-def crosses_kernel(in_ref, mass_ref, membrane_ref, bending_ref):
-    area = 1.0 / (R * C * 32)
-    for x in range(4):
-        v = jnp.concatenate([in_ref[y, PIECE * x : PIECE * x + PIECE] for y in range(8)], axis=0) * area
-        for i, ref in enumerate((mass_ref, membrane_ref, bending_ref)):
-            ref[:, 4 * M * x : 4 * M * x + 4 * M] = v[M * i : M * i + M]
 
 
 def local(old_modes, new_modes, material, density, memb_x, memb_y, bend_table):
@@ -246,20 +207,23 @@
     halos = lax.all_to_all(jnp.broadcast_to(halo[None], (4, *halo.shape)), "x", 0, 0)
     x = lax.axis_index("x")
     beside = [halo] + [lax.dynamic_index_in_dim(halos, lax.rem(x + d, 4), 0, keepdims=False) for d in (1, 2, 3)]
+    other, left, right, beside[1:], panels[1], panels[3] = lax.optimization_barrier(
+        (other, left, right, beside[1:], panels[1], panels[3])
+    )
+    f = fields(material, left, right, tables)
+    f, panels[2] = lax.optimization_barrier((f, panels[2]))
     olds = (old, shifted(old, "c", 1), other, shifted(other, "c", 1))
-    f = fields(material, left, right, tables)
-    part, mass, stiff = panel(new, halo, f, olds, None, True)
-    (part,) = panel(panels[1], beside[1], f, olds, part, False)
-    early = lax.all_to_all(part, "y", 0, 0)
-    (part,) = panel(panels[3], beside[3], f, olds, None, False)
-    (part,) = panel(panels[2], beside[2], f, olds, part, False)
-    late = lax.all_to_all(part, "y", 0, 0)
-    part = small(to_chips_kernel, jax.ShapeDtypeStruct((16, PIECE, 4 * M), F32), early, late)
-    part = lax.all_to_all(part, ("x", "zl"), 0, 0)
-    part = small(to_y_kernel, jax.ShapeDtypeStruct((8, 4 * PIECE, 4 * M), F32), part)
-    part = lax.all_to_all(part, "y", 0, 0)
-    crosses = small(crosses_kernel, [jax.ShapeDtypeStruct((M, 16 * M), F32)] * 3, part)
-    return (*[v.T for v in crosses], mass.transpose(1, 0, 2), stiff.transpose(1, 0, 2))
+    parts, mass, stiff = panel(0, new, halo, f, olds, None)
+    for d in (1, 3, 2):
+        (parts,) = panel(d, panels[d], beside[d], f, olds, parts)
+    parts = jnp.sum(lax.all_to_all(parts, "y", 0, 0), axis=0).reshape(4, 1, PIECE, 4 * M)
+    parts = jnp.broadcast_to(parts, (4, 4, PIECE, 4 * M)).reshape(16, PIECE, 4 * M)
+    parts = lax.all_to_all(parts, ("x", "zl"), 0, 0).reshape(4, 4, PIECE, 4 * M)
+    parts = jnp.sum(parts, axis=1).reshape(1, 4 * PIECE, 4 * M)
+    parts = lax.all_to_all(jnp.broadcast_to(parts, (8, 4 * PIECE, 4 * M)), "y", 0, 0)
+    area = 1.0 / (R * C * n)
+    total = parts.reshape(8, 4, PIECE, 4 * M).transpose(0, 2, 1, 3).reshape(3, M, 16 * M) * area
+    return (*[total[i].T for i in range(3)], mass.transpose(1, 0, 2), stiff.transpose(1, 0, 2))
 
 
 def solution(mesh):

time: 143 us -> 127 us (0.89)
  starting transfers between devices: 56.7 us -> 37.4 us
  Pallas kernels: 22.1 us -> 16.8 us
  waiting for transfers between devices: 24 us -> 28.8 us
  blocking collectives: 29.6 us -> 31.9 us
  local copies, waits for them, and re-layouts: 7.54 us -> 9.1 us
    ppermute x1, waiting for transfers between devices: 1.58 us -> 14.3 us  [local(): left = lax.ppermute(last, SPACE, [(i, i + 1) for i in range(n - 1)])]
    ppermute x1, starting transfers between devices: 14.7 us -> 3.37 us  [local(): left = lax.ppermute(last, SPACE, [(i, i + 1) for i in range(n - 1)])]
    all_to_all x2 -> x1, starting transfers between devices: 10.6 us -> 3.39 us  [local(): lax.all_to_all(jnp.broadcast_to(parts, (8, 4 * PIECE, 4 * M)), 'y', 0, 0)]
    all_to_all x1, waiting for transfers between devices: 5.5 us -> 0.01 us  [local(): lax.all_to_all(jnp.broadcast_to(halo[None], (4, *halo.shape)), 'x', 0, 0)]
    pallas_call x7 -> x4, Pallas kernels: 18.1 us -> 12.8 us  [panel(): pl.pallas_call(lambda *refs: panel_kernel(d, *refs), out_shape=outs, in_s...]
    ppermute x1, waiting for transfers between devices: 4.75 us -> 1.32 us  [local(): right = lax.ppermute(first, SPACE, [(i + 1, i) for i in range(n - 1)])]
    ppermute x6, waiting for transfers between devices: 2.9 us -> 5.6 us  [shifted(): return lax.ppermute(value, axis, [(i, (i + step) % n) for i in range(n)])]
    all_to_all x2, blocking collectives: 29.6 us -> 31.9 us  [the longest x1 16.9 us: local(): lax.all_to_all(parts, 'y', 0, 0)]
  transfers between devices with their start and end apart: 11 -> 10, of which waited for: 6 -> 4; matrix products, arithmetic and copies ran while one was open for 3% -> 3% of each run, Pallas kernels for 12% -> 3%
where the time goes in v3:
time: 127 us; the launch traced here: 126 us
  starting transfers between devices  37.4 us (29%)
  blocking collectives  31.9 us (25%)
  waiting for transfers between devices  28.8 us (23%)
  Pallas kernels  16.8 us (13%)
  local copies, waits for them, and re-layouts  9.1 us (7%)
    ppermute x6, starting transfers between devices, shifted(): return lax.ppermute(value, axis, [(i, (i + step) % n) for i in range(n)])  24.4 us
    all_to_all x1, blocking collectives, local(): lax.all_to_all(parts, 'y', 0, 0)  16.9 us
    all_to_all x1, blocking collectives, local(): parts = lax.all_to_all(parts, ('x', 'zl'), 0, 0).reshape(4, 4, PIECE, 4 * M)  15 us
    ppermute x1, waiting for transfers between devices, local(): left = lax.ppermute(last, SPACE, [(i, i + 1) for i in range(n - 1)])  14.3 us
    pallas_call x4, Pallas kernels, panel(): pl.pallas_call(lambda *refs: panel_kernel(d, *refs), out_shape=outs, in_s...  12.8 us
    all_to_all x1, waiting for transfers between devices, local(): lax.all_to_all(jnp.broadcast_to(parts, (8, 4 * PIECE, 4 * M)), 'y', 0, 0)  7.63 us
    unnamed x28, local copies, waits for them, and re-layouts  6.84 us
    ppermute x6, waiting for transfers between devices, shifted(): return lax.ppermute(value, axis, [(i, (i + step) % n) for i in range(n)])  5.6 us
  transfers between devices with their start and end apart: 10, of which 4 were waited for; matrix products, arithmetic and copies ran while one was open for 3% of the time, Pallas kernels for 3%

profile of v3, /device:TPU:6, one launch (start us, length us, event | category | flops | bytes accessed | tf_op | source)
XLA Modules:
  0.0 125.7 jit_solution(18316971762366023308)
XLA Ops:
  0.6 2.2 %copy.62 = bf16[32,64,128]{2,0,1:T(8,128)(2,1)} copy(bf16[32,64,128]{2,1,0:T(8,128)(2,1)} %param.8) | data formatting | bytes 1048576 | tf_op args[1]
  2.9 7.7 %collective-permute-start.4 = (bf16[64,32,128]{2,1,0:T(8,128)(2,1)}, bf16[64,32,128]{2,1,0:T(8,128)(2,1)S(1)}, u32[]{:S(2)}, u32[]{:S(2)}) collective-permute-start(bf16[64,32,128]{2,1,0:T(8,128)(2,1)} %bitcast.40.u_ref.refs_0_), channel_id=1, source_target_pairs={{0,4},{4,8},{8,12},{12,0},{1,5},{5,9},{9,13},{13,1},{2,6},{6,10},{... | collective-permute-start | bytes 1572872 | tf_op jit(solution)/shard_map/ppermute | solution.py:18
  10.6 1.9 %collective-permute-start.3 = (bf16[64,32,128]{2,1,0:T(8,128)(2,1)}, bf16[64,32,128]{2,1,0:T(8,128)(2,1)S(1)}, u32[]{:S(2)}, u32[]{:S(2)}) collective-permute-start(bf16[64,32,128]{2,1,0:T(8,128)(2,1)} %bitcast.40.u_ref.refs_0_), channel_id=1, source_target_pairs={{0,12},{4,0},{8,4},{12,8},{1,13},{5,1},{9,5},{13,9},{2,14},{6,2},{... | collective-permute-start | bytes 1572872 | tf_op jit(solution)/shard_map/ppermute | solution.py:18
  12.9 7.1 %collective-permute-start = (bf16[64,32,128]{2,1,0:T(8,128)(2,1)S(1)}, bf16[64,32,128]{2,1,0:T(8,128)(2,1)S(1)}, u32[]{:S(2)}, u32[]{:S(2)}) collective-permute-start(bf16[64,32,128]{2,1,0:T(8,128)(2,1)S(1)} %bitcast.42), channel_id=1, source_target_pairs={{0,2},{2,0},{1,3},{3,1},{4,6},{6,4},{5,7},{7,5},{8,10},{10,8},{9,1... | collective-permute-start | bytes 1572872 | tf_op jit(solution)/shard_map/ppermute | solution.py:18
  20.1 0.6 copy-done.10
  20.7 0.6 pad_maximum_fusion.1.tables_ref
  21.3 2.1 %shard_map.110 = (bf16[40,128]{1,0:T(8,128)(2,1)}, bf16[40,128]{1,0:T(8,128)(2,1)}) custom-call(bf16[64,32,128]{2,1,0:T(8,128)(2,1)} %bitcast.40.u_ref.refs_0_, s32[64,128]{1,0:T(8,128)} %mat_ref.3, f32[4,12]{1,0:T(4,128)} %pad_maximum_fusion.1.tables_ref), custom_call_target="tpu_custom_call" | custom-call | flops 1000000 | bytes 1000000 | tf_op jit(solution)/shard_map/pallas_call | solution.py:45
  23.4 3.4 %collective-permute-start.1 = (bf16[40,128]{1,0:T(8,128)(2,1)}, bf16[40,128]{1,0:T(8,128)(2,1)S(1)}, u32[]{:S(2)}, u32[]{:S(2)}) collective-permute-start(bf16[40,128]{1,0:T(8,128)(2,1)} %get-tuple-element.20), channel_id=1, source_target_pairs={{0,16},{16,32},{32,48},{48,64},{64,80},{80,96},{96,112},{112,128},... | collective-permute-start | bytes 30728 | tf_op jit(solution)/shard_map/ppermute | solution.py:204
  26.8 1.3 %collective-permute-start.2 = (bf16[40,128]{1,0:T(8,128)(2,1)}, bf16[40,128]{1,0:T(8,128)(2,1)S(1)}, u32[]{:S(2)}, u32[]{:S(2)}) collective-permute-start(bf16[40,128]{1,0:T(8,128)(2,1)} %get-tuple-element.21), channel_id=1, source_target_pairs={{16,0},{32,16},{48,32},{64,48},{80,64},{96,80},{112,96},{128,112},... | collective-permute-start | bytes 30728 | tf_op jit(solution)/shard_map/ppermute | solution.py:205
  28.1 14.3 %collective-permute-done.1.left_ref = bf16[40,128]{1,0:T(8,128)(2,1)S(1)} collective-permute-done((bf16[40,128]{1,0:T(8,128)(2,1)}, bf16[40,128]{1,0:T(8,128)(2,1)S(1)}, u32[]{:S(2)}, u32[]{:S(2)}) %collective-permute-start.1) | collective-permute-done | bytes 10272 | tf_op jit(solution)/shard_map/ppermute | solution.py:204
  42.4 1.3 %collective-permute-done.2.right_ref = bf16[40,128]{1,0:T(8,128)(2,1)S(1)} collective-permute-done((bf16[40,128]{1,0:T(8,128)(2,1)}, bf16[40,128]{1,0:T(8,128)(2,1)S(1)}, u32[]{:S(2)}, u32[]{:S(2)}) %collective-permute-start.2) | collective-permute-done | bytes 10272 | tf_op jit(solution)/shard_map/ppermute | solution.py:205
  43.7 0.6 copy-done.7
  44.3 0.6 broadcast_in_dim.20
  44.9 5.0 %all-to-all-start = ((bf16[4,2,40,128]{3,2,1,0:T(8,128)(2,1)}), bf16[4,2,40,128]{3,2,1,0:T(8,128)(2,1)S(1)}, u32[]{:S(2)}, u32[]{:S(2)}) async-start(bf16[4,2,40,128]{3,2,1,0:T(8,128)(2,1)} %broadcast_in_dim.20), calls=%async_computation | async-start | bytes 163840 | tf_op jit(solution)/shard_map/all_to_all | solution.py:207
  49.9 3.4 %collective-permute-start.5 = (bf16[64,32,128]{2,1,0:T(8,128)(2,1)}, bf16[64,32,128]{2,1,0:T(8,128)(2,1)}, u32[]{:S(2)}, u32[]{:S(2)}) collective-permute-start(bf16[64,32,128]{2,1,0:T(8,128)(2,1)} %bitcast.40.u_ref.refs_0_), channel_id=1, source_target_pairs={{0,8},{4,12},{8,0},{12,4},{1,9},{5,13},{9,1},{13,5},{2,10},{6,14},... | collective-permute-start | bytes 1572872 | tf_op jit(solution)/shard_map/ppermute | solution.py:18
  53.2 1.9 %collective-permute-start.6 = (bf16[64,32,128]{2,1,0:T(8,128)(2,1)S(1)}, bf16[64,32,128]{2,1,0:T(8,128)(2,1)S(1)}, u32[]{:S(2)}, u32[]{:S(2)}) collective-permute-start(bf16[64,32,128]{2,1,0:T(8,128)(2,1)S(1)} %bitcast.43), channel_id=1, source_target_pairs={{0,1},{1,0},{2,3},{3,2},{4,5},{5,4},{6,7},{7,6},{8,9},{9,8},{10,11... | collective-permute-start | bytes 1572872 | tf_op jit(solution)/shard_map/ppermute | solution.py:18
  55.3 2.4 %collective-permute-start.7 = (bf16[64,32,128]{2,1,0:T(8,128)(2,1)S(1)}, bf16[64,32,128]{2,1,0:T(8,128)(2,1)S(1)}, u32[]{:S(2)}, u32[]{:S(2)}) collective-permute-start(bf16[64,32,128]{2,1,0:T(8,128)(2,1)S(1)} %collective-permute-done.refs_5_), channel_id=1, source_target_pairs={{0,1},{1,0},{2,3},{3,2},{4,5},{5,4},{6,7},{7,6},{8,9},{9,8},{10,11... | collective-permute-start | bytes 1572872 | tf_op jit(solution)/shard_map/ppermute | solution.py:18
  57.7 1.9 %shard_map.111.refs_2_ = f32[64,8,128]{2,1,0:T(8,128)} custom-call(s32[64,128]{1,0:T(8,128)} %mat_ref.3, bf16[40,128]{1,0:T(8,128)(2,1)} %copy-done.6, bf16[40,128]{1,0:T(8,128)(2,1)} %copy-done.7, f32[4,12]{1,0:T(4,128)} %pad_maximum_fusion.1.tables_ref), custom_call_target="tpu_custom_call" | custom-call | flops 1000000 | bytes 1000000 | tf_op jit(solution)/shard_map/pallas_call | solution.py:84
  59.6 5.6 %collective-permute-done.5.refs_0_ = bf16[64,32,128]{2,1,0:T(8,128)(2,1)} collective-permute-done((bf16[64,32,128]{2,1,0:T(8,128)(2,1)}, bf16[64,32,128]{2,1,0:T(8,128)(2,1)}, u32[]{:S(2)}, u32[]{:S(2)}) %collective-permute-start.5) | collective-permute-done | bytes 524320 | tf_op jit(solution)/shard_map/ppermute | solution.py:18
  65.2 0.9 copy-done
  66.1 3.7 %shard_map.112 = (f32[8,48,128]{2,1,0:T(8,128)S(1)}, bf16[64,32,128]{2,1,0:T(8,128)(2,1)S(1)}, bf16[64,32,128]{2,1,0:T(8,128)(2,1)S(1)}) custom-call(bf16[64,32,128]{2,1,0:T(8,128)(2,1)} %bitcast.40.u_ref.refs_0_, bf16[2,40,128]{2,1,0:T(8,128)(2,1)S(1)} %pad_maximum_fusion.refs_1_, f32[64,8,128]{2,1,0:T(8,128)S(1)} %copy-done, ...), custom_call_target="tpu_custom_call" | custom-call | flops 400000000 | bytes 4000000 | tf_op jit(solution)/shard_map/pallas_call | solution.py:177
  69.9 2.6 %shard_map.113.refs_7_ = f32[8,48,128]{2,1,0:T(8,128)S(1)} custom-call(bf16[64,32,128]{2,1,0:T(8,128)(2,1)S(1)} %collective-permute-done.3.refs_0_, bf16[2,40,128]{2,1,0:T(8,128)(2,1)S(1)} %get-tuple-element.31.refs_1_, f32[64,8,128]{2,1,0:T(8,128)S(1)} %copy-done, bf16[64,32,128]{2,1,0:T(8,128)(2,1)S(1)} %bitcast.45, ...), custom_call_target="tpu_custom_call", output_to_operand_aliasing={{}: (7, {})} | custom-call | flops 400000000 | bytes 4000000 | tf_op jit(solution)/shard_map/pallas_call | solution.py:177
  72.5 2.8 %shard_map.114.refs_7_ = f32[8,48,128]{2,1,0:T(8,128)S(1)} custom-call(bf16[64,32,128]{2,1,0:T(8,128)(2,1)S(1)} %collective-permute-done.4.refs_0_, bf16[2,40,128]{2,1,0:T(8,128)(2,1)S(1)} %get-tuple-element.29.refs_1_, f32[64,8,128]{2,1,0:T(8,128)S(1)} %copy-done, bf16[64,32,128]{2,1,0:T(8,128)(2,1)S(1)} %bitcast.46, ...), custom_call_target="tpu_custom_call", output_to_operand_aliasing={{}: (7, {})} | custom-call | flops 400000000 | bytes 4000000 | tf_op jit(solution)/shard_map/pallas_call | solution.py:177
  75.4 3.7 %shard_map.115 = f32[8,48,128]{2,1,0:T(8,128)S(1)} custom-call(bf16[64,32,128]{2,1,0:T(8,128)(2,1)} %collective-permute-done.5.refs_0_, bf16[2,40,128]{2,1,0:T(8,128)(2,1)S(1)} %get-tuple-element.25.refs_1_, f32[64,8,128]{2,1,0:T(8,128)S(1)} %copy-done, bf16[64,32,128]{2,1,0:T(8,128)(2,1)S(1)} %bitcast.47, ...), custom_call_target="tpu_custom_call", output_to_operand_aliasing={{}: (7, {})} | custom-call | flops 400000000 | bytes 4000000 | tf_op jit(solution)/shard_map/pallas_call | solution.py:177
  79.0 16.9 %all_to_all.20 = f32[8,48,128]{2,1,0:T(8,128)S(1)} all-to-all(f32[8,48,128]{2,1,0:T(8,128)S(1)} %shard_map.115), channel_id=1, replica_groups=mesh['y'=8,'zl'=4,'x'=4,'zh'=2,'c'=2] {'y'}, dimensions={0} | all-to-all | bytes 393216 | tf_op jit(solution)/shard_map/all_to_all | solution.py:219
  96.0 15.0 %all_to_all.21 = f32[16,12,128]{2,1,0:T(8,128)S(1)} all-to-all(f32[16,12,128]{2,1,0:T(8,128)S(1)} %bitcast.51), channel_id=1, replica_groups=mesh['y'=8,'zl'=4,'x'=4,'zh'=2,'c'=2] {'x','zl'}, dimensions={0} | all-to-all | bytes 196608 | tf_op jit(solution)/shard_map/all_to_all | solution.py:221
  111.0 0.7 broadcast_in_dim.24
  111.7 3.4 %all-to-all-start.3 = ((f32[8,48,128]{2,1,0:T(8,128)}), f32[8,48,128]{2,1,0:T(8,128)S(1)}, u32[]{:S(2)}, u32[]{:S(2)}) async-start(f32[8,48,128]{2,1,0:T(8,128)} %broadcast_in_dim.24), calls=%async_computation.3 | async-start | bytes 393216 | tf_op jit(solution)/shard_map/all_to_all | solution.py:223
  115.1 1.0 copy.54
  116.1 1.0 copy.55
  117.1 7.6 %all-to-all-done.3 = f32[8,48,128]{2,1,0:T(8,128)S(1)} async-done(((f32[8,48,128]{2,1,0:T(8,128)}), f32[8,48,128]{2,1,0:T(8,128)S(1)}, u32[]{:S(2)}, u32[]{:S(2)}) %all-to-all-start.3) | async-done | bytes 196640 | tf_op jit(solution)/shard_map/all_to_all | solution.py:223
  125.1 0.7 slice_bitcast_fusion
  (39 shorter events, 0.8 us)
Async XLA Ops:
  0.6 11.9 %copy-start.5 = (bf16[32,64,128]{2,1,0:T(8,128)(2,1)S(1)}, bf16[32,64,128]{2,1,0:T(8,128)(2,1)}, u32[]{:S(2)}) copy-start(bf16[32,64,128]{2,1,0:T(8,128)(2,1)} %param.7) | copy-start | bytes 1572868
  2.9 52.4 %collective-permute-start.4 = (bf16[64,32,128]{2,1,0:T(8,128)(2,1)}, bf16[64,32,128]{2,1,0:T(8,128)(2,1)S(1)}, u32[]{:S(2)}, u32[]{:S(2)}) collective-permute-start(bf16[64,32,128]{2,1,0:T(8,128)(2,1)} %bitcast.40.u_ref.refs_0_), channel_id=1, source_target_pairs={{0,4},{4,8},{8,12},{12,0},{1,5},{5,9},{9,13},{13,1},{2,6},{6,10},{... | collective-permute-start | bytes 1572872 | tf_op jit(solution)/shard_map/ppermute | solution.py:18
  10.6 44.6 %collective-permute-start.3 = (bf16[64,32,128]{2,1,0:T(8,128)(2,1)}, bf16[64,32,128]{2,1,0:T(8,128)(2,1)S(1)}, u32[]{:S(2)}, u32[]{:S(2)}) collective-permute-start(bf16[64,32,128]{2,1,0:T(8,128)(2,1)} %bitcast.40.u_ref.refs_0_), channel_id=1, source_target_pairs={{0,12},{4,0},{8,4},{12,8},{1,13},{5,1},{9,5},{13,9},{2,14},{6,2},{... | collective-permute-start | bytes 1572872 | tf_op jit(solution)/shard_map/ppermute | solution.py:18
  12.9 7.1 %copy-start.8 = (bf16[12]{0:T(256)(128)(2,1)S(1)}, bf16[12]{0:T(256)(128)(2,1)}, u32[]{:S(2)}) copy-start(bf16[12]{0:T(256)(128)(2,1)} %param.12) | copy-start | bytes 76
  12.9 7.1 %copy-start.9 = (bf16[12]{0:T(256)(128)(2,1)S(1)}, bf16[12]{0:T(256)(128)(2,1)}, u32[]{:S(2)}) copy-start(bf16[12]{0:T(256)(128)(2,1)} %param.11) | copy-start | bytes 76
  12.9 42.3 %collective-permute-start = (bf16[64,32,128]{2,1,0:T(8,128)(2,1)S(1)}, bf16[64,32,128]{2,1,0:T(8,128)(2,1)S(1)}, u32[]{:S(2)}, u32[]{:S(2)}) collective-permute-start(bf16[64,32,128]{2,1,0:T(8,128)(2,1)S(1)} %bitcast.42), channel_id=1, source_target_pairs={{0,2},{2,0},{1,3},{3,1},{4,6},{6,4},{5,7},{7,5},{8,10},{10,8},{9,1... | collective-permute-start | bytes 1572872 | tf_op jit(solution)/shard_map/ppermute | solution.py:18
  20.1 0.7 copy-start.10
  20.1 0.7 copy-start.11
  23.4 19.0 %collective-permute-start.1 = (bf16[40,128]{1,0:T(8,128)(2,1)}, bf16[40,128]{1,0:T(8,128)(2,1)S(1)}, u32[]{:S(2)}, u32[]{:S(2)}) collective-permute-start(bf16[40,128]{1,0:T(8,128)(2,1)} %get-tuple-element.20), channel_id=1, source_target_pairs={{0,16},{16,32},{32,48},{48,64},{64,80},{80,96},{96,112},{112,128},... | collective-permute-start | bytes 30728 | tf_op jit(solution)/shard_map/ppermute | solution.py:204
  26.8 16.9 %collective-permute-start.2 = (bf16[40,128]{1,0:T(8,128)(2,1)}, bf16[40,128]{1,0:T(8,128)(2,1)S(1)}, u32[]{:S(2)}, u32[]{:S(2)}) collective-permute-start(bf16[40,128]{1,0:T(8,128)(2,1)} %get-tuple-element.21), channel_id=1, source_target_pairs={{16,0},{32,16},{48,32},{64,48},{80,64},{96,80},{112,96},{128,112},... | collective-permute-start | bytes 30728 | tf_op jit(solution)/shard_map/ppermute | solution.py:205
  42.4 1.3 %copy-start.6 = (bf16[40,128]{1,0:T(8,128)(2,1)}, bf16[40,128]{1,0:T(8,128)(2,1)S(1)}, u32[]{:S(2)}) copy-start(bf16[40,128]{1,0:T(8,128)(2,1)S(1)} %collective-permute-done.1.left_ref) | copy-start | bytes 30724
  43.7 0.6 copy-start.7
  44.9 10.3 %all-to-all-start = ((bf16[4,2,40,128]{3,2,1,0:T(8,128)(2,1)}), bf16[4,2,40,128]{3,2,1,0:T(8,128)(2,1)S(1)}, u32[]{:S(2)}, u32[]{:S(2)}) async-start(bf16[4,2,40,128]{3,2,1,0:T(8,128)(2,1)} %broadcast_in_dim.20), calls=%async_computation | async-start | bytes 163840 | tf_op jit(solution)/shard_map/all_to_all | solution.py:207
  49.9 15.3 %collective-permute-start.5 = (bf16[64,32,128]{2,1,0:T(8,128)(2,1)}, bf16[64,32,128]{2,1,0:T(8,128)(2,1)}, u32[]{:S(2)}, u32[]{:S(2)}) collective-permute-start(bf16[64,32,128]{2,1,0:T(8,128)(2,1)} %bitcast.40.u_ref.refs_0_), channel_id=1, source_target_pairs={{0,8},{4,12},{8,0},{12,4},{1,9},{5,13},{9,1},{13,5},{2,10},{6,14},... | collective-permute-start | bytes 1572872 | tf_op jit(solution)/shard_map/ppermute | solution.py:18
  53.2 11.9 %collective-permute-start.6 = (bf16[64,32,128]{2,1,0:T(8,128)(2,1)S(1)}, bf16[64,32,128]{2,1,0:T(8,128)(2,1)S(1)}, u32[]{:S(2)}, u32[]{:S(2)}) collective-permute-start(bf16[64,32,128]{2,1,0:T(8,128)(2,1)S(1)} %bitcast.43), channel_id=1, source_target_pairs={{0,1},{1,0},{2,3},{3,2},{4,5},{5,4},{6,7},{7,6},{8,9},{9,8},{10,11... | collective-permute-start | bytes 1572872 | tf_op jit(solution)/shard_map/ppermute | solution.py:18
  55.3 9.9 %collective-permute-start.7 = (bf16[64,32,128]{2,1,0:T(8,128)(2,1)S(1)}, bf16[64,32,128]{2,1,0:T(8,128)(2,1)S(1)}, u32[]{:S(2)}, u32[]{:S(2)}) collective-permute-start(bf16[64,32,128]{2,1,0:T(8,128)(2,1)S(1)} %collective-permute-done.refs_5_), channel_id=1, source_target_pairs={{0,1},{1,0},{2,3},{3,2},{4,5},{5,4},{6,7},{7,6},{8,9},{9,8},{10,11... | collective-permute-start | bytes 1572872 | tf_op jit(solution)/shard_map/ppermute | solution.py:18
  65.2 1.0 copy-start
  69.9 2.7 %copy-start.1 = (bf16[64,32,128]{2,1,0:T(8,128)(2,1)}, bf16[64,32,128]{2,1,0:T(8,128)(2,1)S(1)}, u32[]{:S(2)}) copy-start(bf16[64,32,128]{2,1,0:T(8,128)(2,1)S(1)} %get-tuple-element.34) | copy-start | bytes 1572868
  69.9 2.7 %copy-start.3 = (bf16[64,32,128]{2,1,0:T(8,128)(2,1)}, bf16[64,32,128]{2,1,0:T(8,128)(2,1)S(1)}, u32[]{:S(2)}) copy-start(bf16[64,32,128]{2,1,0:T(8,128)(2,1)S(1)} %get-tuple-element.33) | copy-start | bytes 1572868
  96.0 19.1 %copy-start.4 = (bf16[64,32,128]{2,1,0:T(8,128)(2,1)S(1)}, bf16[64,32,128]{2,1,0:T(8,128)(2,1)}, u32[]{:S(2)}) copy-start(bf16[64,32,128]{2,1,0:T(8,128)(2,1)} %copy-done.3) | copy-start | bytes 1572868
  111.7 13.1 %all-to-all-start.3 = ((f32[8,48,128]{2,1,0:T(8,128)}), f32[8,48,128]{2,1,0:T(8,128)S(1)}, u32[]{:S(2)}, u32[]{:S(2)}) async-start(f32[8,48,128]{2,1,0:T(8,128)} %broadcast_in_dim.24), calls=%async_computation.3 | async-start | bytes 393216 | tf_op jit(solution)/shard_map/all_to_all | solution.py:223
  115.1 1.0 copy-start.2

commit v4 on v3

--- a/solution.py
+++ b/solution.py
@@ -25,14 +25,14 @@
     return value
 
 
-def edges_kernel(u_ref, mat_ref, tables_ref, first_ref, last_ref, ky):
-    ky[...] = select_table(mat_ref[...], tables_ref, 2)
+def edges_kernel(u_ref, mat_ref, first_ref, last_ref, mat):
+    mat[...] = mat_ref[...].astype(F32)
     pair = lax.broadcasted_iota(jnp.int32, (8, C), 1) // 2
     firsts, lasts = [], []
     for m in range(0, M + 8, 8):
         first = last = jnp.zeros((8, C), F32)
         for r in range(R):
-            v = u_ref[r, m : m + 8, :].astype(F32) if m < M else jnp.broadcast_to(ky[r : r + 1, :], (8, C))
+            v = u_ref[r, m : m + 8, :].astype(F32) if m < M else jnp.broadcast_to(mat[r : r + 1, :], (8, C))
             first = jnp.where(pair == r, pltpu.roll(v, 2 * r, 1), first)
             last = jnp.where(pair == r, pltpu.roll(v, (2 * r + 2) % C, 1), last)
         firsts.append(first)
@@ -41,15 +41,15 @@
     last_ref[...] = jnp.concatenate(lasts, axis=0).astype(BF16)
 
 
-def edges(u, material, tables):
+def edges(u, material):
     return pl.pallas_call(
         edges_kernel,
         out_shape=[jax.ShapeDtypeStruct((M + 8, C), BF16)] * 2,
-        in_specs=[VM, VM, SM],
+        in_specs=[VM, VM],
         out_specs=[VM] * 2,
         scratch_shapes=[pltpu.VMEM((R, C), F32)],
         cost_estimate=pl.CostEstimate(flops=10**6, bytes_accessed=10**6, transcendentals=0),
-    )(u, material, tables)
+    )(u, material)
 
 
 def fields_kernel(mat_ref, left_ref, right_ref, tables_ref, f_ref, kx, ky, rho, dd):
@@ -60,8 +60,11 @@
     rho[...] = select_table(material, tables_ref, 0)
     dd[...] = select_table(material, tables_ref, 3)
     lane = lax.broadcasted_iota(jnp.int32, (1, C), 1)
-    left = left_ref[M : M + 8, :].astype(F32)
-    right = right_ref[M : M + 8, :].astype(F32)
+    space = lax.axis_index("y") * 4 + lax.axis_index("zl")
+    left = select_table(left_ref[M : M + 8, :].astype(F32), tables_ref, 2)
+    left = jnp.where(space > 0, left, 0.0)
+    right = select_table(right_ref[M : M + 8, :].astype(F32), tables_ref, 2)
+    right = jnp.where(space < 31, right, 0.0)
 
     for r in range(R):
         k = ky[r : r + 1, :]
@@ -92,16 +95,16 @@
 
 
 PIECE = 3 * M // 8
+PANEL_FLOPS = 3 * 10**9
 ROWS = 8
 
 
-def panel_kernel(d, u_ref, halo_ref, f_ref, *rest):
-    with_images = d == 0
-    olds, rest = rest[:4], rest[4 if d == 0 else 5 :]
+def panel_kernel(with_images, u_ref, halo_ref, f_ref, *rest):
+    olds, rest = rest[:2], rest[2:]
     if with_images:
-        out_ref, mass_ref, stiff_ref, us, s1, s2, q, img, acc = rest
+        half_ref, img, mass_ref, stiff_ref, us, s1, s2, q, acc = rest
     else:
-        out_ref, us, s1, s2, q, img, acc = rest
+        half_ref, img, us, s1, s2, q, acc = rest
     zero = jnp.zeros((M, C), F32)
     for r in (0, 1, R + 2, R + 3):
         us[r] = zero
@@ -143,53 +146,80 @@
             for i, v in enumerate((mass, membrane, bending)):
                 hi = v.astype(BF16)
                 lo = (v - hi.astype(F32)).astype(BF16)
-                img[step % 2, M * i : M * i + M, C * j : C * j + C] = hi
-                img[step % 2, M * (i + 3) : M * (i + 3) + M, C * j : C * j + C] = lo
+                img[step, M * i : M * i + M, C * j : C * j + C] = hi
+                img[step, M * (i + 3) : M * (i + 3) + M, C * j : C * j + C] = lo
             if with_images:
                 mass_ref[r] = mass.astype(BF16)
                 stiff_ref[r] = (membrane + bending).astype(BF16)
         wide = [jnp.concatenate([o[base + j] for j in range(ROWS)], axis=1) for o in olds]
         acc[...] += lax.dot_general(
-            img[step % 2], jnp.concatenate(wide, axis=0), (((1,), (1,)), ((), ())), preferred_element_type=F32
+            img[step], jnp.concatenate(wide, axis=0), (((1,), (1,)), ((), ())), preferred_element_type=F32
         )
         return 0
 
     for step in range(R // ROWS):
         rows(step, 0)
-    zh, c = lax.axis_index("zh"), lax.axis_index("c")
-    v = pltpu.roll(acc[0 : 3 * M] + acc[3 * M : 6 * M], zh * 64, 1)
-    lane = lax.broadcasted_iota(jnp.int32, (1, 4 * M), 1)
-    swapped = jnp.where(lane % 64 < 32, pltpu.roll(v, 96, 1), pltpu.roll(v, 32, 1))
-    v = jnp.where(c == 1, swapped, v)
-    chip = lax.rem(lax.axis_index("x") + d, 4)
-    for k in range(4):
-
-        @pl.when(chip == k)
-        def _():
-            for i in range(8):
-                out_ref[i, PIECE * k : PIECE * k + PIECE] = v[PIECE * i : PIECE * i + PIECE]
-
-
-def panel(d, u, halo, f, olds, parts):
-    outs = [jax.ShapeDtypeStruct((8, 4 * PIECE, 4 * M), F32)]
-    outs += [jax.ShapeDtypeStruct((R, M, C), BF16)] * (2 if d == 0 else 0)
-    operands = [u, halo, f, *olds] + ([] if d == 0 else [parts])
-    return pl.pallas_call(
-        lambda *refs: panel_kernel(d, *refs),
+    half_ref[...] = acc[0 : 3 * M] + acc[3 * M : 6 * M]
+
+
+def panel(u, halo, f, olds, with_images):
+    outs = [
+        jax.ShapeDtypeStruct((3 * M, 2 * M), F32),
+        jax.ShapeDtypeStruct((R // ROWS, 6 * M, ROWS * C), BF16),
+    ]
+    outs += [jax.ShapeDtypeStruct((R, M, C), BF16)] * (2 if with_images else 0)
+    return pl.pallas_call(
+        lambda *refs: panel_kernel(with_images, *refs),
         out_shape=outs,
-        in_specs=[VM] * 7 + ([] if d == 0 else [pl.BlockSpec(memory_space=pl.ANY)]),
+        in_specs=[VM] * 5,
         out_specs=[VM] * len(outs),
-        input_output_aliases={} if d == 0 else {7: 0},
         scratch_shapes=[
             pltpu.VMEM((R + 4, M, C), F32),
             pltpu.VMEM((R + 2, M, C), F32),
             pltpu.VMEM((R, M, C), F32),
             pltpu.VMEM((R, M, C), F32),
-            pltpu.VMEM((2, 6 * M, ROWS * C), BF16),
-            pltpu.VMEM((6 * M, 4 * M), F32),
+            pltpu.VMEM((6 * M, 2 * M), F32),
         ],
-        compiler_params=pltpu.CompilerParams(vmem_limit_bytes=16 * 2**20),
-        cost_estimate=pl.CostEstimate(flops=4 * 10**8, bytes_accessed=4 * 10**6, transcendentals=0),
+        compiler_params=pltpu.CompilerParams(vmem_limit_bytes=20 * 2**20),
+        cost_estimate=pl.CostEstimate(flops=PANEL_FLOPS, bytes_accessed=4 * 10**6, transcendentals=0),
+    )(u, halo, f, *olds)
+
+
+def rest_kernel(*refs):
+    halves, terms, olds, out_ref, acc = refs[:4], refs[4:8], refs[8:10], refs[10], refs[11]
+    for step in range(R // ROWS):
+        base = step * ROWS
+        wide = [jnp.concatenate([o[base + j] for j in range(ROWS)], axis=1) for o in olds]
+        wide = jnp.concatenate(wide, axis=0)
+        for d in range(4):
+            part = lax.dot_general(terms[d][step], wide, (((1,), (1,)), ((), ())), preferred_element_type=F32)
+            acc[d] = part if step == 0 else acc[d] + part
+    x, zh, c = lax.axis_index("x"), lax.axis_index("zh"), lax.axis_index("c")
+    lane = lax.broadcasted_iota(jnp.int32, (1, 4 * M), 1)
+    for d in range(4):
+        v = jnp.concatenate([halves[d][...], acc[d, 0 : 3 * M] + acc[d, 3 * M : 6 * M]], axis=1)
+        v = pltpu.roll(v, zh * 64, 1)
+        swapped = jnp.where(lane % 64 < 32, pltpu.roll(v, 96, 1), pltpu.roll(v, 32, 1))
+        v = jnp.where(c == 1, swapped, v)
+        chip = lax.rem(x + d, 4)
+        for k in range(4):
+
+            @pl.when(chip == k)
+            def _():
+                for i in range(8):
+                    out_ref[i, PIECE * k : PIECE * k + PIECE] = v[PIECE * i : PIECE * i + PIECE]
+
+
+def rest(halves, terms, olds):
+    operands = (*halves, *terms, *olds)
+    return pl.pallas_call(
+        rest_kernel,
+        out_shape=jax.ShapeDtypeStruct((8, 4 * PIECE, 4 * M), F32),
+        in_specs=[VM] * len(operands),
+        out_specs=VM,
+        scratch_shapes=[pltpu.VMEM((4, 6 * M, 2 * M), F32)],
+        compiler_params=pltpu.CompilerParams(vmem_limit_bytes=20 * 2**20),
+        cost_estimate=pl.CostEstimate(flops=3 * 10**9, bytes_accessed=14 * 10**6, transcendentals=0),
     )(*operands)
 
 
@@ -198,24 +228,28 @@
     old = old_modes.transpose(1, 0, 2)
     new = new_modes.transpose(1, 0, 2)
     other = shifted(old, "zh", 1)
+    first, last = edges(new, material)
+    first, last, new = lax.optimization_barrier((first, last, new))
     panels = [new] + [shifted(new, "x", -d) for d in (1, 2, 3)]
-    first, last = edges(new, material, tables)
     n = 32
     left = lax.ppermute(last, SPACE, [(i, i + 1) for i in range(n - 1)])
     right = lax.ppermute(first, SPACE, [(i + 1, i) for i in range(n - 1)])
     halo = jnp.stack([left, right])
     halos = lax.all_to_all(jnp.broadcast_to(halo[None], (4, *halo.shape)), "x", 0, 0)
     x = lax.axis_index("x")
-    beside = [halo] + [lax.dynamic_index_in_dim(halos, lax.rem(x + d, 4), 0, keepdims=False) for d in (1, 2, 3)]
-    other, left, right, beside[1:], panels[1], panels[3] = lax.optimization_barrier(
-        (other, left, right, beside[1:], panels[1], panels[3])
-    )
     f = fields(material, left, right, tables)
-    f, panels[2] = lax.optimization_barrier((f, panels[2]))
-    olds = (old, shifted(old, "c", 1), other, shifted(other, "c", 1))
-    parts, mass, stiff = panel(0, new, halo, f, olds, None)
+    olds = (old, shifted(old, "c", 1))
+    halves, terms = [None] * 4, [None] * 4
+    halves[0], terms[0], mass, stiff = panel(new, halo, f, olds, True)
+    halves[0], other = lax.optimization_barrier((halves[0], other))
+    other_core = shifted(other, "c", 1)
+    halves[0], other, panels[1], panels[3] = lax.optimization_barrier((halves[0], other, panels[1], panels[3]))
     for d in (1, 3, 2):
-        (parts,) = panel(d, panels[d], beside[d], f, olds, parts)
+        beside = lax.dynamic_index_in_dim(halos, lax.rem(x + d, 4), 0, keepdims=False)
+        if d == 2:
+            halves[1], panels[2] = lax.optimization_barrier((halves[1], panels[2]))
+        halves[d], terms[d] = panel(panels[d], beside, f, olds, False)
+    parts = rest(halves, terms, (other, other_core))
     parts = jnp.sum(lax.all_to_all(parts, "y", 0, 0), axis=0).reshape(4, 1, PIECE, 4 * M)
     parts = jnp.broadcast_to(parts, (4, 4, PIECE, 4 * M)).reshape(16, PIECE, 4 * M)
     parts = lax.all_to_all(parts, ("x", "zl"), 0, 0).reshape(4, 4, PIECE, 4 * M)

time: 127 us -> 137 us (1.079)
  blocking collectives: 31.9 us -> 37.7 us
  Pallas kernels: 16.8 us -> 21.2 us
  waiting for transfers between devices: 28.8 us -> 26.1 us
    all_to_all x1, waiting for transfers between devices: 0.01 us -> 7.15 us  [local(): lax.all_to_all(jnp.broadcast_to(halo[None], (4, *halo.shape)), 'x', 0, 0)]
    ppermute x6, waiting for transfers between devices: 5.6 us -> 0.02 us  [shifted(): return lax.ppermute(value, axis, [(i, (i + step) % n) for i in range(n)])]
    all_to_all x1, blocking collectives: 15 us -> 19.7 us  [local(): parts = lax.all_to_all(parts, ('x', 'zl'), 0, 0).reshape(4, 4, PIECE, 4 * M)]
    pallas_call x4 -> x5, Pallas kernels: 12.8 us -> 17.3 us  [the longest x4 13.1 us: panel(): pl.pallas_call(lambda *refs: panel_kernel(with_images, *refs), out_shape=...]
    ppermute x1, waiting for transfers between devices: 14.3 us -> 11.2 us  [local(): left = lax.ppermute(last, SPACE, [(i, i + 1) for i in range(n - 1)])]
    unnamed x28 -> x14, local copies, waits for them, and re-layouts: 6.84 us -> 7.56 us
  transfers between devices with their start and end apart: 10 -> 10, of which waited for: 4 -> 3; matrix products, arithmetic and copies ran while one was open for 3% -> 5% of each run, Pallas kernels for 3% -> 13%
where the time goes in v4:
time: 137 us; the launch traced here: 135 us
  blocking collectives  37.7 us (28%)
  starting transfers between devices  37.5 us (27%)
  waiting for transfers between devices  26.1 us (19%)
  Pallas kernels  21.2 us (15%)
  local copies, waits for them, and re-layouts  9.81 us (7%)
  other arithmetic  2.04 us (1%)
    ppermute x6, starting transfers between devices, shifted(): return lax.ppermute(value, axis, [(i, (i + step) % n) for i in range(n)])  24.4 us
    all_to_all x1, blocking collectives, local(): parts = lax.all_to_all(parts, ('x', 'zl'), 0, 0).reshape(4, 4, PIECE, 4 * M)  19.7 us
    all_to_all x1, blocking collectives, local(): lax.all_to_all(parts, 'y', 0, 0)  18 us
    pallas_call x4, Pallas kernels, panel(): pl.pallas_call(lambda *refs: panel_kernel(with_images, *refs), out_shape=...  13.1 us
    ppermute x1, waiting for transfers between devices, local(): left = lax.ppermute(last, SPACE, [(i, i + 1) for i in range(n - 1)])  11.2 us
    all_to_all x1, waiting for transfers between devices, local(): lax.all_to_all(jnp.broadcast_to(parts, (8, 4 * PIECE, 4 * M)), 'y', 0, 0)  7.7 us
    unnamed x14, local copies, waits for them, and re-layouts  7.56 us
    all_to_all x1, waiting for transfers between devices, local(): lax.all_to_all(jnp.broadcast_to(halo[None], (4, *halo.shape)), 'x', 0, 0)  7.15 us
  transfers between devices with their start and end apart: 10, of which 3 were waited for; matrix products, arithmetic and copies ran while one was open for 5% of the time, Pallas kernels for 13%

profile of v4, /device:TPU:6, one launch (start us, length us, event | category | flops | bytes accessed | tf_op | source)
XLA Modules:
  0.0 135.2 jit_solution(11762692840377132304)
XLA Ops:
  0.6 1.4 %copy.59 = bf16[32,64,128]{2,0,1:T(8,128)(2,1)S(1)} copy(bf16[32,64,128]{2,1,0:T(8,128)(2,1)} %param.7) | data formatting | bytes 1048576 | tf_op args[0]
  2.0 1.9 %collective-permute-start.2 = (bf16[64,32,128]{2,1,0:T(8,128)(2,1)S(1)}, bf16[64,32,128]{2,1,0:T(8,128)(2,1)S(1)}, u32[]{:S(2)}, u32[]{:S(2)}) collective-permute-start(bf16[64,32,128]{2,1,0:T(8,128)(2,1)S(1)} %bitcast.47), channel_id=1, source_target_pairs={{0,1},{1,0},{2,3},{3,2},{4,5},{5,4},{6,7},{7,6},{8,9},{9,8},{10,11... | collective-permute-start | bytes 1572872 | tf_op jit(solution)/shard_map/ppermute | solution.py:18
  3.9 10.9 %collective-permute-start.3 = (bf16[64,32,128]{2,1,0:T(8,128)(2,1)S(1)}, bf16[64,32,128]{2,1,0:T(8,128)(2,1)S(1)}, u32[]{:S(2)}, u32[]{:S(2)}) collective-permute-start(bf16[64,32,128]{2,1,0:T(8,128)(2,1)S(1)} %bitcast.48), channel_id=1, source_target_pairs={{0,2},{2,0},{1,3},{3,1},{4,6},{6,4},{5,7},{7,5},{8,10},{10,8},{9,1... | collective-permute-start | bytes 1572872 | tf_op jit(solution)/shard_map/ppermute | solution.py:18
  14.9 2.2 %copy.60 = bf16[32,64,128]{2,0,1:T(8,128)(2,1)} copy(bf16[32,64,128]{2,1,0:T(8,128)(2,1)} %param.8) | data formatting | bytes 1048576 | tf_op args[1]
  17.0 2.1 %shard_map.110 = (bf16[40,128]{1,0:T(8,128)(2,1)}, bf16[40,128]{1,0:T(8,128)(2,1)}) custom-call(bf16[64,32,128]{2,1,0:T(8,128)(2,1)} %bitcast.42, s32[64,128]{1,0:T(8,128)} %mat_ref.3), custom_call_target="tpu_custom_call" | custom-call | flops 1000000 | bytes 1000000 | tf_op jit(solution)/shard_map/pallas_call | solution.py:45
  19.1 3.4 %collective-permute-start = (bf16[40,128]{1,0:T(8,128)(2,1)}, bf16[40,128]{1,0:T(8,128)(2,1)S(1)}, u32[]{:S(2)}, u32[]{:S(2)}) collective-permute-start(bf16[40,128]{1,0:T(8,128)(2,1)} %get-tuple-element.31), channel_id=1, source_target_pairs={{0,16},{16,32},{32,48},{48,64},{64,80},{80,96},{96,112},{112,128},... | collective-permute-start | bytes 30728 | tf_op jit(solution)/shard_map/ppermute | solution.py:235
  22.5 1.3 collective-permute-start.1
  23.8 2.7 %collective-permute-start.4 = (bf16[64,32,128]{2,1,0:T(8,128)(2,1)}, bf16[64,32,128]{2,1,0:T(8,128)(2,1)S(1)}, u32[]{:S(2)}, u32[]{:S(2)}) collective-permute-start(bf16[64,32,128]{2,1,0:T(8,128)(2,1)} %bitcast.43), channel_id=1, source_target_pairs={{0,12},{4,0},{8,4},{12,8},{1,13},{5,1},{9,5},{13,9},{2,14},{6,2},{... | collective-permute-start | bytes 1572872 | tf_op jit(solution)/shard_map/ppermute | solution.py:18
  26.5 0.7 bitcast_convert_fusion
  27.2 11.2 %collective-permute-done.left_ref = bf16[40,128]{1,0:T(8,128)(2,1)S(1)} collective-permute-done((bf16[40,128]{1,0:T(8,128)(2,1)}, bf16[40,128]{1,0:T(8,128)(2,1)S(1)}, u32[]{:S(2)}, u32[]{:S(2)}) %collective-permute-start) | collective-permute-done | bytes 10272 | tf_op jit(solution)/shard_map/ppermute | solution.py:235
  38.4 2.2 %collective-permute-start.5 = (bf16[64,32,128]{2,1,0:T(8,128)(2,1)}, bf16[64,32,128]{2,1,0:T(8,128)(2,1)}, u32[]{:S(2)}, u32[]{:S(2)}) collective-permute-start(bf16[64,32,128]{2,1,0:T(8,128)(2,1)} %bitcast.44), channel_id=1, source_target_pairs={{0,4},{4,8},{8,12},{12,0},{1,5},{5,9},{9,13},{13,1},{2,6},{6,10},{... | collective-permute-start | bytes 1572872 | tf_op jit(solution)/shard_map/ppermute | solution.py:18
  40.6 4.5 %collective-permute-start.6 = (bf16[64,32,128]{2,1,0:T(8,128)(2,1)}, bf16[64,32,128]{2,1,0:T(8,128)(2,1)}, u32[]{:S(2)}, u32[]{:S(2)}) collective-permute-start(bf16[64,32,128]{2,1,0:T(8,128)(2,1)} %bitcast.45), channel_id=1, source_target_pairs={{0,8},{4,12},{8,0},{12,4},{1,9},{5,13},{9,1},{13,5},{2,10},{6,14},... | collective-permute-start | bytes 1572872 | tf_op jit(solution)/shard_map/ppermute | solution.py:18
  45.8 5.1 %all-to-all-start = ((bf16[4,2,40,128]{3,2,1,0:T(8,128)(2,1)}), bf16[4,2,40,128]{3,2,1,0:T(8,128)(2,1)S(1)}, u32[]{:S(2)}, u32[]{:S(2)}) async-start(bf16[4,2,40,128]{3,2,1,0:T(8,128)(2,1)} %broadcast_in_dim.20), calls=%async_computation | async-start | bytes 163840 | tf_op jit(solution)/shard_map/all_to_all | solution.py:238
  50.9 1.3 pad_maximum_fusion.1.tables_ref
  52.2 1.9 %shard_map.111.refs_2_ = f32[64,8,128]{2,1,0:T(8,128)} custom-call(s32[64,128]{1,0:T(8,128)} %mat_ref.3, bf16[40,128]{1,0:T(8,128)(2,1)} %copy-done.3, bf16[40,128]{1,0:T(8,128)(2,1)} %copy-done.4, f32[4,12]{1,0:T(4,128)} %pad_maximum_fusion.1.tables_ref), custom_call_target="tpu_custom_call" | custom-call | flops 1000000 | bytes 1000000 | tf_op jit(solution)/shard_map/pallas_call | solution.py:87
  54.1 7.2 %all-to-all-done = bf16[4,2,40,128]{3,2,1,0:T(8,128)(2,1)S(1)} async-done(((bf16[4,2,40,128]{3,2,1,0:T(8,128)(2,1)}), bf16[4,2,40,128]{3,2,1,0:T(8,128)(2,1)S(1)}, u32[]{:S(2)}, u32[]{:S(2)}) %all-to-all-start) | async-done | bytes 81952 | tf_op jit(solution)/shard_map/all_to_all | solution.py:238
  61.2 1.0 copy-done
  62.3 0.9 copy-done.1
  63.2 2.9 %shard_map.112 = (f32[96,64]{1,0:T(8,128)S(1)}, bf16[8,192,1024]{2,1,0:T(8,128)(2,1)S(1)}, bf16[64,32,128]{2,1,0:T(8,128)(2,1)S(1)}, bf16[64,32,128]{2,1,0:T(8,128)(2,1)S(1)}) custom-call(bf16[64,32,128]{2,1,0:T(8,128)(2,1)S(1)} %bitcast.46, bf16[2,40,128]{2,1,0:T(8,128)(2,1)S(1)} %pad_maximum_fusion.refs_1_, f32[64,8,128]{2,1,0:T(8,128)S(1)} %copy-done.1, ...), custom_call_target="tpu_custom_call" | custom-call | flops 3000000000 | bytes 4000000 | tf_op jit(solution)/shard_map/pallas_call | solution.py:171
  66.1 2.1 %collective-permute-start.7 = (bf16[64,32,128]{2,1,0:T(8,128)(2,1)S(1)}, bf16[64,32,128]{2,1,0:T(8,128)(2,1)S(1)}, u32[]{:S(2)}, u32[]{:S(2)}) collective-permute-start(bf16[64,32,128]{2,1,0:T(8,128)(2,1)S(1)} %collective-permute-done.3.refs_8_), channel_id=1, source_target_pairs={{0,1},{1,0},{2,3},{3,2},{4,5},{5,4},{6,7},{7,6},{8,9},{9,8},{10,11... | collective-permute-start | bytes 1572872 | tf_op jit(solution)/shard_map/ppermute | solution.py:18
  68.3 2.9 %shard_map.113 = (f32[96,64]{1,0:T(8,128)S(1)}, bf16[8,192,1024]{2,1,0:T(8,128)(2,1)S(1)}) custom-call(bf16[64,32,128]{2,1,0:T(8,128)(2,1)S(1)} %collective-permute-done.4.refs_0_, bf16[2,40,128]{2,1,0:T(8,128)(2,1)S(1)} %get-tuple-element.91.refs_1_, f32[64,8,128]{2,1,0:T(8,128)S(1)} %copy-done.2, bf16[64,32,128]{2,1,0:T(8,128)(2,1)S(1)} %bitcast.50, ...), custom_call_target="tpu_custom_call" | custom-call | flops 3000000000 | bytes 4000000 | tf_op jit(solution)/shard_map/pallas_call | solution.py:171
  71.1 3.7 %shard_map.114 = (f32[96,64]{1,0:T(8,128)S(1)}, bf16[8,192,1024]{2,1,0:T(8,128)(2,1)S(1)}) custom-call(bf16[64,32,128]{2,1,0:T(8,128)(2,1)} %collective-permute-done.6.refs_0_, bf16[2,40,128]{2,1,0:T(8,128)(2,1)S(1)} %get-tuple-element.90.refs_1_, f32[64,8,128]{2,1,0:T(8,128)S(1)} %copy-done.2, bf16[64,32,128]{2,1,0:T(8,128)(2,1)S(1)} %bitcast.51, ...), custom_call_target="tpu_custom_call" | custom-call | flops 3000000000 | bytes 4000000 | tf_op jit(solution)/shard_map/pallas_call | solution.py:171
  74.8 3.7 %shard_map.115 = (f32[96,64]{1,0:T(8,128)S(1)}, bf16[8,192,1024]{2,1,0:T(8,128)(2,1)S(1)}) custom-call(bf16[64,32,128]{2,1,0:T(8,128)(2,1)} %collective-permute-done.5.refs_0_, bf16[2,40,128]{2,1,0:T(8,128)(2,1)S(1)} %get-tuple-element.89.refs_1_, f32[64,8,128]{2,1,0:T(8,128)S(1)} %copy-done.2, bf16[64,32,128]{2,1,0:T(8,128)(2,1)S(1)} %bitcast.52, ...), custom_call_target="tpu_custom_call" | custom-call | flops 3000000000 | bytes 4000000 | tf_op jit(solution)/shard_map/pallas_call | solution.py:171
  78.5 4.2 %shard_map.116 = f32[8,48,128]{2,1,0:T(8,128)S(1)} custom-call(f32[96,64]{1,0:T(8,128)S(1)} %get-tuple-element.36.refs_0_, f32[96,64]{1,0:T(8,128)S(1)} %get-tuple-element.39.refs_1_, f32[96,64]{1,0:T(8,128)S(1)} %get-tuple-element.41.refs_2_, f32[96,64]{1,0:T(8,128)S(1)} %get-tuple-element.43.refs_3_, bf16[8,192,1024]{2,1,0:T(8,128)(2,1)S(1)} %get-tuple-element.44.refs_4_, ...), custom_call_target="tpu_custom_call" | custom-call | flops 3000000000 | bytes 14000000 | tf_op jit(solution)/shard_map/pallas_call | solution.py:215
  82.7 18.0 %all_to_all.20 = f32[8,48,128]{2,1,0:T(8,128)S(1)} all-to-all(f32[8,48,128]{2,1,0:T(8,128)S(1)} %shard_map.116), channel_id=1, replica_groups=mesh['y'=8,'zl'=4,'x'=4,'zh'=2,'c'=2] {'y'}, dimensions={0} | all-to-all | bytes 393216 | tf_op jit(solution)/shard_map/all_to_all | solution.py:253
  100.8 19.7 %all_to_all.21 = f32[16,12,128]{2,1,0:T(8,128)S(1)} all-to-all(f32[16,12,128]{2,1,0:T(8,128)S(1)} %bitcast.56), channel_id=1, replica_groups=mesh['y'=8,'zl'=4,'x'=4,'zh'=2,'c'=2] {'x','zl'}, dimensions={0} | all-to-all | bytes 196608 | tf_op jit(solution)/shard_map/all_to_all | solution.py:255
  120.5 0.7 broadcast_in_dim.24
  121.2 3.4 %all-to-all-start.3 = ((f32[8,48,128]{2,1,0:T(8,128)}), f32[8,48,128]{2,1,0:T(8,128)S(1)}, u32[]{:S(2)}, u32[]{:S(2)}) async-start(f32[8,48,128]{2,1,0:T(8,128)} %broadcast_in_dim.24), calls=%async_computation.3 | async-start | bytes 393216 | tf_op jit(solution)/shard_map/all_to_all | solution.py:257
  124.6 1.0 copy.51
  125.6 1.0 copy.52
  126.6 7.7 %all-to-all-done.3 = f32[8,48,128]{2,1,0:T(8,128)S(1)} async-done(((f32[8,48,128]{2,1,0:T(8,128)}), f32[8,48,128]{2,1,0:T(8,128)S(1)}, u32[]{:S(2)}, u32[]{:S(2)}) %all-to-all-start.3) | async-done | bytes 196640 | tf_op jit(solution)/shard_map/all_to_all | solution.py:257
  134.6 0.7 slice_bitcast_fusion
  (26 shorter events, 1.0 us)
Async XLA Ops:
  2.0 59.2 %collective-permute-start.2 = (bf16[64,32,128]{2,1,0:T(8,128)(2,1)S(1)}, bf16[64,32,128]{2,1,0:T(8,128)(2,1)S(1)}, u32[]{:S(2)}, u32[]{:S(2)}) collective-permute-start(bf16[64,32,128]{2,1,0:T(8,128)(2,1)S(1)} %bitcast.47), channel_id=1, source_target_pairs={{0,1},{1,0},{2,3},{3,2},{4,5},{5,4},{6,7},{7,6},{8,9},{9,8},{10,11... | collective-permute-start | bytes 1572872 | tf_op jit(solution)/shard_map/ppermute | solution.py:18
  3.9 62.2 %collective-permute-start.3 = (bf16[64,32,128]{2,1,0:T(8,128)(2,1)S(1)}, bf16[64,32,128]{2,1,0:T(8,128)(2,1)S(1)}, u32[]{:S(2)}, u32[]{:S(2)}) collective-permute-start(bf16[64,32,128]{2,1,0:T(8,128)(2,1)S(1)} %bitcast.48), channel_id=1, source_target_pairs={{0,2},{2,0},{1,3},{3,1},{4,6},{6,4},{5,7},{7,5},{8,10},{10,8},{9,1... | collective-permute-start | bytes 1572872 | tf_op jit(solution)/shard_map/ppermute | solution.py:18
  19.1 19.3 %collective-permute-start = (bf16[40,128]{1,0:T(8,128)(2,1)}, bf16[40,128]{1,0:T(8,128)(2,1)S(1)}, u32[]{:S(2)}, u32[]{:S(2)}) collective-permute-start(bf16[40,128]{1,0:T(8,128)(2,1)} %get-tuple-element.31), channel_id=1, source_target_pairs={{0,16},{16,32},{32,48},{48,64},{64,80},{80,96},{96,112},{112,128},... | collective-permute-start | bytes 30728 | tf_op jit(solution)/shard_map/ppermute | solution.py:235
  22.5 18.1 %collective-permute-start.1 = (bf16[40,128]{1,0:T(8,128)(2,1)}, bf16[40,128]{1,0:T(8,128)(2,1)S(1)}, u32[]{:S(2)}, u32[]{:S(2)}) collective-permute-start(bf16[40,128]{1,0:T(8,128)(2,1)} %get-tuple-element.32), channel_id=1, source_target_pairs={{16,0},{32,16},{48,32},{64,48},{80,64},{96,80},{112,96},{128,112},... | collective-permute-start | bytes 30728 | tf_op jit(solution)/shard_map/ppermute | solution.py:236
  23.8 44.4 %collective-permute-start.4 = (bf16[64,32,128]{2,1,0:T(8,128)(2,1)}, bf16[64,32,128]{2,1,0:T(8,128)(2,1)S(1)}, u32[]{:S(2)}, u32[]{:S(2)}) collective-permute-start(bf16[64,32,128]{2,1,0:T(8,128)(2,1)} %bitcast.43), channel_id=1, source_target_pairs={{0,12},{4,0},{8,4},{12,8},{1,13},{5,1},{9,5},{13,9},{2,14},{6,2},{... | collective-permute-start | bytes 1572872 | tf_op jit(solution)/shard_map/ppermute | solution.py:18
  38.4 13.7 %copy-start.3 = (bf16[40,128]{1,0:T(8,128)(2,1)}, bf16[40,128]{1,0:T(8,128)(2,1)S(1)}, u32[]{:S(2)}) copy-start(bf16[40,128]{1,0:T(8,128)(2,1)S(1)} %collective-permute-done.left_ref) | copy-start | bytes 30724
  38.4 29.8 %collective-permute-start.5 = (bf16[64,32,128]{2,1,0:T(8,128)(2,1)}, bf16[64,32,128]{2,1,0:T(8,128)(2,1)}, u32[]{:S(2)}, u32[]{:S(2)}) collective-permute-start(bf16[64,32,128]{2,1,0:T(8,128)(2,1)} %bitcast.44), channel_id=1, source_target_pairs={{0,4},{4,8},{8,12},{12,0},{1,5},{5,9},{9,13},{13,1},{2,6},{6,10},{... | collective-permute-start | bytes 1572872 | tf_op jit(solution)/shard_map/ppermute | solution.py:18
  40.6 11.5 %copy-start.4 = (bf16[40,128]{1,0:T(8,128)(2,1)}, bf16[40,128]{1,0:T(8,128)(2,1)S(1)}, u32[]{:S(2)}) copy-start(bf16[40,128]{1,0:T(8,128)(2,1)S(1)} %collective-permute-done.1.right_ref) | copy-start | bytes 30724
  40.6 30.5 %collective-permute-start.6 = (bf16[64,32,128]{2,1,0:T(8,128)(2,1)}, bf16[64,32,128]{2,1,0:T(8,128)(2,1)}, u32[]{:S(2)}, u32[]{:S(2)}) collective-permute-start(bf16[64,32,128]{2,1,0:T(8,128)(2,1)} %bitcast.45), channel_id=1, source_target_pairs={{0,8},{4,12},{8,0},{12,4},{1,9},{5,13},{9,1},{13,5},{2,10},{6,14},... | collective-permute-start | bytes 1572872 | tf_op jit(solution)/shard_map/ppermute | solution.py:18
  45.8 15.4 %all-to-all-start = ((bf16[4,2,40,128]{3,2,1,0:T(8,128)(2,1)}), bf16[4,2,40,128]{3,2,1,0:T(8,128)(2,1)S(1)}, u32[]{:S(2)}, u32[]{:S(2)}) async-start(bf16[4,2,40,128]{3,2,1,0:T(8,128)(2,1)} %broadcast_in_dim.20), calls=%async_computation | async-start | bytes 163840 | tf_op jit(solution)/shard_map/all_to_all | solution.py:238
  61.2 1.0 copy-start
  62.3 0.9 copy-start.1
  63.2 5.0 %copy-start.2 = (f32[64,8,128]{2,1,0:T(8,128)S(1)}, f32[64,8,128]{2,1,0:T(8,128)}, u32[]{:S(2)}) copy-start(f32[64,8,128]{2,1,0:T(8,128)} %shard_map.111.refs_2_) | copy-start | bytes 786436
  66.1 12.4 %collective-permute-start.7 = (bf16[64,32,128]{2,1,0:T(8,128)(2,1)S(1)}, bf16[64,32,128]{2,1,0:T(8,128)(2,1)S(1)}, u32[]{:S(2)}, u32[]{:S(2)}) collective-permute-start(bf16[64,32,128]{2,1,0:T(8,128)(2,1)S(1)} %collective-permute-done.3.refs_8_), channel_id=1, source_target_pairs={{0,1},{1,0},{2,3},{3,2},{4,5},{5,4},{6,7},{7,6},{8,9},{9,8},{10,11... | collective-permute-start | bytes 1572872 | tf_op jit(solution)/shard_map/ppermute | solution.py:18
  121.2 13.1 %all-to-all-start.3 = ((f32[8,48,128]{2,1,0:T(8,128)}), f32[8,48,128]{2,1,0:T(8,128)S(1)}, u32[]{:S(2)}, u32[]{:S(2)}) async-start(f32[8,48,128]{2,1,0:T(8,128)} %broadcast_in_dim.24), calls=%async_computation.3 | async-start | bytes 393216 | tf_op jit(solution)/shard_map/all_to_all | solution.py:257

commit v5 on v4

--- a/solution.py
+++ b/solution.py
@@ -25,8 +25,10 @@
     return value
 
 
-def edges_kernel(u_ref, mat_ref, first_ref, last_ref, mat):
+def edges_kernel(u_ref, mat_ref, first_ref, last_ref, sent_ref, mat):
     mat[...] = mat_ref[...].astype(F32)
+    sent_ref[0:R] = u_ref[...]
+    sent_ref[R : R + 2] = jnp.zeros((2, M, C), BF16)
     pair = lax.broadcasted_iota(jnp.int32, (8, C), 1) // 2
     firsts, lasts = [], []
     for m in range(0, M + 8, 8):
@@ -44,9 +46,9 @@
 def edges(u, material):
     return pl.pallas_call(
         edges_kernel,
-        out_shape=[jax.ShapeDtypeStruct((M + 8, C), BF16)] * 2,
+        out_shape=[jax.ShapeDtypeStruct((M + 8, C), BF16)] * 2 + [jax.ShapeDtypeStruct((R + 2, M, C), BF16)],
         in_specs=[VM, VM],
-        out_specs=[VM] * 2,
+        out_specs=[VM] * 3,
         scratch_shapes=[pltpu.VMEM((R, C), F32)],
         cost_estimate=pl.CostEstimate(flops=10**6, bytes_accessed=10**6, transcendentals=0),
     )(u, material)
@@ -99,7 +101,7 @@
 ROWS = 8
 
 
-def panel_kernel(with_images, u_ref, halo_ref, f_ref, *rest):
+def panel_kernel(with_images, u_ref, f_ref, *rest):
     olds, rest = rest[:2], rest[2:]
     if with_images:
         half_ref, img, mass_ref, stiff_ref, us, s1, s2, q, acc = rest
@@ -111,8 +113,8 @@
     s1[0] = zero
     s1[R + 1] = zero
     lane = lax.broadcasted_iota(jnp.int32, (1, C), 1)
-    left = halo_ref[0].astype(F32)[0:M]
-    right = halo_ref[1].astype(F32)[0:M]
+    left = u_ref[R].astype(F32)
+    right = u_ref[R + 1].astype(F32)
     first = jnp.where(lane % 2 == 0, right, left)
     right = pltpu.roll(right, C - 2, 1)
     second = [jnp.where((lane // 2) % 2 == p, left, right) for p in (0, 1)]
@@ -162,7 +164,7 @@
     half_ref[...] = acc[0 : 3 * M] + acc[3 * M : 6 * M]
 
 
-def panel(u, halo, f, olds, with_images):
+def panel(u, f, olds, with_images):
     outs = [
         jax.ShapeDtypeStruct((3 * M, 2 * M), F32),
         jax.ShapeDtypeStruct((R // ROWS, 6 * M, ROWS * C), BF16),
@@ -171,7 +173,7 @@
     return pl.pallas_call(
         lambda *refs: panel_kernel(with_images, *refs),
         out_shape=outs,
-        in_specs=[VM] * 5,
+        in_specs=[VM] * 4,
         out_specs=[VM] * len(outs),
         scratch_shapes=[
             pltpu.VMEM((R + 4, M, C), F32),
@@ -182,7 +184,7 @@
         ],
         compiler_params=pltpu.CompilerParams(vmem_limit_bytes=20 * 2**20),
         cost_estimate=pl.CostEstimate(flops=PANEL_FLOPS, bytes_accessed=4 * 10**6, transcendentals=0),
-    )(u, halo, f, *olds)
+    )(u, f, *olds)
 
 
 def rest_kernel(*refs):
@@ -225,30 +227,25 @@
 
 def local(old_modes, new_modes, material, density, memb_x, memb_y, bend_table):
     tables = jnp.stack([density, memb_x.astype(F32), memb_y.astype(F32), bend_table])
+    first, last, sent = edges(new_modes.transpose(1, 0, 2), material)
     old = old_modes.transpose(1, 0, 2)
-    new = new_modes.transpose(1, 0, 2)
-    other = shifted(old, "zh", 1)
-    first, last = edges(new, material)
-    first, last, new = lax.optimization_barrier((first, last, new))
-    panels = [new] + [shifted(new, "x", -d) for d in (1, 2, 3)]
     n = 32
     left = lax.ppermute(last, SPACE, [(i, i + 1) for i in range(n - 1)])
     right = lax.ppermute(first, SPACE, [(i + 1, i) for i in range(n - 1)])
-    halo = jnp.stack([left, right])
-    halos = lax.all_to_all(jnp.broadcast_to(halo[None], (4, *halo.shape)), "x", 0, 0)
-    x = lax.axis_index("x")
+    left, right, far, tables = lax.optimization_barrier((left, right, old, tables))
+    other = shifted(far, "zh", 1)
+    own = lax.dynamic_update_slice(sent, jnp.stack([left[:M], right[:M]]), (R, 0, 0))
+    panels = [own] + [shifted(own, "x", -d) for d in (1, 2, 3)]
     f = fields(material, left, right, tables)
     olds = (old, shifted(old, "c", 1))
     halves, terms = [None] * 4, [None] * 4
-    halves[0], terms[0], mass, stiff = panel(new, halo, f, olds, True)
-    halves[0], other = lax.optimization_barrier((halves[0], other))
+    halves[0], terms[0], mass, stiff = panel(own, f, olds, True)
+    halves[0], other, panels[1], panels[3] = lax.optimization_barrier((halves[0], other, panels[1], panels[3]))
     other_core = shifted(other, "c", 1)
-    halves[0], other, panels[1], panels[3] = lax.optimization_barrier((halves[0], other, panels[1], panels[3]))
     for d in (1, 3, 2):
-        beside = lax.dynamic_index_in_dim(halos, lax.rem(x + d, 4), 0, keepdims=False)
         if d == 2:
             halves[1], panels[2] = lax.optimization_barrier((halves[1], panels[2]))
-        halves[d], terms[d] = panel(panels[d], beside, f, olds, False)
+        halves[d], terms[d] = panel(panels[d], f, olds, False)
     parts = rest(halves, terms, (other, other_core))
     parts = jnp.sum(lax.all_to_all(parts, "y", 0, 0), axis=0).reshape(4, 1, PIECE, 4 * M)
     parts = jnp.broadcast_to(parts, (4, 4, PIECE, 4 * M)).reshape(16, PIECE, 4 * M)

time: 137 us -> 124 us (0.905)
  waiting for transfers between devices: 26.1 us -> 9.86 us
  blocking collectives: 37.7 us -> 44.5 us
  starting transfers between devices: 37.5 us -> 32.1 us
  local copies, waits for them, and re-layouts: 9.81 us -> 12 us
    all_to_all x1, blocking collectives: 18 us -> 33.8 us  [local(): lax.all_to_all(parts, 'y', 0, 0)]
    ppermute x1, waiting for transfers between devices: 11.2 us -> 0.01 us  [local(): left = lax.ppermute(last, SPACE, [(i, i + 1) for i in range(n - 1)])]
    all_to_all x1, blocking collectives: 19.7 us -> 10.7 us  [local(): parts = lax.all_to_all(parts, ('x', 'zl'), 0, 0).reshape(4, 4, PIECE, 4 * M)]
    all_to_all x1 -> x0, waiting for transfers between devices: 7.15 us -> none  [local(): lax.all_to_all(jnp.broadcast_to(halo[None], (4, *halo.shape)), 'x', 0, 0)]
    all_to_all x1 -> x0, starting transfers between devices: 5.07 us -> none  [local(): lax.all_to_all(jnp.broadcast_to(halo[None], (4, *halo.shape)), 'x', 0, 0)]
    unnamed x14 -> x22, local copies, waits for them, and re-layouts: 7.56 us -> 10.4 us
    ppermute x6, waiting for transfers between devices: 0.02 us -> 2.15 us  [shifted(): return lax.ppermute(value, axis, [(i, (i + step) % n) for i in range(n)])]
    pallas_call x4, Pallas kernels: 13.1 us -> 11.7 us  [panel(): pl.pallas_call(lambda *refs: panel_kernel(with_images, *refs), out_shape=...]
  transfers between devices with their start and end apart: 10 -> 9, of which waited for: 3 -> 3; matrix products, arithmetic and copies ran while one was open for 5% -> 5% of each run, Pallas kernels for 13% -> 11%
where the time goes in v5:
time: 124 us; the launch traced here: 122 us
  blocking collectives  44.5 us (36%)
  starting transfers between devices  32.1 us (26%)
  Pallas kernels  20.1 us (16%)
  local copies, waits for them, and re-layouts  12 us (10%)
  waiting for transfers between devices  9.86 us (8%)
  other arithmetic  2.63 us (2%)
    all_to_all x1, blocking collectives, local(): lax.all_to_all(parts, 'y', 0, 0)  33.8 us
    ppermute x6, starting transfers between devices, shifted(): return lax.ppermute(value, axis, [(i, (i + step) % n) for i in range(n)])  23.2 us
    pallas_call x4, Pallas kernels, panel(): pl.pallas_call(lambda *refs: panel_kernel(with_images, *refs), out_shape=...  11.7 us
    all_to_all x1, blocking collectives, local(): parts = lax.all_to_all(parts, ('x', 'zl'), 0, 0).reshape(4, 4, PIECE, 4 * M)  10.7 us
    unnamed x22, local copies, waits for them, and re-layouts  10.4 us
    all_to_all x1, waiting for transfers between devices, local(): lax.all_to_all(jnp.broadcast_to(parts, (8, 4 * PIECE, 4 * M)), 'y', 0, 0)  7.7 us
    ppermute x1, starting transfers between devices, local(): left = lax.ppermute(last, SPACE, [(i, i + 1) for i in range(n - 1)])  4.26 us
    pallas_call x1, Pallas kernels, rest(): pl.pallas_call(rest_kernel, out_shape=jax.ShapeDtypeStruct((8, 4 * PIECE,...  4.17 us
  transfers between devices with their start and end apart: 9, of which 3 were waited for; matrix products, arithmetic and copies ran while one was open for 5% of the time, Pallas kernels for 11%

profile of v5, /device:TPU:6, one launch (start us, length us, event | category | flops | bytes accessed | tf_op | source)
XLA Modules:
  0.0 122.1 jit_solution(14632062655492990368)
XLA Ops:
  0.6 2.2 %copy.60 = bf16[32,64,128]{2,0,1:T(8,128)(2,1)} copy(bf16[32,64,128]{2,1,0:T(8,128)(2,1)} %param.8) | data formatting | bytes 1048576 | tf_op args[1]
  2.8 2.3 %shard_map.110 = (bf16[40,128]{1,0:T(8,128)(2,1)}, bf16[40,128]{1,0:T(8,128)(2,1)}, bf16[66,32,128]{2,1,0:T(8,128)(2,1)}) custom-call(bf16[64,32,128]{2,1,0:T(8,128)(2,1)} %bitcast.46, s32[64,128]{1,0:T(8,128)} %mat_ref.3), custom_call_target="tpu_custom_call" | custom-call | flops 1000000 | bytes 1000000 | tf_op jit(solution)/shard_map/pallas_call | solution.py:47
  5.1 4.3 %collective-permute-start = (bf16[40,128]{1,0:T(8,128)(2,1)}, bf16[40,128]{1,0:T(8,128)(2,1)S(1)}, u32[]{:S(2)}, u32[]{:S(2)}) collective-permute-start(bf16[40,128]{1,0:T(8,128)(2,1)} %get-tuple-element.29), channel_id=1, source_target_pairs={{0,16},{16,32},{32,48},{48,64},{64,80},{80,96},{96,112},{112,128},... | collective-permute-start | bytes 30728 | tf_op jit(solution)/shard_map/ppermute | solution.py:233
  9.4 1.3 %collective-permute-start.1 = (bf16[40,128]{1,0:T(8,128)(2,1)}, bf16[40,128]{1,0:T(8,128)(2,1)S(1)}, u32[]{:S(2)}, u32[]{:S(2)}) collective-permute-start(bf16[40,128]{1,0:T(8,128)(2,1)} %get-tuple-element.30), channel_id=1, source_target_pairs={{16,0},{32,16},{48,32},{64,48},{80,64},{96,80},{112,96},{128,112},... | collective-permute-start | bytes 30728 | tf_op jit(solution)/shard_map/ppermute | solution.py:234
  10.7 1.4 %copy.59 = bf16[32,64,128]{2,0,1:T(8,128)(2,1)S(1)} copy(bf16[32,64,128]{2,1,0:T(8,128)(2,1)} %param.7) | data formatting | bytes 1048576 | tf_op args[0]
  12.1 1.9 %collective-permute-start.2 = (bf16[64,32,128]{2,1,0:T(8,128)(2,1)S(1)}, bf16[64,32,128]{2,1,0:T(8,128)(2,1)S(1)}, u32[]{:S(2)}, u32[]{:S(2)}) collective-permute-start(bf16[64,32,128]{2,1,0:T(8,128)(2,1)S(1)} %bitcast.38), channel_id=1, source_target_pairs={{0,1},{1,0},{2,3},{3,2},{4,5},{5,4},{6,7},{7,6},{8,9},{9,8},{10,11... | collective-permute-start | bytes 1572872 | tf_op jit(solution)/shard_map/ppermute | solution.py:18
  14.7 1.3 %pad_maximum_fusion.tables_ref = f32[4,12]{1,0:T(4,128)} fusion(f32[1,12]{1,0:T(1,128)} %bitcast.49, f32[1,12]{1,0:T(1,128)S(1)} %get-tuple-element.89, f32[1,12]{1,0:T(1,128)S(1)} %get-tuple-element.90, f32[1,12]{1,0:T(1,128)} %bitcast.50), kind=kLoop, calls=%fused_computation.10 | loop fusion | flops 144 | bytes 384 | tf_op jit(solution)/shard_map/stack | solution.py:229
  16.6 2.7 %collective-permute-start.4 = (bf16[66,32,128]{2,1,0:T(8,128)(2,1)}, bf16[66,32,128]{2,1,0:T(8,128)(2,1)}, u32[]{:S(2)}, u32[]{:S(2)}) collective-permute-start(bf16[66,32,128]{2,1,0:T(8,128)(2,1)} %maximum_dynamic-update-slice_fusion.refs_0_), channel_id=1, source_target_pairs={{0,12},{4,0},{8,4},{12,8},{1,13},{5,1},{9,5},{13,9},{2,14},{6,2},{... | collective-permute-start | bytes 1622024 | tf_op jit(solution)/shard_map/ppermute | solution.py:18
  19.3 4.3 %collective-permute-start.5 = (bf16[66,32,128]{2,1,0:T(8,128)(2,1)}, bf16[66,32,128]{2,1,0:T(8,128)(2,1)S(1)}, u32[]{:S(2)}, u32[]{:S(2)}) collective-permute-start(bf16[66,32,128]{2,1,0:T(8,128)(2,1)} %maximum_dynamic-update-slice_fusion.refs_0_), channel_id=1, source_target_pairs={{0,4},{4,8},{8,12},{12,0},{1,5},{5,9},{9,13},{13,1},{2,6},{6,10},{... | collective-permute-start | bytes 1622024 | tf_op jit(solution)/shard_map/ppermute | solution.py:18
  23.6 10.0 %collective-permute-start.3 = (bf16[64,32,128]{2,1,0:T(8,128)(2,1)S(1)}, bf16[64,32,128]{2,1,0:T(8,128)(2,1)S(1)}, u32[]{:S(2)}, u32[]{:S(2)}) collective-permute-start(bf16[64,32,128]{2,1,0:T(8,128)(2,1)S(1)} %bitcast.39), channel_id=1, source_target_pairs={{0,2},{2,0},{1,3},{3,1},{4,6},{6,4},{5,7},{7,5},{8,10},{10,8},{9,1... | collective-permute-start | bytes 1572872 | tf_op jit(solution)/shard_map/ppermute | solution.py:18
  33.6 2.1 %collective-permute-start.6 = (bf16[66,32,128]{2,1,0:T(8,128)(2,1)}, bf16[66,32,128]{2,1,0:T(8,128)(2,1)S(1)}, u32[]{:S(2)}, u32[]{:S(2)}) collective-permute-start(bf16[66,32,128]{2,1,0:T(8,128)(2,1)} %maximum_dynamic-update-slice_fusion.refs_0_), channel_id=1, source_target_pairs={{0,8},{4,12},{8,0},{12,4},{1,9},{5,13},{9,1},{13,5},{2,10},{6,14},... | collective-permute-start | bytes 1622024 | tf_op jit(solution)/shard_map/ppermute | solution.py:18
  35.8 1.9 %shard_map.111.refs_1_ = f32[64,8,128]{2,1,0:T(8,128)} custom-call(s32[64,128]{1,0:T(8,128)} %mat_ref.3, bf16[40,128]{1,0:T(8,128)(2,1)} %copy-done.7, bf16[40,128]{1,0:T(8,128)(2,1)} %copy-done.8, f32[4,12]{1,0:T(4,128)} %pad_maximum_fusion.tables_ref), custom_call_target="tpu_custom_call" | custom-call | flops 1000000 | bytes 1000000 | tf_op jit(solution)/shard_map/pallas_call | solution.py:89
  37.7 0.8 copy-done.3
  38.5 0.9 copy-done
  39.4 1.0 copy-done.2
  40.5 1.0 copy-done.4
  41.5 2.6 %shard_map.112 = (f32[96,64]{1,0:T(8,128)S(1)}, bf16[8,192,1024]{2,1,0:T(8,128)(2,1)S(1)}, bf16[64,32,128]{2,1,0:T(8,128)(2,1)S(1)}, bf16[64,32,128]{2,1,0:T(8,128)(2,1)S(1)}) custom-call(bf16[66,32,128]{2,1,0:T(8,128)(2,1)S(1)} %copy-done.2, f32[64,8,128]{2,1,0:T(8,128)S(1)} %copy-done, bf16[64,32,128]{2,1,0:T(8,128)(2,1)S(1)} %bitcast.40, ...), custom_call_target="tpu_custom_call" | custom-call | flops 3000000000 | bytes 4000000 | tf_op jit(solution)/shard_map/pallas_call | solution.py:173
  44.2 1.6 %collective-permute-done.3.refs_8_ = bf16[64,32,128]{2,1,0:T(8,128)(2,1)S(1)} collective-permute-done((bf16[64,32,128]{2,1,0:T(8,128)(2,1)S(1)}, bf16[64,32,128]{2,1,0:T(8,128)(2,1)S(1)}, u32[]{:S(2)}, u32[]{:S(2)}) %collective-permute-start.3) | collective-permute-done | bytes 524320 | tf_op jit(solution)/shard_map/ppermute | solution.py:18
  45.8 1.0 copy-done.5
  46.9 3.7 %shard_map.113 = (f32[96,64]{1,0:T(8,128)S(1)}, bf16[8,192,1024]{2,1,0:T(8,128)(2,1)S(1)}) custom-call(bf16[66,32,128]{2,1,0:T(8,128)(2,1)} %collective-permute-done.4.refs_0_, f32[64,8,128]{2,1,0:T(8,128)S(1)} %copy-done.1, bf16[64,32,128]{2,1,0:T(8,128)(2,1)S(1)} %bitcast.41, bf16[64,32,128]{2,1,0:T(8,128)(2,1)S(1)} %copy-done.5), custom_call_target="tpu_custom_call" | custom-call | flops 3000000000 | bytes 4000000 | tf_op jit(solution)/shard_map/pallas_call | solution.py:173
  51.1 2.1 %collective-permute-start.7 = (bf16[64,32,128]{2,1,0:T(8,128)(2,1)S(1)}, bf16[64,32,128]{2,1,0:T(8,128)(2,1)S(1)}, u32[]{:S(2)}, u32[]{:S(2)}) collective-permute-start(bf16[64,32,128]{2,1,0:T(8,128)(2,1)S(1)} %collective-permute-done.3.refs_8_), channel_id=1, source_target_pairs={{0,1},{1,0},{2,3},{3,2},{4,5},{5,4},{6,7},{7,6},{8,9},{9,8},{10,11... | collective-permute-start | bytes 1572872 | tf_op jit(solution)/shard_map/ppermute | solution.py:18
  53.2 2.7 %shard_map.115 = (f32[96,64]{1,0:T(8,128)S(1)}, bf16[8,192,1024]{2,1,0:T(8,128)(2,1)S(1)}) custom-call(bf16[66,32,128]{2,1,0:T(8,128)(2,1)S(1)} %collective-permute-done.5.refs_0_, f32[64,8,128]{2,1,0:T(8,128)S(1)} %copy-done.1, bf16[64,32,128]{2,1,0:T(8,128)(2,1)S(1)} %bitcast.42, bf16[64,32,128]{2,1,0:T(8,128)(2,1)S(1)} %copy-done.6), custom_call_target="tpu_custom_call" | custom-call | flops 3000000000 | bytes 4000000 | tf_op jit(solution)/shard_map/pallas_call | solution.py:173
  55.9 2.7 %shard_map.114 = (f32[96,64]{1,0:T(8,128)S(1)}, bf16[8,192,1024]{2,1,0:T(8,128)(2,1)S(1)}) custom-call(bf16[66,32,128]{2,1,0:T(8,128)(2,1)S(1)} %collective-permute-done.6.refs_0_, f32[64,8,128]{2,1,0:T(8,128)S(1)} %copy-done.1, bf16[64,32,128]{2,1,0:T(8,128)(2,1)S(1)} %bitcast.43, bf16[64,32,128]{2,1,0:T(8,128)(2,1)S(1)} %copy-done.6), custom_call_target="tpu_custom_call" | custom-call | flops 3000000000 | bytes 4000000 | tf_op jit(solution)/shard_map/pallas_call | solution.py:173
  58.6 4.2 %shard_map.116 = f32[8,48,128]{2,1,0:T(8,128)S(1)} custom-call(f32[96,64]{1,0:T(8,128)S(1)} %get-tuple-element.36.refs_0_, f32[96,64]{1,0:T(8,128)S(1)} %get-tuple-element.39.refs_1_, f32[96,64]{1,0:T(8,128)S(1)} %get-tuple-element.41.refs_2_, f32[96,64]{1,0:T(8,128)S(1)} %get-tuple-element.43.refs_3_, bf16[8,192,1024]{2,1,0:T(8,128)(2,1)S(1)} %get-tuple-element.44.refs_4_, ...), custom_call_target="tpu_custom_call" | custom-call | flops 3000000000 | bytes 14000000 | tf_op jit(solution)/shard_map/pallas_call | solution.py:217
  62.8 33.8 %all_to_all.15 = f32[8,48,128]{2,1,0:T(8,128)S(1)} all-to-all(f32[8,48,128]{2,1,0:T(8,128)S(1)} %shard_map.116), channel_id=1, replica_groups=mesh['y'=8,'zl'=4,'x'=4,'zh'=2,'c'=2] {'y'}, dimensions={0} | all-to-all | bytes 393216 | tf_op jit(solution)/shard_map/all_to_all | solution.py:250
  96.6 10.7 %all_to_all.16 = f32[16,12,128]{2,1,0:T(8,128)S(1)} all-to-all(f32[16,12,128]{2,1,0:T(8,128)S(1)} %bitcast.48), channel_id=1, replica_groups=mesh['y'=8,'zl'=4,'x'=4,'zh'=2,'c'=2] {'x','zl'}, dimensions={0} | all-to-all | bytes 196608 | tf_op jit(solution)/shard_map/all_to_all | solution.py:252
  107.4 0.7 broadcast_in_dim.17
  108.1 3.4 %all-to-all-start.2 = ((f32[8,48,128]{2,1,0:T(8,128)}), f32[8,48,128]{2,1,0:T(8,128)S(1)}, u32[]{:S(2)}, u32[]{:S(2)}) async-start(f32[8,48,128]{2,1,0:T(8,128)} %broadcast_in_dim.17), calls=%async_computation.2 | async-start | bytes 393216 | tf_op jit(solution)/shard_map/all_to_all | solution.py:254
  111.5 1.0 copy.51
  112.5 1.0 copy.52
  113.5 7.7 %all-to-all-done.2 = f32[8,48,128]{2,1,0:T(8,128)S(1)} async-done(((f32[8,48,128]{2,1,0:T(8,128)}), f32[8,48,128]{2,1,0:T(8,128)S(1)}, u32[]{:S(2)}, u32[]{:S(2)}) %all-to-all-start.2) | async-done | bytes 196640 | tf_op jit(solution)/shard_map/all_to_all | solution.py:254
  121.5 0.7 slice_bitcast_fusion
  (32 shorter events, 2.2 us)
Async XLA Ops:
  5.1 10.8 %collective-permute-start = (bf16[40,128]{1,0:T(8,128)(2,1)}, bf16[40,128]{1,0:T(8,128)(2,1)S(1)}, u32[]{:S(2)}, u32[]{:S(2)}) collective-permute-start(bf16[40,128]{1,0:T(8,128)(2,1)} %get-tuple-element.29), channel_id=1, source_target_pairs={{0,16},{16,32},{32,48},{48,64},{64,80},{80,96},{96,112},{112,128},... | collective-permute-start | bytes 30728 | tf_op jit(solution)/shard_map/ppermute | solution.py:233
  9.4 6.6 %collective-permute-start.1 = (bf16[40,128]{1,0:T(8,128)(2,1)}, bf16[40,128]{1,0:T(8,128)(2,1)S(1)}, u32[]{:S(2)}, u32[]{:S(2)}) collective-permute-start(bf16[40,128]{1,0:T(8,128)(2,1)} %get-tuple-element.30), channel_id=1, source_target_pairs={{16,0},{32,16},{48,32},{64,48},{80,64},{96,80},{112,96},{128,112},... | collective-permute-start | bytes 30728 | tf_op jit(solution)/shard_map/ppermute | solution.py:234
  12.1 25.6 %collective-permute-start.2 = (bf16[64,32,128]{2,1,0:T(8,128)(2,1)S(1)}, bf16[64,32,128]{2,1,0:T(8,128)(2,1)S(1)}, u32[]{:S(2)}, u32[]{:S(2)}) collective-permute-start(bf16[64,32,128]{2,1,0:T(8,128)(2,1)S(1)} %bitcast.38), channel_id=1, source_target_pairs={{0,1},{1,0},{2,3},{3,2},{4,5},{5,4},{6,7},{7,6},{8,9},{9,8},{10,11... | collective-permute-start | bytes 1572872 | tf_op jit(solution)/shard_map/ppermute | solution.py:18
  15.9 19.8 %copy-start.7 = (bf16[40,128]{1,0:T(8,128)(2,1)}, bf16[40,128]{1,0:T(8,128)(2,1)S(1)}, u32[]{:S(2)}) copy-start(bf16[40,128]{1,0:T(8,128)(2,1)S(1)} %collective-permute-done.left_ref) | copy-start | bytes 30724
  15.9 19.8 %copy-start.8 = (bf16[40,128]{1,0:T(8,128)(2,1)}, bf16[40,128]{1,0:T(8,128)(2,1)S(1)}, u32[]{:S(2)}) copy-start(bf16[40,128]{1,0:T(8,128)(2,1)S(1)} %collective-permute-done.1.right_ref) | copy-start | bytes 30724
  16.6 29.2 %collective-permute-start.4 = (bf16[66,32,128]{2,1,0:T(8,128)(2,1)}, bf16[66,32,128]{2,1,0:T(8,128)(2,1)}, u32[]{:S(2)}, u32[]{:S(2)}) collective-permute-start(bf16[66,32,128]{2,1,0:T(8,128)(2,1)} %maximum_dynamic-update-slice_fusion.refs_0_), channel_id=1, source_target_pairs={{0,12},{4,0},{8,4},{12,8},{1,13},{5,1},{9,5},{13,9},{2,14},{6,2},{... | collective-permute-start | bytes 1622024 | tf_op jit(solution)/shard_map/ppermute | solution.py:18
  19.3 26.5 %collective-permute-start.5 = (bf16[66,32,128]{2,1,0:T(8,128)(2,1)}, bf16[66,32,128]{2,1,0:T(8,128)(2,1)S(1)}, u32[]{:S(2)}, u32[]{:S(2)}) collective-permute-start(bf16[66,32,128]{2,1,0:T(8,128)(2,1)} %maximum_dynamic-update-slice_fusion.refs_0_), channel_id=1, source_target_pairs={{0,4},{4,8},{8,12},{12,0},{1,5},{5,9},{9,13},{13,1},{2,6},{6,10},{... | collective-permute-start | bytes 1622024 | tf_op jit(solution)/shard_map/ppermute | solution.py:18
  23.6 22.2 %collective-permute-start.3 = (bf16[64,32,128]{2,1,0:T(8,128)(2,1)S(1)}, bf16[64,32,128]{2,1,0:T(8,128)(2,1)S(1)}, u32[]{:S(2)}, u32[]{:S(2)}) collective-permute-start(bf16[64,32,128]{2,1,0:T(8,128)(2,1)S(1)} %bitcast.39), channel_id=1, source_target_pairs={{0,2},{2,0},{1,3},{3,1},{4,6},{6,4},{5,7},{7,5},{8,10},{10,8},{9,1... | collective-permute-start | bytes 1572872 | tf_op jit(solution)/shard_map/ppermute | solution.py:18
  33.6 17.4 %collective-permute-start.6 = (bf16[66,32,128]{2,1,0:T(8,128)(2,1)}, bf16[66,32,128]{2,1,0:T(8,128)(2,1)S(1)}, u32[]{:S(2)}, u32[]{:S(2)}) collective-permute-start(bf16[66,32,128]{2,1,0:T(8,128)(2,1)} %maximum_dynamic-update-slice_fusion.refs_0_), channel_id=1, source_target_pairs={{0,8},{4,12},{8,0},{12,4},{1,9},{5,13},{9,1},{13,5},{2,10},{6,14},... | collective-permute-start | bytes 1622024 | tf_op jit(solution)/shard_map/ppermute | solution.py:18
  37.7 0.8 copy-start.3
  38.5 0.9 copy-start
  39.4 1.0 copy-start.2
  40.5 1.0 copy-start.4
  41.5 4.3 %copy-start.1 = (f32[64,8,128]{2,1,0:T(8,128)S(1)}, f32[64,8,128]{2,1,0:T(8,128)}, u32[]{:S(2)}) copy-start(f32[64,8,128]{2,1,0:T(8,128)} %shard_map.111.refs_1_) | copy-start | bytes 786436
  45.8 1.0 copy-start.5
  46.9 6.3 %copy-start.6 = (bf16[64,32,128]{2,1,0:T(8,128)(2,1)S(1)}, bf16[64,32,128]{2,1,0:T(8,128)(2,1)}, u32[]{:S(2)}) copy-start(bf16[64,32,128]{2,1,0:T(8,128)(2,1)} %copy-done.3) | copy-start | bytes 1572868
  51.1 7.5 %collective-permute-start.7 = (bf16[64,32,128]{2,1,0:T(8,128)(2,1)S(1)}, bf16[64,32,128]{2,1,0:T(8,128)(2,1)S(1)}, u32[]{:S(2)}, u32[]{:S(2)}) collective-permute-start(bf16[64,32,128]{2,1,0:T(8,128)(2,1)S(1)} %collective-permute-done.3.refs_8_), channel_id=1, source_target_pairs={{0,1},{1,0},{2,3},{3,2},{4,5},{5,4},{6,7},{7,6},{8,9},{9,8},{10,11... | collective-permute-start | bytes 1572872 | tf_op jit(solution)/shard_map/ppermute | solution.py:18
  108.1 13.1 %all-to-all-start.2 = ((f32[8,48,128]{2,1,0:T(8,128)}), f32[8,48,128]{2,1,0:T(8,128)S(1)}, u32[]{:S(2)}, u32[]{:S(2)}) async-start(f32[8,48,128]{2,1,0:T(8,128)} %broadcast_in_dim.17), calls=%async_computation.2 | async-start | bytes 393216 | tf_op jit(solution)/shard_map/all_to_all | solution.py:254

commit v6 on v5

--- a/solution.py
+++ b/solution.py
@@ -228,23 +228,25 @@
 def local(old_modes, new_modes, material, density, memb_x, memb_y, bend_table):
     tables = jnp.stack([density, memb_x.astype(F32), memb_y.astype(F32), bend_table])
     first, last, sent = edges(new_modes.transpose(1, 0, 2), material)
+    first, last, old_modes = lax.optimization_barrier((first, last, old_modes))
     old = old_modes.transpose(1, 0, 2)
+    other = shifted(old, "zh", 1)
     n = 32
     left = lax.ppermute(last, SPACE, [(i, i + 1) for i in range(n - 1)])
     right = lax.ppermute(first, SPACE, [(i + 1, i) for i in range(n - 1)])
-    left, right, far, tables = lax.optimization_barrier((left, right, old, tables))
-    other = shifted(far, "zh", 1)
+    left, right, near, tables = lax.optimization_barrier((left, right, old, tables))
     own = lax.dynamic_update_slice(sent, jnp.stack([left[:M], right[:M]]), (R, 0, 0))
     panels = [own] + [shifted(own, "x", -d) for d in (1, 2, 3)]
     f = fields(material, left, right, tables)
-    olds = (old, shifted(old, "c", 1))
+    olds = (old, shifted(near, "c", 1))
     halves, terms = [None] * 4, [None] * 4
+    f, other = lax.optimization_barrier((f, other))
+    other_core = shifted(other, "c", 1)
     halves[0], terms[0], mass, stiff = panel(own, f, olds, True)
-    halves[0], other, panels[1], panels[3] = lax.optimization_barrier((halves[0], other, panels[1], panels[3]))
-    other_core = shifted(other, "c", 1)
+    halves[0], panels[1], panels[3] = lax.optimization_barrier((halves[0], panels[1], panels[3]))
     for d in (1, 3, 2):
         if d == 2:
-            halves[1], panels[2] = lax.optimization_barrier((halves[1], panels[2]))
+            halves[3], panels[2] = lax.optimization_barrier((halves[3], panels[2]))
         halves[d], terms[d] = panel(panels[d], f, olds, False)
     parts = rest(halves, terms, (other, other_core))
     parts = jnp.sum(lax.all_to_all(parts, "y", 0, 0), axis=0).reshape(4, 1, PIECE, 4 * M)

time: 124 us -> 124 us (level)
  blocking collectives: 44.5 us -> 34.6 us
  waiting for transfers between devices: 9.86 us -> 18.9 us
    all_to_all x1, blocking collectives: 33.8 us -> 21.8 us  [local(): lax.all_to_all(parts, 'y', 0, 0)]
    ppermute x6, waiting for transfers between devices: 2.15 us -> 11.2 us  [shifted(): return lax.ppermute(value, axis, [(i, (i + step) % n) for i in range(n)])]
    all_to_all x1, blocking collectives: 10.7 us -> 12.8 us  [local(): parts = lax.all_to_all(parts, ('x', 'zl'), 0, 0).reshape(4, 4, PIECE, 4 * M)]
    unnamed x22 -> x19, local copies, waits for them, and re-layouts: 10.4 us -> 9.05 us
    optimization_barrier x0 -> x1, local copies, waits for them, and re-layouts: none -> 1.39 us  [local(): first, last, old_modes = lax.optimization_barrier((first, last, old_modes))]
  transfers between devices with their start and end apart: 9 -> 9, of which waited for: 3 -> 3; matrix products, arithmetic and copies ran while one was open for 5% -> 5% of each run, Pallas kernels for 11% -> 12%
where the time goes in v6:
time: 124 us; the launch traced here: 122 us
  blocking collectives  34.6 us (28%)
  starting transfers between devices  32.1 us (26%)
  Pallas kernels  21.3 us (17%)
  waiting for transfers between devices  18.9 us (15%)
  local copies, waits for them, and re-layouts  12 us (10%)
  other arithmetic  2.63 us (2%)
    ppermute x6, starting transfers between devices, shifted(): return lax.ppermute(value, axis, [(i, (i + step) % n) for i in range(n)])  23.2 us
    all_to_all x1, blocking collectives, local(): lax.all_to_all(parts, 'y', 0, 0)  21.8 us
    all_to_all x1, blocking collectives, local(): parts = lax.all_to_all(parts, ('x', 'zl'), 0, 0).reshape(4, 4, PIECE, 4 * M)  12.8 us
    pallas_call x4, Pallas kernels, panel(): pl.pallas_call(lambda *refs: panel_kernel(with_images, *refs), out_shape=...  12.7 us
    ppermute x6, waiting for transfers between devices, shifted(): return lax.ppermute(value, axis, [(i, (i + step) % n) for i in range(n)])  11.2 us
    unnamed x19, local copies, waits for them, and re-layouts  9.05 us
    all_to_all x1, waiting for transfers between devices, local(): lax.all_to_all(jnp.broadcast_to(parts, (8, 4 * PIECE, 4 * M)), 'y', 0, 0)  7.69 us
    pallas_call x1, Pallas kernels, rest(): pl.pallas_call(rest_kernel, out_shape=jax.ShapeDtypeStruct((8, 4 * PIECE,...  4.41 us
  transfers between devices with their start and end apart: 9, of which 3 were waited for; matrix products, arithmetic and copies ran while one was open for 5% of the time, Pallas kernels for 12%

profile of v6, /device:TPU:6, one launch (start us, length us, event | category | flops | bytes accessed | tf_op | source)
XLA Modules:
  0.0 122.4 jit_solution(2595264646886258352)
XLA Ops:
  0.6 2.2 %copy.60 = bf16[32,64,128]{2,0,1:T(8,128)(2,1)} copy(bf16[32,64,128]{2,1,0:T(8,128)(2,1)} %param.8) | data formatting | bytes 1048576 | tf_op args[1]
  2.8 2.3 %shard_map.110 = (bf16[40,128]{1,0:T(8,128)(2,1)}, bf16[40,128]{1,0:T(8,128)(2,1)}, bf16[66,32,128]{2,1,0:T(8,128)(2,1)}) custom-call(bf16[64,32,128]{2,1,0:T(8,128)(2,1)} %bitcast.46, s32[64,128]{1,0:T(8,128)} %mat_ref.3), custom_call_target="tpu_custom_call" | custom-call | flops 1000000 | bytes 1000000 | tf_op jit(solution)/shard_map/pallas_call | solution.py:47
  5.1 4.3 %collective-permute-start = (bf16[40,128]{1,0:T(8,128)(2,1)}, bf16[40,128]{1,0:T(8,128)(2,1)S(1)}, u32[]{:S(2)}, u32[]{:S(2)}) collective-permute-start(bf16[40,128]{1,0:T(8,128)(2,1)} %get-tuple-element.35), channel_id=1, source_target_pairs={{0,16},{16,32},{32,48},{48,64},{64,80},{80,96},{96,112},{112,128},... | collective-permute-start | bytes 30728 | tf_op jit(solution)/shard_map/ppermute | solution.py:235
  9.4 1.3 %collective-permute-start.1 = (bf16[40,128]{1,0:T(8,128)(2,1)}, bf16[40,128]{1,0:T(8,128)(2,1)S(1)}, u32[]{:S(2)}, u32[]{:S(2)}) collective-permute-start(bf16[40,128]{1,0:T(8,128)(2,1)} %get-tuple-element.36), channel_id=1, source_target_pairs={{16,0},{32,16},{48,32},{64,48},{80,64},{96,80},{112,96},{128,112},... | collective-permute-start | bytes 30728 | tf_op jit(solution)/shard_map/ppermute | solution.py:236
  10.7 1.4 %copy.59 = bf16[32,64,128]{2,0,1:T(8,128)(2,1)S(1)} copy(bf16[32,64,128]{2,1,0:T(8,128)(2,1)} %param.7) | data formatting | bytes 1048576 | tf_op jit(solution)/shard_map/optimization_barrier | solution.py:231
  12.0 10.0 %collective-permute-start.2 = (bf16[64,32,128]{2,1,0:T(8,128)(2,1)S(1)}, bf16[64,32,128]{2,1,0:T(8,128)(2,1)S(1)}, u32[]{:S(2)}, u32[]{:S(2)}) collective-permute-start(bf16[64,32,128]{2,1,0:T(8,128)(2,1)S(1)} %bitcast.38), channel_id=1, source_target_pairs={{0,2},{2,0},{1,3},{3,1},{4,6},{6,4},{5,7},{7,5},{8,10},{10,8},{9,1... | collective-permute-start | bytes 1572872 | tf_op jit(solution)/shard_map/ppermute | solution.py:18
  22.7 1.3 %pad_maximum_fusion.tables_ref = f32[4,12]{1,0:T(4,128)} fusion(f32[1,12]{1,0:T(1,128)} %bitcast.49, f32[1,12]{1,0:T(1,128)S(1)} %get-tuple-element.97, f32[1,12]{1,0:T(1,128)S(1)} %get-tuple-element.98, f32[1,12]{1,0:T(1,128)} %bitcast.50), kind=kLoop, calls=%fused_computation.10 | loop fusion | flops 144 | bytes 384 | tf_op jit(solution)/shard_map/stack | solution.py:229
  24.0 1.9 %collective-permute-start.3 = (bf16[64,32,128]{2,1,0:T(8,128)(2,1)S(1)}, bf16[64,32,128]{2,1,0:T(8,128)(2,1)S(1)}, u32[]{:S(2)}, u32[]{:S(2)}) collective-permute-start(bf16[64,32,128]{2,1,0:T(8,128)(2,1)S(1)} %bitcast.39), channel_id=1, source_target_pairs={{0,1},{1,0},{2,3},{3,2},{4,5},{5,4},{6,7},{7,6},{8,9},{9,8},{10,11... | collective-permute-start | bytes 1572872 | tf_op jit(solution)/shard_map/ppermute | solution.py:18
  26.6 2.7 %collective-permute-start.4 = (bf16[66,32,128]{2,1,0:T(8,128)(2,1)}, bf16[66,32,128]{2,1,0:T(8,128)(2,1)S(1)}, u32[]{:S(2)}, u32[]{:S(2)}) collective-permute-start(bf16[66,32,128]{2,1,0:T(8,128)(2,1)} %maximum_dynamic-update-slice_fusion.refs_0_), channel_id=1, source_target_pairs={{0,12},{4,0},{8,4},{12,8},{1,13},{5,1},{9,5},{13,9},{2,14},{6,2},{... | collective-permute-start | bytes 1622024 | tf_op jit(solution)/shard_map/ppermute | solution.py:18
  29.3 4.3 %collective-permute-start.5 = (bf16[66,32,128]{2,1,0:T(8,128)(2,1)}, bf16[66,32,128]{2,1,0:T(8,128)(2,1)}, u32[]{:S(2)}, u32[]{:S(2)}) collective-permute-start(bf16[66,32,128]{2,1,0:T(8,128)(2,1)} %maximum_dynamic-update-slice_fusion.refs_0_), channel_id=1, source_target_pairs={{0,4},{4,8},{8,12},{12,0},{1,5},{5,9},{9,13},{13,1},{2,6},{6,10},{... | collective-permute-start | bytes 1622024 | tf_op jit(solution)/shard_map/ppermute | solution.py:18
  33.6 2.1 %collective-permute-start.6 = (bf16[66,32,128]{2,1,0:T(8,128)(2,1)}, bf16[66,32,128]{2,1,0:T(8,128)(2,1)}, u32[]{:S(2)}, u32[]{:S(2)}) collective-permute-start(bf16[66,32,128]{2,1,0:T(8,128)(2,1)} %maximum_dynamic-update-slice_fusion.refs_0_), channel_id=1, source_target_pairs={{0,8},{4,12},{8,0},{12,4},{1,9},{5,13},{9,1},{13,5},{2,10},{6,14},... | collective-permute-start | bytes 1622024 | tf_op jit(solution)/shard_map/ppermute | solution.py:18
  35.8 1.9 %shard_map.111.refs_1_ = f32[64,8,128]{2,1,0:T(8,128)} custom-call(s32[64,128]{1,0:T(8,128)} %mat_ref.3, bf16[40,128]{1,0:T(8,128)(2,1)} %copy-done.6, bf16[40,128]{1,0:T(8,128)(2,1)} %copy-done.7, f32[4,12]{1,0:T(4,128)} %pad_maximum_fusion.tables_ref), custom_call_target="tpu_custom_call" | custom-call | flops 1000000 | bytes 1000000 | tf_op jit(solution)/shard_map/pallas_call | solution.py:89
  37.7 2.1 %collective-permute-start.7 = (bf16[64,32,128]{2,1,0:T(8,128)(2,1)S(1)}, bf16[64,32,128]{2,1,0:T(8,128)(2,1)S(1)}, u32[]{:S(2)}, u32[]{:S(2)}) collective-permute-start(bf16[64,32,128]{2,1,0:T(8,128)(2,1)S(1)} %collective-permute-done.2.refs_8_), channel_id=1, source_target_pairs={{0,1},{1,0},{2,3},{3,2},{4,5},{5,4},{6,7},{7,6},{8,9},{9,8},{10,11... | collective-permute-start | bytes 1572872 | tf_op jit(solution)/shard_map/ppermute | solution.py:18
  39.8 0.8 copy-done.2
  40.6 0.9 copy-done
  41.5 1.0 copy-done.1
  42.6 1.0 copy-done.3
  43.6 2.6 %shard_map.112 = (f32[96,64]{1,0:T(8,128)S(1)}, bf16[8,192,1024]{2,1,0:T(8,128)(2,1)S(1)}, bf16[64,32,128]{2,1,0:T(8,128)(2,1)S(1)}, bf16[64,32,128]{2,1,0:T(8,128)(2,1)S(1)}) custom-call(bf16[66,32,128]{2,1,0:T(8,128)(2,1)S(1)} %copy-done.1, f32[64,8,128]{2,1,0:T(8,128)S(1)} %copy-done, bf16[64,32,128]{2,1,0:T(8,128)(2,1)S(1)} %bitcast.40, ...), custom_call_target="tpu_custom_call" | custom-call | flops 3000000000 | bytes 4000000 | tf_op jit(solution)/shard_map/pallas_call | solution.py:173
  46.3 9.9 %collective-permute-done.4.refs_0_ = bf16[66,32,128]{2,1,0:T(8,128)(2,1)S(1)} collective-permute-done((bf16[66,32,128]{2,1,0:T(8,128)(2,1)}, bf16[66,32,128]{2,1,0:T(8,128)(2,1)S(1)}, u32[]{:S(2)}, u32[]{:S(2)}) %collective-permute-start.4) | collective-permute-done | bytes 540704 | tf_op jit(solution)/shard_map/ppermute | solution.py:18
  56.1 1.3 %collective-permute-done.5.refs_0_ = bf16[66,32,128]{2,1,0:T(8,128)(2,1)} collective-permute-done((bf16[66,32,128]{2,1,0:T(8,128)(2,1)}, bf16[66,32,128]{2,1,0:T(8,128)(2,1)}, u32[]{:S(2)}, u32[]{:S(2)}) %collective-permute-start.5) | collective-permute-done | bytes 540704 | tf_op jit(solution)/shard_map/ppermute | solution.py:18
  57.5 1.0 copy-done.4
  58.5 3.7 %shard_map.114 = (f32[96,64]{1,0:T(8,128)S(1)}, bf16[8,192,1024]{2,1,0:T(8,128)(2,1)S(1)}) custom-call(bf16[66,32,128]{2,1,0:T(8,128)(2,1)} %collective-permute-done.5.refs_0_, f32[64,8,128]{2,1,0:T(8,128)S(1)} %copy-done, bf16[64,32,128]{2,1,0:T(8,128)(2,1)S(1)} %bitcast.41, bf16[64,32,128]{2,1,0:T(8,128)(2,1)S(1)} %copy-done.4), custom_call_target="tpu_custom_call" | custom-call | flops 3000000000 | bytes 4000000 | tf_op jit(solution)/shard_map/pallas_call | solution.py:173
  62.2 3.7 %shard_map.115 = (f32[96,64]{1,0:T(8,128)S(1)}, bf16[8,192,1024]{2,1,0:T(8,128)(2,1)S(1)}) custom-call(bf16[66,32,128]{2,1,0:T(8,128)(2,1)} %collective-permute-done.6.refs_0_, f32[64,8,128]{2,1,0:T(8,128)S(1)} %copy-done, bf16[64,32,128]{2,1,0:T(8,128)(2,1)S(1)} %bitcast.42, bf16[64,32,128]{2,1,0:T(8,128)(2,1)S(1)} %copy-done.5), custom_call_target="tpu_custom_call" | custom-call | flops 3000000000 | bytes 4000000 | tf_op jit(solution)/shard_map/pallas_call | solution.py:173
  65.9 2.7 %shard_map.113 = (f32[96,64]{1,0:T(8,128)S(1)}, bf16[8,192,1024]{2,1,0:T(8,128)(2,1)S(1)}) custom-call(bf16[66,32,128]{2,1,0:T(8,128)(2,1)S(1)} %collective-permute-done.4.refs_0_, f32[64,8,128]{2,1,0:T(8,128)S(1)} %copy-done, bf16[64,32,128]{2,1,0:T(8,128)(2,1)S(1)} %bitcast.43, bf16[64,32,128]{2,1,0:T(8,128)(2,1)S(1)} %copy-done.5), custom_call_target="tpu_custom_call" | custom-call | flops 3000000000 | bytes 4000000 | tf_op jit(solution)/shard_map/pallas_call | solution.py:173
  68.6 4.4 %shard_map.116 = f32[8,48,128]{2,1,0:T(8,128)S(1)} custom-call(f32[96,64]{1,0:T(8,128)S(1)} %get-tuple-element.44.refs_0_, f32[96,64]{1,0:T(8,128)S(1)} %get-tuple-element.46.refs_1_, f32[96,64]{1,0:T(8,128)S(1)} %get-tuple-element.50.refs_2_, f32[96,64]{1,0:T(8,128)S(1)} %get-tuple-element.51.refs_3_, bf16[8,192,1024]{2,1,0:T(8,128)(2,1)S(1)} %get-tuple-element.52.refs_4_, ...), custom_call_target="tpu_custom_call" | custom-call | flops 3000000000 | bytes 14000000 | tf_op jit(solution)/shard_map/pallas_call | solution.py:217
  73.0 21.8 %all_to_all.15 = f32[8,48,128]{2,1,0:T(8,128)S(1)} all-to-all(f32[8,48,128]{2,1,0:T(8,128)S(1)} %shard_map.116), channel_id=1, replica_groups=mesh['y'=8,'zl'=4,'x'=4,'zh'=2,'c'=2] {'y'}, dimensions={0} | all-to-all | bytes 393216 | tf_op jit(solution)/shard_map/all_to_all | solution.py:252
  94.8 12.8 %all_to_all.16 = f32[16,12,128]{2,1,0:T(8,128)S(1)} all-to-all(f32[16,12,128]{2,1,0:T(8,128)S(1)} %bitcast.48), channel_id=1, replica_groups=mesh['y'=8,'zl'=4,'x'=4,'zh'=2,'c'=2] {'x','zl'}, dimensions={0} | all-to-all | bytes 196608 | tf_op jit(solution)/shard_map/all_to_all | solution.py:254
  107.7 0.7 broadcast_in_dim.17
  108.3 3.4 %all-to-all-start.2 = ((f32[8,48,128]{2,1,0:T(8,128)}), f32[8,48,128]{2,1,0:T(8,128)S(1)}, u32[]{:S(2)}, u32[]{:S(2)}) async-start(f32[8,48,128]{2,1,0:T(8,128)} %broadcast_in_dim.17), calls=%async_computation.2 | async-start | bytes 393216 | tf_op jit(solution)/shard_map/all_to_all | solution.py:256
  111.7 1.0 copy.51
  112.7 1.0 copy.52
  113.7 7.7 %all-to-all-done.2 = f32[8,48,128]{2,1,0:T(8,128)S(1)} async-done(((f32[8,48,128]{2,1,0:T(8,128)}), f32[8,48,128]{2,1,0:T(8,128)S(1)}, u32[]{:S(2)}, u32[]{:S(2)}) %all-to-all-start.2) | async-done | bytes 196640 | tf_op jit(solution)/shard_map/all_to_all | solution.py:256
  (30 shorter events, 2.3 us)
Async XLA Ops:
  5.1 18.9 %collective-permute-start = (bf16[40,128]{1,0:T(8,128)(2,1)}, bf16[40,128]{1,0:T(8,128)(2,1)S(1)}, u32[]{:S(2)}, u32[]{:S(2)}) collective-permute-start(bf16[40,128]{1,0:T(8,128)(2,1)} %get-tuple-element.35), channel_id=1, source_target_pairs={{0,16},{16,32},{32,48},{48,64},{64,80},{80,96},{96,112},{112,128},... | collective-permute-start | bytes 30728 | tf_op jit(solution)/shard_map/ppermute | solution.py:235
  9.4 14.7 %collective-permute-start.1 = (bf16[40,128]{1,0:T(8,128)(2,1)}, bf16[40,128]{1,0:T(8,128)(2,1)S(1)}, u32[]{:S(2)}, u32[]{:S(2)}) collective-permute-start(bf16[40,128]{1,0:T(8,128)(2,1)} %get-tuple-element.36), channel_id=1, source_target_pairs={{16,0},{32,16},{48,32},{64,48},{80,64},{96,80},{112,96},{128,112},... | collective-permute-start | bytes 30728 | tf_op jit(solution)/shard_map/ppermute | solution.py:236
  12.0 25.6 %collective-permute-start.2 = (bf16[64,32,128]{2,1,0:T(8,128)(2,1)S(1)}, bf16[64,32,128]{2,1,0:T(8,128)(2,1)S(1)}, u32[]{:S(2)}, u32[]{:S(2)}) collective-permute-start(bf16[64,32,128]{2,1,0:T(8,128)(2,1)S(1)} %bitcast.38), channel_id=1, source_target_pairs={{0,2},{2,0},{1,3},{3,1},{4,6},{6,4},{5,7},{7,5},{8,10},{10,8},{9,1... | collective-permute-start | bytes 1572872 | tf_op jit(solution)/shard_map/ppermute | solution.py:18
  24.0 11.7 %copy-start.6 = (bf16[40,128]{1,0:T(8,128)(2,1)}, bf16[40,128]{1,0:T(8,128)(2,1)S(1)}, u32[]{:S(2)}) copy-start(bf16[40,128]{1,0:T(8,128)(2,1)S(1)} %collective-permute-done.left_ref) | copy-start | bytes 30724
  24.0 11.7 %copy-start.7 = (bf16[40,128]{1,0:T(8,128)(2,1)}, bf16[40,128]{1,0:T(8,128)(2,1)S(1)}, u32[]{:S(2)}) copy-start(bf16[40,128]{1,0:T(8,128)(2,1)S(1)} %collective-permute-done.1.right_ref) | copy-start | bytes 30724
  24.0 15.7 %collective-permute-start.3 = (bf16[64,32,128]{2,1,0:T(8,128)(2,1)S(1)}, bf16[64,32,128]{2,1,0:T(8,128)(2,1)S(1)}, u32[]{:S(2)}, u32[]{:S(2)}) collective-permute-start(bf16[64,32,128]{2,1,0:T(8,128)(2,1)S(1)} %bitcast.39), channel_id=1, source_target_pairs={{0,1},{1,0},{2,3},{3,2},{4,5},{5,4},{6,7},{7,6},{8,9},{9,8},{10,11... | collective-permute-start | bytes 1572872 | tf_op jit(solution)/shard_map/ppermute | solution.py:18
  26.6 29.6 %collective-permute-start.4 = (bf16[66,32,128]{2,1,0:T(8,128)(2,1)}, bf16[66,32,128]{2,1,0:T(8,128)(2,1)S(1)}, u32[]{:S(2)}, u32[]{:S(2)}) collective-permute-start(bf16[66,32,128]{2,1,0:T(8,128)(2,1)} %maximum_dynamic-update-slice_fusion.refs_0_), channel_id=1, source_target_pairs={{0,12},{4,0},{8,4},{12,8},{1,13},{5,1},{9,5},{13,9},{2,14},{6,2},{... | collective-permute-start | bytes 1622024 | tf_op jit(solution)/shard_map/ppermute | solution.py:18
  29.3 28.2 %collective-permute-start.5 = (bf16[66,32,128]{2,1,0:T(8,128)(2,1)}, bf16[66,32,128]{2,1,0:T(8,128)(2,1)}, u32[]{:S(2)}, u32[]{:S(2)}) collective-permute-start(bf16[66,32,128]{2,1,0:T(8,128)(2,1)} %maximum_dynamic-update-slice_fusion.refs_0_), channel_id=1, source_target_pairs={{0,4},{4,8},{8,12},{12,0},{1,5},{5,9},{9,13},{13,1},{2,6},{6,10},{... | collective-permute-start | bytes 1622024 | tf_op jit(solution)/shard_map/ppermute | solution.py:18
  33.6 28.6 %collective-permute-start.6 = (bf16[66,32,128]{2,1,0:T(8,128)(2,1)}, bf16[66,32,128]{2,1,0:T(8,128)(2,1)}, u32[]{:S(2)}, u32[]{:S(2)}) collective-permute-start(bf16[66,32,128]{2,1,0:T(8,128)(2,1)} %maximum_dynamic-update-slice_fusion.refs_0_), channel_id=1, source_target_pairs={{0,8},{4,12},{8,0},{12,4},{1,9},{5,13},{9,1},{13,5},{2,10},{6,14},... | collective-permute-start | bytes 1622024 | tf_op jit(solution)/shard_map/ppermute | solution.py:18
  37.7 30.9 %collective-permute-start.7 = (bf16[64,32,128]{2,1,0:T(8,128)(2,1)S(1)}, bf16[64,32,128]{2,1,0:T(8,128)(2,1)S(1)}, u32[]{:S(2)}, u32[]{:S(2)}) collective-permute-start(bf16[64,32,128]{2,1,0:T(8,128)(2,1)S(1)} %collective-permute-done.2.refs_8_), channel_id=1, source_target_pairs={{0,1},{1,0},{2,3},{3,2},{4,5},{5,4},{6,7},{7,6},{8,9},{9,8},{10,11... | collective-permute-start | bytes 1572872 | tf_op jit(solution)/shard_map/ppermute | solution.py:18
  39.8 0.8 copy-start.2
  40.6 0.9 copy-start
  41.5 1.0 copy-start.1
  42.6 1.0 copy-start.3
  57.5 1.0 copy-start.4
  58.5 3.7 %copy-start.5 = (bf16[64,32,128]{2,1,0:T(8,128)(2,1)S(1)}, bf16[64,32,128]{2,1,0:T(8,128)(2,1)}, u32[]{:S(2)}) copy-start(bf16[64,32,128]{2,1,0:T(8,128)(2,1)} %copy-done.2) | copy-start | bytes 1572868
  108.3 13.1 %all-to-all-start.2 = ((f32[8,48,128]{2,1,0:T(8,128)}), f32[8,48,128]{2,1,0:T(8,128)S(1)}, u32[]{:S(2)}, u32[]{:S(2)}) async-start(f32[8,48,128]{2,1,0:T(8,128)} %broadcast_in_dim.17), calls=%async_computation.2 | async-start | bytes 393216 | tf_op jit(solution)/shard_map/all_to_all | solution.py:256

commit v7 on v3

--- a/solution.py
+++ b/solution.py
@@ -18,21 +18,23 @@
     return lax.ppermute(value, axis, [(i, (i + step) % n) for i in range(n)])
 
 
-def select_table(material, tables_ref, which):
+def select_table(material, values):
     value = jnp.zeros(material.shape, F32)
-    for level in range(tables_ref.shape[1]):
-        value = jnp.where(material == level, tables_ref[which, level], value)
+    for level, entry in enumerate(values):
+        value = jnp.where(material == level, entry, value)
     return value
 
 
-def edges_kernel(u_ref, mat_ref, tables_ref, first_ref, last_ref, ky):
-    ky[...] = select_table(mat_ref[...], tables_ref, 2)
+def edges_kernel(u_ref, mat_ref, first_ref, last_ref, sent_ref, mat):
+    mat[...] = mat_ref[...].astype(F32)
+    sent_ref[0:R] = u_ref[...]
+    sent_ref[R : R + 2] = jnp.zeros((2, M, C), BF16)
     pair = lax.broadcasted_iota(jnp.int32, (8, C), 1) // 2
     firsts, lasts = [], []
     for m in range(0, M + 8, 8):
         first = last = jnp.zeros((8, C), F32)
         for r in range(R):
-            v = u_ref[r, m : m + 8, :].astype(F32) if m < M else jnp.broadcast_to(ky[r : r + 1, :], (8, C))
+            v = u_ref[r, m : m + 8, :].astype(F32) if m < M else jnp.broadcast_to(mat[r : r + 1, :], (8, C))
             first = jnp.where(pair == r, pltpu.roll(v, 2 * r, 1), first)
             last = jnp.where(pair == r, pltpu.roll(v, (2 * r + 2) % C, 1), last)
         firsts.append(first)
@@ -41,27 +43,33 @@
     last_ref[...] = jnp.concatenate(lasts, axis=0).astype(BF16)
 
 
-def edges(u, material, tables):
+def edges(u, material):
     return pl.pallas_call(
         edges_kernel,
-        out_shape=[jax.ShapeDtypeStruct((M + 8, C), BF16)] * 2,
-        in_specs=[VM, VM, SM],
-        out_specs=[VM] * 2,
+        out_shape=[jax.ShapeDtypeStruct((M + 8, C), BF16)] * 2 + [jax.ShapeDtypeStruct((R + 2, M, C), BF16)],
+        in_specs=[VM, VM],
+        out_specs=[VM] * 3,
         scratch_shapes=[pltpu.VMEM((R, C), F32)],
         cost_estimate=pl.CostEstimate(flops=10**6, bytes_accessed=10**6, transcendentals=0),
-    )(u, material, tables)
-
-
-def fields_kernel(mat_ref, left_ref, right_ref, tables_ref, f_ref, kx, ky, rho, dd):
+    )(u, material)
+
+
+def fields_kernel(mat_ref, left_ref, right_ref, rho_ref, mx_ref, my_ref, dd_ref, f_ref, kx, ky, rho, dd):
     material = mat_ref[...]
+    count = rho_ref.shape[0]
+    densities, bends = ([ref[i] for i in range(count)] for ref in (rho_ref, dd_ref))
+    mx, my = ([ref[:, i : i + 1].astype(F32) for i in range(count)] for ref in (mx_ref, my_ref))
     kx[...] = jnp.zeros(kx.shape, F32)
-    kx[8 : 8 + R, :] = select_table(material, tables_ref, 1)
-    ky[...] = select_table(material, tables_ref, 2)
-    rho[...] = select_table(material, tables_ref, 0)
-    dd[...] = select_table(material, tables_ref, 3)
+    kx[8 : 8 + R, :] = select_table(material, mx)
+    ky[...] = select_table(material, my)
+    rho[...] = select_table(material, densities)
+    dd[...] = select_table(material, bends)
     lane = lax.broadcasted_iota(jnp.int32, (1, C), 1)
-    left = left_ref[M : M + 8, :].astype(F32)
-    right = right_ref[M : M + 8, :].astype(F32)
+    space = lax.axis_index("y") * 4 + lax.axis_index("zl")
+    left = select_table(left_ref[M : M + 8, :].astype(F32), my)
+    left = jnp.where(space > 0, left, 0.0)
+    right = select_table(right_ref[M : M + 8, :].astype(F32), my)
+    right = jnp.where(space < 31, right, 0.0)
 
     for r in range(R):
         k = ky[r : r + 1, :]
@@ -80,22 +88,22 @@
         f_ref[r] = jnp.concatenate(rows, axis=0)
 
 
-def fields(material, left, right, tables):
+def fields(material, left, right, density, memb_x, memb_y, bend_table):
     return pl.pallas_call(
         fields_kernel,
         out_shape=jax.ShapeDtypeStruct((R, 8, C), F32),
-        in_specs=[VM, VM, VM, SM],
+        in_specs=[VM, VM, VM, SM, VM, VM, SM],
         out_specs=VM,
         scratch_shapes=[pltpu.VMEM((R + 16, C), F32)] + [pltpu.VMEM((R, C), F32)] * 3,
         cost_estimate=pl.CostEstimate(flops=10**6, bytes_accessed=10**6, transcendentals=0),
-    )(material, left, right, tables)
+    )(material, left, right, density, memb_x[None], memb_y[None], bend_table)
 
 
 PIECE = 3 * M // 8
 ROWS = 8
 
 
-def panel_kernel(d, u_ref, halo_ref, f_ref, *rest):
+def panel_kernel(d, u_ref, f_ref, *rest):
     with_images = d == 0
     olds, rest = rest[:4], rest[4 if d == 0 else 5 :]
     if with_images:
@@ -108,8 +116,8 @@
     s1[0] = zero
     s1[R + 1] = zero
     lane = lax.broadcasted_iota(jnp.int32, (1, C), 1)
-    left = halo_ref[0].astype(F32)[0:M]
-    right = halo_ref[1].astype(F32)[0:M]
+    left = u_ref[R].astype(F32)
+    right = u_ref[R + 1].astype(F32)
     first = jnp.where(lane % 2 == 0, right, left)
     right = pltpu.roll(right, C - 2, 1)
     second = [jnp.where((lane // 2) % 2 == p, left, right) for p in (0, 1)]
@@ -170,16 +178,16 @@
                 out_ref[i, PIECE * k : PIECE * k + PIECE] = v[PIECE * i : PIECE * i + PIECE]
 
 
-def panel(d, u, halo, f, olds, parts):
+def panel(d, u, f, olds, parts):
     outs = [jax.ShapeDtypeStruct((8, 4 * PIECE, 4 * M), F32)]
     outs += [jax.ShapeDtypeStruct((R, M, C), BF16)] * (2 if d == 0 else 0)
-    operands = [u, halo, f, *olds] + ([] if d == 0 else [parts])
+    operands = [u, f, *olds] + ([] if d == 0 else [parts])
     return pl.pallas_call(
         lambda *refs: panel_kernel(d, *refs),
         out_shape=outs,
-        in_specs=[VM] * 7 + ([] if d == 0 else [pl.BlockSpec(memory_space=pl.ANY)]),
+        in_specs=[VM] * 6 + ([] if d == 0 else [pl.BlockSpec(memory_space=pl.ANY)]),
         out_specs=[VM] * len(outs),
-        input_output_aliases={} if d == 0 else {7: 0},
+        input_output_aliases={} if d == 0 else {6: 0},
         scratch_shapes=[
             pltpu.VMEM((R + 4, M, C), F32),
             pltpu.VMEM((R + 2, M, C), F32),
@@ -194,28 +202,24 @@
 
 
 def local(old_modes, new_modes, material, density, memb_x, memb_y, bend_table):
-    tables = jnp.stack([density, memb_x.astype(F32), memb_y.astype(F32), bend_table])
+    first, last, sent = edges(new_modes.transpose(1, 0, 2), material)
+    first, last, old_modes = lax.optimization_barrier((first, last, old_modes))
     old = old_modes.transpose(1, 0, 2)
-    new = new_modes.transpose(1, 0, 2)
     other = shifted(old, "zh", 1)
-    panels = [new] + [shifted(new, "x", -d) for d in (1, 2, 3)]
-    first, last = edges(new, material, tables)
+    old_core = shifted(old, "c", 1)
     n = 32
     left = lax.ppermute(last, SPACE, [(i, i + 1) for i in range(n - 1)])
     right = lax.ppermute(first, SPACE, [(i + 1, i) for i in range(n - 1)])
-    halo = jnp.stack([left, right])
-    halos = lax.all_to_all(jnp.broadcast_to(halo[None], (4, *halo.shape)), "x", 0, 0)
-    x = lax.axis_index("x")
-    beside = [halo] + [lax.dynamic_index_in_dim(halos, lax.rem(x + d, 4), 0, keepdims=False) for d in (1, 2, 3)]
-    other, left, right, beside[1:], panels[1], panels[3] = lax.optimization_barrier(
-        (other, left, right, beside[1:], panels[1], panels[3])
-    )
-    f = fields(material, left, right, tables)
-    f, panels[2] = lax.optimization_barrier((f, panels[2]))
-    olds = (old, shifted(old, "c", 1), other, shifted(other, "c", 1))
-    parts, mass, stiff = panel(0, new, halo, f, olds, None)
+    own = lax.dynamic_update_slice(sent, jnp.stack([left[:M], right[:M]]), (R, 0, 0))
+    panels = [own] + [shifted(own, "x", -d) for d in (1, 2, 3)]
+    f = fields(material, left, right, density, memb_x, memb_y, bend_table)
+    f, other = lax.optimization_barrier((f, other))
+    other_core = shifted(other, "c", 1)
+    other_core, panels[1:] = lax.optimization_barrier((other_core, panels[1:]))
+    olds = (old, old_core, other, other_core)
+    parts, mass, stiff = panel(0, own, f, olds, None)
     for d in (1, 3, 2):
-        (parts,) = panel(d, panels[d], beside[d], f, olds, parts)
+        (parts,) = panel(d, panels[d], f, olds, parts)
     parts = jnp.sum(lax.all_to_all(parts, "y", 0, 0), axis=0).reshape(4, 1, PIECE, 4 * M)
     parts = jnp.broadcast_to(parts, (4, 4, PIECE, 4 * M)).reshape(16, PIECE, 4 * M)
     parts = lax.all_to_all(parts, ("x", "zl"), 0, 0).reshape(4, 4, PIECE, 4 * M)

time: 127 us -> 114 us (0.90)
  waiting for transfers between devices: 28.8 us -> 23.2 us
  starting transfers between devices: 37.4 us -> 32 us
  Pallas kernels: 16.8 us -> 15.1 us
  local copies, waits for them, and re-layouts: 9.1 us -> 7.7 us
  blocking collectives: 31.9 us -> 33.2 us
    ppermute x1, waiting for transfers between devices: 14.3 us -> 0.01 us  [local(): left = lax.ppermute(last, SPACE, [(i, i + 1) for i in range(n - 1)])]
    ppermute x6, waiting for transfers between devices: 5.6 us -> 15.5 us  [shifted(): return lax.ppermute(value, axis, [(i, (i + step) % n) for i in range(n)])]
    all_to_all x1, blocking collectives: 16.9 us -> 22.4 us  [local(): lax.all_to_all(parts, 'y', 0, 0)]
    all_to_all x1 -> x0, starting transfers between devices: 4.96 us -> none  [local(): lax.all_to_all(jnp.broadcast_to(halo[None], (4, *halo.shape)), 'x', 0, 0)]
    all_to_all x1, blocking collectives: 15 us -> 10.9 us  [local(): parts = lax.all_to_all(parts, ('x', 'zl'), 0, 0).reshape(4, 4, PIECE, 4 * M)]
    pallas_call x4, Pallas kernels: 12.8 us -> 10.7 us  [panel(): pl.pallas_call(lambda *refs: panel_kernel(d, *refs), out_shape=outs, in_s...]
    ppermute x6, starting transfers between devices: 24.4 us -> 23 us  [shifted(): return lax.ppermute(value, axis, [(i, (i + step) % n) for i in range(n)])]
    ppermute x1, waiting for transfers between devices: 1.32 us -> 0.01 us  [local(): right = lax.ppermute(first, SPACE, [(i + 1, i) for i in range(n - 1)])]
  transfers between devices with their start and end apart: 10 -> 9, of which waited for: 4 -> 5; matrix products, arithmetic and copies ran while one was open for 3% -> 2% of each run, Pallas kernels for 3% -> 2%
where the time goes in v7:
time: 114 us; the launch traced here: 112 us
  blocking collectives  33.2 us (29%)
  starting transfers between devices  32 us (28%)
  waiting for transfers between devices  23.2 us (20%)
  Pallas kernels  15.1 us (13%)
  local copies, waits for them, and re-layouts  7.7 us (7%)
    ppermute x6, starting transfers between devices, shifted(): return lax.ppermute(value, axis, [(i, (i + step) % n) for i in range(n)])  23 us
    all_to_all x1, blocking collectives, local(): lax.all_to_all(parts, 'y', 0, 0)  22.4 us
    ppermute x6, waiting for transfers between devices, shifted(): return lax.ppermute(value, axis, [(i, (i + step) % n) for i in range(n)])  15.5 us
    all_to_all x1, blocking collectives, local(): parts = lax.all_to_all(parts, ('x', 'zl'), 0, 0).reshape(4, 4, PIECE, 4 * M)  10.9 us
    pallas_call x4, Pallas kernels, panel(): pl.pallas_call(lambda *refs: panel_kernel(d, *refs), out_shape=outs, in_s...  10.7 us
    all_to_all x1, waiting for transfers between devices, local(): lax.all_to_all(jnp.broadcast_to(parts, (8, 4 * PIECE, 4 * M)), 'y', 0, 0)  7.63 us
    unnamed x21, local copies, waits for them, and re-layouts  5.76 us
    ppermute x1, starting transfers between devices, local(): left = lax.ppermute(last, SPACE, [(i, i + 1) for i in range(n - 1)])  4.4 us
  transfers between devices with their start and end apart: 9, of which 5 were waited for; matrix products, arithmetic and copies ran while one was open for 2% of the time, Pallas kernels for 2%

profile of v7, /device:TPU:6, one launch (start us, length us, event | category | flops | bytes accessed | tf_op | source)
XLA Modules:
  0.0 112.2 jit_solution(10370935657153023246)
XLA Ops:
  0.6 2.2 %copy.63 = bf16[32,64,128]{2,0,1:T(8,128)(2,1)} copy(bf16[32,64,128]{2,1,0:T(8,128)(2,1)} %param.8) | data formatting | bytes 1048576 | tf_op args[1]
  2.8 2.3 %shard_map.110 = (bf16[40,128]{1,0:T(8,128)(2,1)}, bf16[40,128]{1,0:T(8,128)(2,1)}, bf16[66,32,128]{2,1,0:T(8,128)(2,1)}) custom-call(bf16[64,32,128]{2,1,0:T(8,128)(2,1)} %bitcast.40, s32[64,128]{1,0:T(8,128)} %mat_ref.3), custom_call_target="tpu_custom_call" | custom-call | flops 1000000 | bytes 1000000 | tf_op jit(solution)/shard_map/pallas_call | solution.py:47
  5.1 4.4 %collective-permute-start = (bf16[40,128]{1,0:T(8,128)(2,1)}, bf16[40,128]{1,0:T(8,128)(2,1)S(1)}, u32[]{:S(2)}, u32[]{:S(2)}) collective-permute-start(bf16[40,128]{1,0:T(8,128)(2,1)} %get-tuple-element.22), channel_id=1, source_target_pairs={{0,16},{16,32},{32,48},{48,64},{64,80},{80,96},{96,112},{112,128},... | collective-permute-start | bytes 30728 | tf_op jit(solution)/shard_map/ppermute | solution.py:211
  9.5 1.3 %collective-permute-start.1 = (bf16[40,128]{1,0:T(8,128)(2,1)}, bf16[40,128]{1,0:T(8,128)(2,1)S(1)}, u32[]{:S(2)}, u32[]{:S(2)}) collective-permute-start(bf16[40,128]{1,0:T(8,128)(2,1)} %get-tuple-element.23), channel_id=1, source_target_pairs={{16,0},{32,16},{48,32},{64,48},{80,64},{96,80},{112,96},{128,112},... | collective-permute-start | bytes 30728 | tf_op jit(solution)/shard_map/ppermute | solution.py:212
  10.9 0.3 copy.62
  11.2 10.0 %collective-permute-start.2 = (bf16[64,32,128]{2,1,0:T(8,128)(2,1)S(1)}, bf16[64,32,128]{2,1,0:T(8,128)(2,1)S(1)}, u32[]{:S(2)}, u32[]{:S(2)}) collective-permute-start(bf16[64,32,128]{2,1,0:T(8,128)(2,1)S(1)} %bitcast.32), channel_id=1, source_target_pairs={{0,2},{2,0},{1,3},{3,1},{4,6},{6,4},{5,7},{7,5},{8,10},{10,8},{9,1... | collective-permute-start | bytes 1572872 | tf_op jit(solution)/shard_map/ppermute | solution.py:18
  21.3 0.5 copy-done.7
  21.9 2.4 %collective-permute-start.6 = (bf16[66,32,128]{2,1,0:T(8,128)(2,1)S(1)}, bf16[66,32,128]{2,1,0:T(8,128)(2,1)S(1)}, u32[]{:S(2)}, u32[]{:S(2)}) collective-permute-start(bf16[66,32,128]{2,1,0:T(8,128)(2,1)S(1)} %maximum_dynamic-update-slice_fusion.refs_0_), channel_id=1, source_target_pairs={{0,4},{4,8},{8,12},{12,0},{1,5},{5,9},{9,13},{13,1},{2,6},{6,10},{... | collective-permute-start | bytes 1622024 | tf_op jit(solution)/shard_map/ppermute | solution.py:18
  24.3 4.3 %collective-permute-start.5 = (bf16[66,32,128]{2,1,0:T(8,128)(2,1)S(1)}, bf16[66,32,128]{2,1,0:T(8,128)(2,1)S(1)}, u32[]{:S(2)}, u32[]{:S(2)}) collective-permute-start(bf16[66,32,128]{2,1,0:T(8,128)(2,1)S(1)} %maximum_dynamic-update-slice_fusion.refs_0_), channel_id=1, source_target_pairs={{0,8},{4,12},{8,0},{12,4},{1,9},{5,13},{9,1},{13,5},{2,10},{6,14},... | collective-permute-start | bytes 1622024 | tf_op jit(solution)/shard_map/ppermute | solution.py:18
  28.6 1.9 %collective-permute-start.4 = (bf16[66,32,128]{2,1,0:T(8,128)(2,1)S(1)}, bf16[66,32,128]{2,1,0:T(8,128)(2,1)S(1)}, u32[]{:S(2)}, u32[]{:S(2)}) collective-permute-start(bf16[66,32,128]{2,1,0:T(8,128)(2,1)S(1)} %maximum_dynamic-update-slice_fusion.refs_0_), channel_id=1, source_target_pairs={{0,12},{4,0},{8,4},{12,8},{1,13},{5,1},{9,5},{13,9},{2,14},{6,2},{... | collective-permute-start | bytes 1622024 | tf_op jit(solution)/shard_map/ppermute | solution.py:18
  30.5 2.0 %shard_map.111.refs_1_ = f32[64,8,128]{2,1,0:T(8,128)} custom-call(s32[64,128]{1,0:T(8,128)} %mat_ref.3, bf16[40,128]{1,0:T(8,128)(2,1)} %copy-done.7, bf16[40,128]{1,0:T(8,128)(2,1)} %copy-done.8, f32[12]{0:T(128)} %rho_ref.1, bf16[1,12]{1,0:T(2,128)(2,1)} %bitcast.43, bf16[1,12]{1,0:T(2,128)(2,1)} %bitcast.44, f32[12]{0:T(128)} %dd_ref.1), custom_call_target="tpu_custom_call" | custom-call | flops 1000000 | bytes 1000000 | tf_op jit(solution)/shard_map/pallas_call | solution.py:92
  32.6 0.7 collective-permute-done.2.refs_4_
  33.2 1.9 %collective-permute-start.3 = (bf16[64,32,128]{2,1,0:T(8,128)(2,1)S(1)}, bf16[64,32,128]{2,1,0:T(8,128)(2,1)S(1)}, u32[]{:S(2)}, u32[]{:S(2)}) collective-permute-start(bf16[64,32,128]{2,1,0:T(8,128)(2,1)S(1)} %collective-permute-done.2.refs_4_), channel_id=1, source_target_pairs={{0,1},{1,0},{2,3},{3,2},{4,5},{5,4},{6,7},{7,6},{8,9},{9,8},{10,11... | collective-permute-start | bytes 1572872 | tf_op jit(solution)/shard_map/ppermute | solution.py:18
  35.2 2.4 %collective-permute-start.7 = (bf16[64,32,128]{2,1,0:T(8,128)(2,1)S(1)}, bf16[64,32,128]{2,1,0:T(8,128)(2,1)S(1)}, u32[]{:S(2)}, u32[]{:S(2)}) collective-permute-start(bf16[64,32,128]{2,1,0:T(8,128)(2,1)S(1)} %bitcast.33), channel_id=1, source_target_pairs={{0,1},{1,0},{2,3},{3,2},{4,5},{5,4},{6,7},{7,6},{8,9},{9,8},{10,11... | collective-permute-start | bytes 1572872 | tf_op jit(solution)/shard_map/ppermute | solution.py:18
  37.6 1.4 %collective-permute-done.6.refs_0_ = bf16[66,32,128]{2,1,0:T(8,128)(2,1)S(1)} collective-permute-done((bf16[66,32,128]{2,1,0:T(8,128)(2,1)S(1)}, bf16[66,32,128]{2,1,0:T(8,128)(2,1)S(1)}, u32[]{:S(2)}, u32[]{:S(2)}) %collective-permute-start.6) | collective-permute-done | bytes 540704 | tf_op jit(solution)/shard_map/ppermute | solution.py:18
  39.0 3.9 %collective-permute-done.5.refs_0_ = bf16[66,32,128]{2,1,0:T(8,128)(2,1)S(1)} collective-permute-done((bf16[66,32,128]{2,1,0:T(8,128)(2,1)S(1)}, bf16[66,32,128]{2,1,0:T(8,128)(2,1)S(1)}, u32[]{:S(2)}, u32[]{:S(2)}) %collective-permute-start.5) | collective-permute-done | bytes 540704 | tf_op jit(solution)/shard_map/ppermute | solution.py:18
  42.9 9.5 %collective-permute-done.4.refs_0_ = bf16[66,32,128]{2,1,0:T(8,128)(2,1)S(1)} collective-permute-done((bf16[66,32,128]{2,1,0:T(8,128)(2,1)S(1)}, bf16[66,32,128]{2,1,0:T(8,128)(2,1)S(1)}, u32[]{:S(2)}, u32[]{:S(2)}) %collective-permute-start.4) | collective-permute-done | bytes 540704 | tf_op jit(solution)/shard_map/ppermute | solution.py:18
  52.4 0.9 copy-done
  53.4 2.7 %shard_map.112 = (f32[8,48,128]{2,1,0:T(8,128)S(1)}, bf16[64,32,128]{2,1,0:T(8,128)(2,1)S(1)}, bf16[64,32,128]{2,1,0:T(8,128)(2,1)S(1)}) custom-call(bf16[66,32,128]{2,1,0:T(8,128)(2,1)S(1)} %maximum_dynamic-update-slice_fusion.refs_0_, f32[64,8,128]{2,1,0:T(8,128)S(1)} %copy-done, bf16[64,32,128]{2,1,0:T(8,128)(2,1)S(1)} %bitcast.34, ...), custom_call_target="tpu_custom_call" | custom-call | flops 400000000 | bytes 4000000 | tf_op jit(solution)/shard_map/pallas_call | solution.py:185
  56.1 2.6 %shard_map.113.refs_6_ = f32[8,48,128]{2,1,0:T(8,128)S(1)} custom-call(bf16[66,32,128]{2,1,0:T(8,128)(2,1)S(1)} %collective-permute-done.4.refs_0_, f32[64,8,128]{2,1,0:T(8,128)S(1)} %copy-done, bf16[64,32,128]{2,1,0:T(8,128)(2,1)S(1)} %bitcast.35, bf16[64,32,128]{2,1,0:T(8,128)(2,1)S(1)} %collective-permute-done.7.refs_3_, ...), custom_call_target="tpu_custom_call", output_to_operand_aliasing={{}: (6, {})} | custom-call | flops 400000000 | bytes 4000000 | tf_op jit(solution)/shard_map/pallas_call | solution.py:185
  58.7 2.8 %shard_map.114.refs_6_ = f32[8,48,128]{2,1,0:T(8,128)S(1)} custom-call(bf16[66,32,128]{2,1,0:T(8,128)(2,1)S(1)} %collective-permute-done.6.refs_0_, f32[64,8,128]{2,1,0:T(8,128)S(1)} %copy-done, bf16[64,32,128]{2,1,0:T(8,128)(2,1)S(1)} %bitcast.36, bf16[64,32,128]{2,1,0:T(8,128)(2,1)S(1)} %collective-permute-done.7.refs_3_, ...), custom_call_target="tpu_custom_call", output_to_operand_aliasing={{}: (6, {})} | custom-call | flops 400000000 | bytes 4000000 | tf_op jit(solution)/shard_map/pallas_call | solution.py:185
  61.5 2.6 %shard_map.115 = f32[8,48,128]{2,1,0:T(8,128)S(1)} custom-call(bf16[66,32,128]{2,1,0:T(8,128)(2,1)S(1)} %collective-permute-done.5.refs_0_, f32[64,8,128]{2,1,0:T(8,128)S(1)} %copy-done, bf16[64,32,128]{2,1,0:T(8,128)(2,1)S(1)} %bitcast.37, bf16[64,32,128]{2,1,0:T(8,128)(2,1)S(1)} %collective-permute-done.7.refs_3_, ...), custom_call_target="tpu_custom_call", output_to_operand_aliasing={{}: (6, {})} | custom-call | flops 400000000 | bytes 4000000 | tf_op jit(solution)/shard_map/pallas_call | solution.py:185
  64.2 22.4 %all_to_all.15 = f32[8,48,128]{2,1,0:T(8,128)S(1)} all-to-all(f32[8,48,128]{2,1,0:T(8,128)S(1)} %shard_map.115), channel_id=1, replica_groups=mesh['y'=8,'zl'=4,'x'=4,'zh'=2,'c'=2] {'y'}, dimensions={0} | all-to-all | bytes 393216 | tf_op jit(solution)/shard_map/all_to_all | solution.py:223
  86.6 10.9 %all_to_all.16 = f32[16,12,128]{2,1,0:T(8,128)S(1)} all-to-all(f32[16,12,128]{2,1,0:T(8,128)S(1)} %bitcast.42), channel_id=1, replica_groups=mesh['y'=8,'zl'=4,'x'=4,'zh'=2,'c'=2] {'x','zl'}, dimensions={0} | all-to-all | bytes 196608 | tf_op jit(solution)/shard_map/all_to_all | solution.py:225
  97.5 0.7 broadcast_in_dim.25
  98.2 3.4 %all-to-all-start.2 = ((f32[8,48,128]{2,1,0:T(8,128)}), f32[8,48,128]{2,1,0:T(8,128)S(1)}, u32[]{:S(2)}, u32[]{:S(2)}) async-start(f32[8,48,128]{2,1,0:T(8,128)} %broadcast_in_dim.25), calls=%async_computation.2 | async-start | bytes 393216 | tf_op jit(solution)/shard_map/all_to_all | solution.py:227
  101.6 1.0 copy.54
  102.6 1.0 copy.55
  103.6 7.6 %all-to-all-done.2 = f32[8,48,128]{2,1,0:T(8,128)S(1)} async-done(((f32[8,48,128]{2,1,0:T(8,128)}), f32[8,48,128]{2,1,0:T(8,128)S(1)}, u32[]{:S(2)}, u32[]{:S(2)}) %all-to-all-start.2) | async-done | bytes 196640 | tf_op jit(solution)/shard_map/all_to_all | solution.py:227
  111.3 0.1 copy.53
  111.5 0.1 mul.19
  111.6 0.7 slice_bitcast_fusion
  (29 shorter events, 0.2 us)
Async XLA Ops:
  2.8 8.0 %copy-start.6 = (bf16[32,64,128]{2,1,0:T(8,128)(2,1)S(1)}, bf16[32,64,128]{2,1,0:T(8,128)(2,1)}, u32[]{:S(2)}) copy-start(bf16[32,64,128]{2,1,0:T(8,128)(2,1)} %param.7) | copy-start | bytes 1572868
  5.1 16.7 %copy-start.1 = (bf16[66,32,128]{2,1,0:T(8,128)(2,1)S(1)}, bf16[66,32,128]{2,1,0:T(8,128)(2,1)}, u32[]{:S(2)}) copy-start(bf16[66,32,128]{2,1,0:T(8,128)(2,1)} %get-tuple-element.26) | copy-start | bytes 1622020
  5.1 16.1 %collective-permute-start = (bf16[40,128]{1,0:T(8,128)(2,1)}, bf16[40,128]{1,0:T(8,128)(2,1)S(1)}, u32[]{:S(2)}, u32[]{:S(2)}) collective-permute-start(bf16[40,128]{1,0:T(8,128)(2,1)} %get-tuple-element.22), channel_id=1, source_target_pairs={{0,16},{16,32},{32,48},{48,64},{64,80},{80,96},{96,112},{112,128},... | collective-permute-start | bytes 30728 | tf_op jit(solution)/shard_map/ppermute | solution.py:211
  9.5 11.7 %collective-permute-start.1 = (bf16[40,128]{1,0:T(8,128)(2,1)}, bf16[40,128]{1,0:T(8,128)(2,1)S(1)}, u32[]{:S(2)}, u32[]{:S(2)}) collective-permute-start(bf16[40,128]{1,0:T(8,128)(2,1)} %get-tuple-element.23), channel_id=1, source_target_pairs={{16,0},{32,16},{48,32},{64,48},{80,64},{96,80},{112,96},{128,112},... | collective-permute-start | bytes 30728 | tf_op jit(solution)/shard_map/ppermute | solution.py:212
  11.2 22.0 %collective-permute-start.2 = (bf16[64,32,128]{2,1,0:T(8,128)(2,1)S(1)}, bf16[64,32,128]{2,1,0:T(8,128)(2,1)S(1)}, u32[]{:S(2)}, u32[]{:S(2)}) collective-permute-start(bf16[64,32,128]{2,1,0:T(8,128)(2,1)S(1)} %bitcast.32), channel_id=1, source_target_pairs={{0,2},{2,0},{1,3},{3,1},{4,6},{6,4},{5,7},{7,5},{8,10},{10,8},{9,1... | collective-permute-start | bytes 1572872 | tf_op jit(solution)/shard_map/ppermute | solution.py:18
  21.2 0.6 copy-start.7
  21.3 0.6 copy-start.8
  21.9 17.1 %collective-permute-start.6 = (bf16[66,32,128]{2,1,0:T(8,128)(2,1)S(1)}, bf16[66,32,128]{2,1,0:T(8,128)(2,1)S(1)}, u32[]{:S(2)}, u32[]{:S(2)}) collective-permute-start(bf16[66,32,128]{2,1,0:T(8,128)(2,1)S(1)} %maximum_dynamic-update-slice_fusion.refs_0_), channel_id=1, source_target_pairs={{0,4},{4,8},{8,12},{12,0},{1,5},{5,9},{9,13},{13,1},{2,6},{6,10},{... | collective-permute-start | bytes 1622024 | tf_op jit(solution)/shard_map/ppermute | solution.py:18
  24.3 18.7 %collective-permute-start.5 = (bf16[66,32,128]{2,1,0:T(8,128)(2,1)S(1)}, bf16[66,32,128]{2,1,0:T(8,128)(2,1)S(1)}, u32[]{:S(2)}, u32[]{:S(2)}) collective-permute-start(bf16[66,32,128]{2,1,0:T(8,128)(2,1)S(1)} %maximum_dynamic-update-slice_fusion.refs_0_), channel_id=1, source_target_pairs={{0,8},{4,12},{8,0},{12,4},{1,9},{5,13},{9,1},{13,5},{2,10},{6,14},... | collective-permute-start | bytes 1622024 | tf_op jit(solution)/shard_map/ppermute | solution.py:18
  28.6 23.8 %collective-permute-start.4 = (bf16[66,32,128]{2,1,0:T(8,128)(2,1)S(1)}, bf16[66,32,128]{2,1,0:T(8,128)(2,1)S(1)}, u32[]{:S(2)}, u32[]{:S(2)}) collective-permute-start(bf16[66,32,128]{2,1,0:T(8,128)(2,1)S(1)} %maximum_dynamic-update-slice_fusion.refs_0_), channel_id=1, source_target_pairs={{0,12},{4,0},{8,4},{12,8},{1,13},{5,1},{9,5},{13,9},{2,14},{6,2},{... | collective-permute-start | bytes 1622024 | tf_op jit(solution)/shard_map/ppermute | solution.py:18
  33.2 19.2 %collective-permute-start.3 = (bf16[64,32,128]{2,1,0:T(8,128)(2,1)S(1)}, bf16[64,32,128]{2,1,0:T(8,128)(2,1)S(1)}, u32[]{:S(2)}, u32[]{:S(2)}) collective-permute-start(bf16[64,32,128]{2,1,0:T(8,128)(2,1)S(1)} %collective-permute-done.2.refs_4_), channel_id=1, source_target_pairs={{0,1},{1,0},{2,3},{3,2},{4,5},{5,4},{6,7},{7,6},{8,9},{9,8},{10,11... | collective-permute-start | bytes 1572872 | tf_op jit(solution)/shard_map/ppermute | solution.py:18
  35.2 17.3 %collective-permute-start.7 = (bf16[64,32,128]{2,1,0:T(8,128)(2,1)S(1)}, bf16[64,32,128]{2,1,0:T(8,128)(2,1)S(1)}, u32[]{:S(2)}, u32[]{:S(2)}) collective-permute-start(bf16[64,32,128]{2,1,0:T(8,128)(2,1)S(1)} %bitcast.33), channel_id=1, source_target_pairs={{0,1},{1,0},{2,3},{3,2},{4,5},{5,4},{6,7},{7,6},{8,9},{9,8},{10,11... | collective-permute-start | bytes 1572872 | tf_op jit(solution)/shard_map/ppermute | solution.py:18
  52.4 1.0 copy-start
  56.1 2.6 %copy-start.2 = (bf16[64,32,128]{2,1,0:T(8,128)(2,1)}, bf16[64,32,128]{2,1,0:T(8,128)(2,1)S(1)}, u32[]{:S(2)}) copy-start(bf16[64,32,128]{2,1,0:T(8,128)(2,1)S(1)} %get-tuple-element.34) | copy-start | bytes 1572868
  56.1 2.6 %copy-start.4 = (bf16[64,32,128]{2,1,0:T(8,128)(2,1)}, bf16[64,32,128]{2,1,0:T(8,128)(2,1)S(1)}, u32[]{:S(2)}) copy-start(bf16[64,32,128]{2,1,0:T(8,128)(2,1)S(1)} %get-tuple-element.33) | copy-start | bytes 1572868
  86.6 15.0 %copy-start.5 = (bf16[64,32,128]{2,1,0:T(8,128)(2,1)S(1)}, bf16[64,32,128]{2,1,0:T(8,128)(2,1)}, u32[]{:S(2)}) copy-start(bf16[64,32,128]{2,1,0:T(8,128)(2,1)} %copy-done.4) | copy-start | bytes 1572868
  98.2 13.1 %all-to-all-start.2 = ((f32[8,48,128]{2,1,0:T(8,128)}), f32[8,48,128]{2,1,0:T(8,128)S(1)}, u32[]{:S(2)}, u32[]{:S(2)}) async-start(f32[8,48,128]{2,1,0:T(8,128)} %broadcast_in_dim.25), calls=%async_computation.2 | async-start | bytes 393216 | tf_op jit(solution)/shard_map/all_to_all | solution.py:227
  101.6 1.0 copy-start.3

commit v8 on v7

--- a/solution.py
+++ b/solution.py
@@ -3,6 +3,7 @@
 from jax import lax
 from jax.experimental import pallas as pl
 from jax.experimental.pallas import tpu as pltpu
+from jax.experimental.layout import Layout, with_layout_constraint
 from jax.sharding import Mesh, PartitionSpec as P
 
 SPACE = ("y", "zl")
@@ -104,12 +105,11 @@
 
 
 def panel_kernel(d, u_ref, f_ref, *rest):
-    with_images = d == 0
-    olds, rest = rest[:4], rest[4 if d == 0 else 5 :]
-    if with_images:
-        out_ref, mass_ref, stiff_ref, us, s1, s2, q, img, acc = rest
+    if d == 0:
+        img, mass_ref, stiff_ref, us, s1, s2, q = rest
     else:
-        out_ref, us, s1, s2, q, img, acc = rest
+        olds, own_ref = rest[:4], rest[4]
+        out_ref, us, s1, s2, q, img, acc = rest[5:]
     zero = jnp.zeros((M, C), F32)
     for r in (0, 1, R + 2, R + 3):
         us[r] = zero
@@ -135,9 +135,10 @@
         s2[r] = south2 + north2
         q[r] = f_ref[r, 5:6, :] * north + f_ref[r, 6:7, :] * south
 
-    acc[...] = jnp.zeros(acc.shape, F32)
-
-    def rows(step, _):
+    if d > 0:
+        acc[...] = jnp.zeros(acc.shape, F32)
+
+    def rows(step, slot):
         base = step * ROWS
         for j in range(ROWS):
             r = base + j
@@ -151,25 +152,34 @@
             for i, v in enumerate((mass, membrane, bending)):
                 hi = v.astype(BF16)
                 lo = (v - hi.astype(F32)).astype(BF16)
-                img[step % 2, M * i : M * i + M, C * j : C * j + C] = hi
-                img[step % 2, M * (i + 3) : M * (i + 3) + M, C * j : C * j + C] = lo
-            if with_images:
+                img[slot, M * i : M * i + M, C * j : C * j + C] = hi
+                img[slot, M * (i + 3) : M * (i + 3) + M, C * j : C * j + C] = lo
+            if d == 0:
                 mass_ref[r] = mass.astype(BF16)
                 stiff_ref[r] = (membrane + bending).astype(BF16)
+        if d == 0:
+            return
         wide = [jnp.concatenate([o[base + j] for j in range(ROWS)], axis=1) for o in olds]
-        acc[...] += lax.dot_general(
-            img[step % 2], jnp.concatenate(wide, axis=0), (((1,), (1,)), ((), ())), preferred_element_type=F32
-        )
-        return 0
+        wide = jnp.concatenate(wide, axis=0)
+        dims = (((1,), (1,)), ((), ()))
+        acc[0] += lax.dot_general(img[slot], wide, dims, preferred_element_type=F32)
+        if d == 1:
+            acc[1] += lax.dot_general(own_ref[step], wide, dims, preferred_element_type=F32)
 
     for step in range(R // ROWS):
-        rows(step, 0)
+        rows(step, step if d == 0 else step % 2)
+    if d == 0:
+        return
     zh, c = lax.axis_index("zh"), lax.axis_index("c")
-    v = pltpu.roll(acc[0 : 3 * M] + acc[3 * M : 6 * M], zh * 64, 1)
     lane = lax.broadcasted_iota(jnp.int32, (1, 4 * M), 1)
-    swapped = jnp.where(lane % 64 < 32, pltpu.roll(v, 96, 1), pltpu.roll(v, 32, 1))
-    v = jnp.where(c == 1, swapped, v)
-    chip = lax.rem(lax.axis_index("x") + d, 4)
+    for i, away in enumerate((d, 0) if d == 1 else (d,)):
+        v = pltpu.roll(acc[i, 0 : 3 * M] + acc[i, 3 * M : 6 * M], zh * 64, 1)
+        swapped = jnp.where(lane % 64 < 32, pltpu.roll(v, 96, 1), pltpu.roll(v, 32, 1))
+        v = jnp.where(c == 1, swapped, v)
+        put(out_ref, v, lax.rem(lax.axis_index("x") + away, 4))
+
+
+def put(out_ref, v, chip):
     for k in range(4):
 
         @pl.when(chip == k)
@@ -178,25 +188,37 @@
                 out_ref[i, PIECE * k : PIECE * k + PIECE] = v[PIECE * i : PIECE * i + PIECE]
 
 
-def panel(d, u, f, olds, parts):
-    outs = [jax.ShapeDtypeStruct((8, 4 * PIECE, 4 * M), F32)]
-    outs += [jax.ShapeDtypeStruct((R, M, C), BF16)] * (2 if d == 0 else 0)
-    operands = [u, f, *olds] + ([] if d == 0 else [parts])
+TERMS = (R // ROWS, 6 * M, ROWS * C)
+
+
+def fields_scratch():
+    shapes = ((R + 4, M, C), (R + 2, M, C), (R, M, C), (R, M, C))
+    return [pltpu.VMEM(shape, F32) for shape in shapes]
+
+
+def own_panel(u, f):
+    return pl.pallas_call(
+        lambda *refs: panel_kernel(0, *refs),
+        out_shape=[jax.ShapeDtypeStruct(TERMS, BF16)] + [jax.ShapeDtypeStruct((R, M, C), BF16)] * 2,
+        in_specs=[VM] * 2,
+        out_specs=[VM] * 3,
+        scratch_shapes=fields_scratch(),
+        compiler_params=pltpu.CompilerParams(vmem_limit_bytes=20 * 2**20),
+        cost_estimate=pl.CostEstimate(flops=4 * 10**8, bytes_accessed=4 * 10**6, transcendentals=0),
+    )(u, f)
+
+
+def panel(d, u, f, olds, extra):
+    operands = [u, f, *olds, extra]
     return pl.pallas_call(
         lambda *refs: panel_kernel(d, *refs),
-        out_shape=outs,
-        in_specs=[VM] * 6 + ([] if d == 0 else [pl.BlockSpec(memory_space=pl.ANY)]),
-        out_specs=[VM] * len(outs),
-        input_output_aliases={} if d == 0 else {6: 0},
-        scratch_shapes=[
-            pltpu.VMEM((R + 4, M, C), F32),
-            pltpu.VMEM((R + 2, M, C), F32),
-            pltpu.VMEM((R, M, C), F32),
-            pltpu.VMEM((R, M, C), F32),
-            pltpu.VMEM((2, 6 * M, ROWS * C), BF16),
-            pltpu.VMEM((6 * M, 4 * M), F32),
-        ],
-        compiler_params=pltpu.CompilerParams(vmem_limit_bytes=16 * 2**20),
+        out_shape=jax.ShapeDtypeStruct((8, 4 * PIECE, 4 * M), F32),
+        in_specs=[VM] * 6 + [VM if d == 1 else pl.BlockSpec(memory_space=pl.ANY)],
+        out_specs=VM,
+        input_output_aliases={} if d == 1 else {6: 0},
+        scratch_shapes=fields_scratch()
+        + [pltpu.VMEM((2, 6 * M, ROWS * C), BF16), pltpu.VMEM((2 if d == 1 else 1, 6 * M, 4 * M), F32)],
+        compiler_params=pltpu.CompilerParams(vmem_limit_bytes=20 * 2**20),
         cost_estimate=pl.CostEstimate(flops=4 * 10**8, bytes_accessed=4 * 10**6, transcendentals=0),
     )(*operands)
 
@@ -213,13 +235,16 @@
     own = lax.dynamic_update_slice(sent, jnp.stack([left[:M], right[:M]]), (R, 0, 0))
     panels = [own] + [shifted(own, "x", -d) for d in (1, 2, 3)]
     f = fields(material, left, right, density, memb_x, memb_y, bend_table)
-    f, other = lax.optimization_barrier((f, other))
+    terms, mass, stiff = own_panel(own, f)
+    rowwise = Layout(major_to_minor=(0, 1, 2))
+    mass, stiff = (with_layout_constraint(v.transpose(1, 0, 2), rowwise) for v in (mass, stiff))
+    f, other, terms, mass, stiff = lax.optimization_barrier((f, other, terms, mass, stiff))
     other_core = shifted(other, "c", 1)
     other_core, panels[1:] = lax.optimization_barrier((other_core, panels[1:]))
     olds = (old, old_core, other, other_core)
-    parts, mass, stiff = panel(0, own, f, olds, None)
-    for d in (1, 3, 2):
-        (parts,) = panel(d, panels[d], f, olds, parts)
+    parts = panel(1, panels[1], f, olds, terms)
+    for d in (3, 2):
+        parts = panel(d, panels[d], f, olds, parts)
     parts = jnp.sum(lax.all_to_all(parts, "y", 0, 0), axis=0).reshape(4, 1, PIECE, 4 * M)
     parts = jnp.broadcast_to(parts, (4, 4, PIECE, 4 * M)).reshape(16, PIECE, 4 * M)
     parts = lax.all_to_all(parts, ("x", "zl"), 0, 0).reshape(4, 4, PIECE, 4 * M)
@@ -227,7 +252,7 @@
     parts = lax.all_to_all(jnp.broadcast_to(parts, (8, 4 * PIECE, 4 * M)), "y", 0, 0)
     area = 1.0 / (R * C * n)
     total = parts.reshape(8, 4, PIECE, 4 * M).transpose(0, 2, 1, 3).reshape(3, M, 16 * M) * area
-    return (*[total[i].T for i in range(3)], mass.transpose(1, 0, 2), stiff.transpose(1, 0, 2))
+    return (*[total[i].T for i in range(3)], mass, stiff)
 
 
 def solution(mesh):

time: 114 us -> 112 us (0.982)
  waiting for transfers between devices: 23.2 us -> 9.11 us
  blocking collectives: 33.2 us -> 46.1 us
  starting transfers between devices: 32 us -> 30.8 us
    all_to_all x0 -> x1, blocking collectives: none -> 12.2 us  [local(): lax.all_to_all(jnp.broadcast_to(parts, (8, 4 * PIECE, 4 * M)), 'y', 0, 0)]
    all_to_all x1 -> x0, waiting for transfers between devices: 7.63 us -> none  [local(): lax.all_to_all(jnp.broadcast_to(parts, (8, 4 * PIECE, 4 * M)), 'y', 0, 0)]
    ppermute x6, waiting for transfers between devices: 15.5 us -> 9.1 us  [shifted(): return lax.ppermute(value, axis, [(i, (i + step) % n) for i in range(n)])]
    all_to_all x1, blocking collectives: 10.9 us -> 15.7 us  [local(): parts = lax.all_to_all(parts, ('x', 'zl'), 0, 0).reshape(4, 4, PIECE, 4 * M)]
    all_to_all x1, blocking collectives: 22.4 us -> 18.2 us  [local(): lax.all_to_all(parts, 'y', 0, 0)]
    all_to_all x1 -> x0, starting transfers between devices: 3.39 us -> none  [local(): lax.all_to_all(jnp.broadcast_to(parts, (8, 4 * PIECE, 4 * M)), 'y', 0, 0)]
    ppermute x6, starting transfers between devices: 23 us -> 24.6 us  [shifted(): return lax.ppermute(value, axis, [(i, (i + step) % n) for i in range(n)])]
    unnamed x21 -> x11, local copies, waits for them, and re-layouts: 5.76 us -> 4.19 us
  transfers between devices with their start and end apart: 9 -> 8, of which waited for: 5 -> 2; matrix products, arithmetic and copies ran while one was open for 2% -> 3% of each run, Pallas kernels for 2% -> 4%
where the time goes in v8:
time: 112 us; the launch traced here: 110 us
  blocking collectives  46.1 us (41%)
  starting transfers between devices  30.8 us (28%)
  Pallas kernels  14.9 us (13%)
  waiting for transfers between devices  9.11 us (8%)
  local copies, waits for them, and re-layouts  7.88 us (7%)
    ppermute x6, starting transfers between devices, shifted(): return lax.ppermute(value, axis, [(i, (i + step) % n) for i in range(n)])  24.6 us
    all_to_all x1, blocking collectives, local(): lax.all_to_all(parts, 'y', 0, 0)  18.2 us
    all_to_all x1, blocking collectives, local(): parts = lax.all_to_all(parts, ('x', 'zl'), 0, 0).reshape(4, 4, PIECE, 4 * M)  15.7 us
    all_to_all x1, blocking collectives, local(): lax.all_to_all(jnp.broadcast_to(parts, (8, 4 * PIECE, 4 * M)), 'y', 0, 0)  12.2 us
    ppermute x6, waiting for transfers between devices, shifted(): return lax.ppermute(value, axis, [(i, (i + step) % n) for i in range(n)])  9.1 us
    pallas_call x3, Pallas kernels, panel(): pl.pallas_call(lambda *refs: panel_kernel(d, *refs), out_shape=jax.ShapeD...  8.6 us
    ppermute x1, starting transfers between devices, local(): left = lax.ppermute(last, SPACE, [(i, i + 1) for i in range(n - 1)])  4.9 us
    unnamed x11, local copies, waits for them, and re-layouts  4.19 us
  transfers between devices with their start and end apart: 8, of which 2 were waited for; matrix products, arithmetic and copies ran while one was open for 3% of the time, Pallas kernels for 4%

profile of v8, /device:TPU:6, one launch (start us, length us, event | category | flops | bytes accessed | tf_op | source)
XLA Modules:
  0.0 110.3 jit_solution(10219255826317900600)
XLA Ops:
  0.6 2.2 %copy.64 = bf16[32,64,128]{2,0,1:T(8,128)(2,1)} copy(bf16[32,64,128]{2,1,0:T(8,128)(2,1)} %param.8) | data formatting | bytes 1048576 | tf_op args[1]
  2.8 2.3 %shard_map.110 = (bf16[40,128]{1,0:T(8,128)(2,1)}, bf16[40,128]{1,0:T(8,128)(2,1)}, bf16[66,32,128]{2,1,0:T(8,128)(2,1)}) custom-call(bf16[64,32,128]{2,1,0:T(8,128)(2,1)} %bitcast.39, s32[64,128]{1,0:T(8,128)} %mat_ref.3), custom_call_target="tpu_custom_call" | custom-call | flops 1000000 | bytes 1000000 | tf_op jit(solution)/shard_map/pallas_call | solution.py:48
  5.1 1.3 %collective-permute-start.1 = (bf16[40,128]{1,0:T(8,128)(2,1)}, bf16[40,128]{1,0:T(8,128)(2,1)S(1)}, u32[]{:S(2)}, u32[]{:S(2)}) collective-permute-start(bf16[40,128]{1,0:T(8,128)(2,1)} %get-tuple-element.26), channel_id=1, source_target_pairs={{16,0},{32,16},{48,32},{64,48},{80,64},{96,80},{112,96},{128,112},... | collective-permute-start | bytes 30728 | tf_op jit(solution)/shard_map/ppermute | solution.py:234
  6.4 4.9 %collective-permute-start = (bf16[40,128]{1,0:T(8,128)(2,1)}, bf16[40,128]{1,0:T(8,128)(2,1)S(1)}, u32[]{:S(2)}, u32[]{:S(2)}) collective-permute-start(bf16[40,128]{1,0:T(8,128)(2,1)} %get-tuple-element.25), channel_id=1, source_target_pairs={{0,16},{16,32},{32,48},{48,64},{64,80},{80,96},{96,112},{112,128},... | collective-permute-start | bytes 30728 | tf_op jit(solution)/shard_map/ppermute | solution.py:233
  11.3 1.4 %copy.63 = bf16[32,64,128]{2,0,1:T(8,128)(2,1)S(1)} copy(bf16[32,64,128]{2,1,0:T(8,128)(2,1)} %param.7) | data formatting | bytes 1048576 | tf_op jit(solution)/shard_map/optimization_barrier | solution.py:228
  12.7 10.6 %collective-permute-start.2 = (bf16[64,32,128]{2,1,0:T(8,128)(2,1)S(1)}, bf16[64,32,128]{2,1,0:T(8,128)(2,1)S(1)}, u32[]{:S(2)}, u32[]{:S(2)}) collective-permute-start(bf16[64,32,128]{2,1,0:T(8,128)(2,1)S(1)} %bitcast.34), channel_id=1, source_target_pairs={{0,2},{2,0},{1,3},{3,1},{4,6},{6,4},{5,7},{7,5},{8,10},{10,8},{9,1... | collective-permute-start | bytes 1572872 | tf_op jit(solution)/shard_map/ppermute | solution.py:19
  23.3 0.0 copy-start.3
  23.3 0.0 copy-start.4
  23.3 0.6 maximum_dynamic-update-slice_fusion.refs_0_
  23.9 2.7 %collective-permute-start.4 = (bf16[66,32,128]{2,1,0:T(8,128)(2,1)}, bf16[66,32,128]{2,1,0:T(8,128)(2,1)S(1)}, u32[]{:S(2)}, u32[]{:S(2)}) collective-permute-start(bf16[66,32,128]{2,1,0:T(8,128)(2,1)} %maximum_dynamic-update-slice_fusion.refs_0_), channel_id=1, source_target_pairs={{0,12},{4,0},{8,4},{12,8},{1,13},{5,1},{9,5},{13,9},{2,14},{6,2},{... | collective-permute-start | bytes 1622024 | tf_op jit(solution)/shard_map/ppermute | solution.py:19
  26.6 3.0 %collective-permute-start.5 = (bf16[66,32,128]{2,1,0:T(8,128)(2,1)}, bf16[66,32,128]{2,1,0:T(8,128)(2,1)S(1)}, u32[]{:S(2)}, u32[]{:S(2)}) collective-permute-start(bf16[66,32,128]{2,1,0:T(8,128)(2,1)} %maximum_dynamic-update-slice_fusion.refs_0_), channel_id=1, source_target_pairs={{0,8},{4,12},{8,0},{12,4},{1,9},{5,13},{9,1},{13,5},{2,10},{6,14},... | collective-permute-start | bytes 1622024 | tf_op jit(solution)/shard_map/ppermute | solution.py:19
  29.7 4.0 %collective-permute-start.6 = (bf16[66,32,128]{2,1,0:T(8,128)(2,1)}, bf16[66,32,128]{2,1,0:T(8,128)(2,1)S(1)}, u32[]{:S(2)}, u32[]{:S(2)}) collective-permute-start(bf16[66,32,128]{2,1,0:T(8,128)(2,1)} %maximum_dynamic-update-slice_fusion.refs_0_), channel_id=1, source_target_pairs={{0,4},{4,8},{8,12},{12,0},{1,5},{5,9},{9,13},{13,1},{2,6},{6,10},{... | collective-permute-start | bytes 1622024 | tf_op jit(solution)/shard_map/ppermute | solution.py:19
  33.7 2.0 %shard_map.111.refs_1_ = f32[64,8,128]{2,1,0:T(8,128)} custom-call(s32[64,128]{1,0:T(8,128)} %mat_ref.3, bf16[40,128]{1,0:T(8,128)(2,1)} %copy-done.4, bf16[40,128]{1,0:T(8,128)(2,1)} %copy-done.3, f32[12]{0:T(128)} %rho_ref.1, bf16[1,12]{1,0:T(2,128)(2,1)} %bitcast.42, bf16[1,12]{1,0:T(2,128)(2,1)} %bitcast.43, f32[12]{0:T(128)} %dd_ref.1), custom_call_target="tpu_custom_call" | custom-call | flops 1000000 | bytes 1000000 | tf_op jit(solution)/shard_map/pallas_call | solution.py:93
  35.7 0.9 copy-done
  36.7 1.0 copy-done.2
  37.7 2.0 %shard_map.112 = (bf16[8,192,1024]{2,1,0:T(8,128)(2,1)S(1)}, bf16[64,32,128]{2,1,0:T(8,128)(2,1)S(1)}, bf16[64,32,128]{2,1,0:T(8,128)(2,1)S(1)}) custom-call(bf16[66,32,128]{2,1,0:T(8,128)(2,1)S(1)} %copy-done.2, f32[64,8,128]{2,1,0:T(8,128)S(1)} %copy-done), custom_call_target="tpu_custom_call" | custom-call | flops 400000000 | bytes 4000000 | tf_op jit(solution)/shard_map/pallas_call | solution.py:200
  39.7 1.4 %copy_bitcast_fusion = (bf16[32,64,128]{2,1,0:T(8,128)(2,1)}, bf16[32,64,128]{2,1,0:T(8,128)(2,1)}) fusion(bf16[64,32,128]{2,1,0:T(8,128)(2,1)S(1)} %get-tuple-element.31, bf16[64,32,128]{2,1,0:T(8,128)(2,1)S(1)} %get-tuple-element.30), kind=kLoop, calls=%fused_computation | loop fusion | bytes 2097152 | tf_op jit(solution)/shard_map/transpose | solution.py:240
  41.1 0.0 collective-permute-done.2.refs_4_
  41.1 1.9 %collective-permute-start.3 = (bf16[64,32,128]{2,1,0:T(8,128)(2,1)S(1)}, bf16[64,32,128]{2,1,0:T(8,128)(2,1)S(1)}, u32[]{:S(2)}, u32[]{:S(2)}) collective-permute-start(bf16[64,32,128]{2,1,0:T(8,128)(2,1)S(1)} %collective-permute-done.2.refs_4_), channel_id=1, source_target_pairs={{0,1},{1,0},{2,3},{3,2},{4,5},{5,4},{6,7},{7,6},{8,9},{9,8},{10,11... | collective-permute-start | bytes 1572872 | tf_op jit(solution)/shard_map/ppermute | solution.py:19
  43.0 2.4 %collective-permute-start.7 = (bf16[64,32,128]{2,1,0:T(8,128)(2,1)S(1)}, bf16[64,32,128]{2,1,0:T(8,128)(2,1)S(1)}, u32[]{:S(2)}, u32[]{:S(2)}) collective-permute-start(bf16[64,32,128]{2,1,0:T(8,128)(2,1)S(1)} %bitcast.35), channel_id=1, source_target_pairs={{0,1},{1,0},{2,3},{3,2},{4,5},{5,4},{6,7},{7,6},{8,9},{9,8},{10,11... | collective-permute-start | bytes 1572872 | tf_op jit(solution)/shard_map/ppermute | solution.py:19
  45.4 6.6 %collective-permute-done.4.refs_0_ = bf16[66,32,128]{2,1,0:T(8,128)(2,1)S(1)} collective-permute-done((bf16[66,32,128]{2,1,0:T(8,128)(2,1)}, bf16[66,32,128]{2,1,0:T(8,128)(2,1)S(1)}, u32[]{:S(2)}, u32[]{:S(2)}) %collective-permute-start.4) | collective-permute-done | bytes 540704 | tf_op jit(solution)/shard_map/ppermute | solution.py:19
  52.0 2.5 %collective-permute-done.6.refs_0_ = bf16[66,32,128]{2,1,0:T(8,128)(2,1)S(1)} collective-permute-done((bf16[66,32,128]{2,1,0:T(8,128)(2,1)}, bf16[66,32,128]{2,1,0:T(8,128)(2,1)S(1)}, u32[]{:S(2)}, u32[]{:S(2)}) %collective-permute-start.6) | collective-permute-done | bytes 540704 | tf_op jit(solution)/shard_map/ppermute | solution.py:19
  54.5 3.2 %shard_map.113.refs_6_ = f32[8,48,128]{2,1,0:T(8,128)S(1)} custom-call(bf16[66,32,128]{2,1,0:T(8,128)(2,1)S(1)} %collective-permute-done.4.refs_0_, f32[64,8,128]{2,1,0:T(8,128)S(1)} %copy-done.1, bf16[64,32,128]{2,1,0:T(8,128)(2,1)S(1)} %bitcast.36, bf16[64,32,128]{2,1,0:T(8,128)(2,1)S(1)} %collective-permute-done.7.refs_3_, ...), custom_call_target="tpu_custom_call" | custom-call | flops 400000000 | bytes 4000000 | tf_op jit(solution)/shard_map/pallas_call | solution.py:213
  57.7 2.8 %shard_map.114.refs_6_ = f32[8,48,128]{2,1,0:T(8,128)S(1)} custom-call(bf16[66,32,128]{2,1,0:T(8,128)(2,1)S(1)} %collective-permute-done.6.refs_0_, f32[64,8,128]{2,1,0:T(8,128)S(1)} %copy-done.1, bf16[64,32,128]{2,1,0:T(8,128)(2,1)S(1)} %bitcast.37, bf16[64,32,128]{2,1,0:T(8,128)(2,1)S(1)} %collective-permute-done.7.refs_3_, ...), custom_call_target="tpu_custom_call", output_to_operand_aliasing={{}: (6, {})} | custom-call | flops 400000000 | bytes 4000000 | tf_op jit(solution)/shard_map/pallas_call | solution.py:213
  60.5 2.6 %shard_map.115 = f32[8,48,128]{2,1,0:T(8,128)S(1)} custom-call(bf16[66,32,128]{2,1,0:T(8,128)(2,1)S(1)} %collective-permute-done.5.refs_0_, f32[64,8,128]{2,1,0:T(8,128)S(1)} %copy-done.1, bf16[64,32,128]{2,1,0:T(8,128)(2,1)S(1)} %bitcast.38, bf16[64,32,128]{2,1,0:T(8,128)(2,1)S(1)} %collective-permute-done.7.refs_3_, ...), custom_call_target="tpu_custom_call", output_to_operand_aliasing={{}: (6, {})} | custom-call | flops 400000000 | bytes 4000000 | tf_op jit(solution)/shard_map/pallas_call | solution.py:213
  63.1 18.2 %all_to_all.15 = f32[8,48,128]{2,1,0:T(8,128)S(1)} all-to-all(f32[8,48,128]{2,1,0:T(8,128)S(1)} %shard_map.115), channel_id=1, replica_groups=mesh['y'=8,'zl'=4,'x'=4,'zh'=2,'c'=2] {'y'}, dimensions={0} | all-to-all | bytes 393216 | tf_op jit(solution)/shard_map/all_to_all | solution.py:248
  81.4 15.7 %all_to_all.16 = f32[16,12,128]{2,1,0:T(8,128)S(1)} all-to-all(f32[16,12,128]{2,1,0:T(8,128)S(1)} %bitcast.41), channel_id=1, replica_groups=mesh['y'=8,'zl'=4,'x'=4,'zh'=2,'c'=2] {'x','zl'}, dimensions={0} | all-to-all | bytes 196608 | tf_op jit(solution)/shard_map/all_to_all | solution.py:250
  97.2 12.2 %all_to_all.17 = f32[8,48,128]{2,1,0:T(8,128)S(1)} all-to-all(f32[8,48,128]{2,1,0:T(8,128)S(1)} %broadcast_in_dim.25), channel_id=1, replica_groups=mesh['y'=8,'zl'=4,'x'=4,'zh'=2,'c'=2] {'y'}, dimensions={0} | all-to-all | bytes 393216 | tf_op jit(solution)/shard_map/all_to_all | solution.py:252
  109.3 0.1 copy_multiply_fusion
  109.4 0.1 copy.54
  109.6 0.1 mul.19
  109.6 0.7 slice_bitcast_fusion
  (19 shorter events, 0.1 us)
Async XLA Ops:
  5.1 18.2 %collective-permute-start.1 = (bf16[40,128]{1,0:T(8,128)(2,1)}, bf16[40,128]{1,0:T(8,128)(2,1)S(1)}, u32[]{:S(2)}, u32[]{:S(2)}) collective-permute-start(bf16[40,128]{1,0:T(8,128)(2,1)} %get-tuple-element.26), channel_id=1, source_target_pairs={{16,0},{32,16},{48,32},{64,48},{80,64},{96,80},{112,96},{128,112},... | collective-permute-start | bytes 30728 | tf_op jit(solution)/shard_map/ppermute | solution.py:234
  6.4 16.9 %collective-permute-start = (bf16[40,128]{1,0:T(8,128)(2,1)}, bf16[40,128]{1,0:T(8,128)(2,1)S(1)}, u32[]{:S(2)}, u32[]{:S(2)}) collective-permute-start(bf16[40,128]{1,0:T(8,128)(2,1)} %get-tuple-element.25), channel_id=1, source_target_pairs={{0,16},{16,32},{32,48},{48,64},{64,80},{80,96},{96,112},{112,128},... | collective-permute-start | bytes 30728 | tf_op jit(solution)/shard_map/ppermute | solution.py:233
  12.7 28.4 %collective-permute-start.2 = (bf16[64,32,128]{2,1,0:T(8,128)(2,1)S(1)}, bf16[64,32,128]{2,1,0:T(8,128)(2,1)S(1)}, u32[]{:S(2)}, u32[]{:S(2)}) collective-permute-start(bf16[64,32,128]{2,1,0:T(8,128)(2,1)S(1)} %bitcast.34), channel_id=1, source_target_pairs={{0,2},{2,0},{1,3},{3,1},{4,6},{6,4},{5,7},{7,5},{8,10},{10,8},{9,1... | collective-permute-start | bytes 1572872 | tf_op jit(solution)/shard_map/ppermute | solution.py:19
  23.3 10.4 %copy-start.3 = (bf16[40,128]{1,0:T(8,128)(2,1)}, bf16[40,128]{1,0:T(8,128)(2,1)S(1)}, u32[]{:S(2)}) copy-start(bf16[40,128]{1,0:T(8,128)(2,1)S(1)} %collective-permute-done.1.right_ref) | copy-start | bytes 30724
  23.3 10.4 %copy-start.4 = (bf16[40,128]{1,0:T(8,128)(2,1)}, bf16[40,128]{1,0:T(8,128)(2,1)S(1)}, u32[]{:S(2)}) copy-start(bf16[40,128]{1,0:T(8,128)(2,1)S(1)} %collective-permute-done.left_ref) | copy-start | bytes 30724
  23.9 28.1 %collective-permute-start.4 = (bf16[66,32,128]{2,1,0:T(8,128)(2,1)}, bf16[66,32,128]{2,1,0:T(8,128)(2,1)S(1)}, u32[]{:S(2)}, u32[]{:S(2)}) collective-permute-start(bf16[66,32,128]{2,1,0:T(8,128)(2,1)} %maximum_dynamic-update-slice_fusion.refs_0_), channel_id=1, source_target_pairs={{0,12},{4,0},{8,4},{12,8},{1,13},{5,1},{9,5},{13,9},{2,14},{6,2},{... | collective-permute-start | bytes 1622024 | tf_op jit(solution)/shard_map/ppermute | solution.py:19
  26.6 25.3 %collective-permute-start.5 = (bf16[66,32,128]{2,1,0:T(8,128)(2,1)}, bf16[66,32,128]{2,1,0:T(8,128)(2,1)S(1)}, u32[]{:S(2)}, u32[]{:S(2)}) collective-permute-start(bf16[66,32,128]{2,1,0:T(8,128)(2,1)} %maximum_dynamic-update-slice_fusion.refs_0_), channel_id=1, source_target_pairs={{0,8},{4,12},{8,0},{12,4},{1,9},{5,13},{9,1},{13,5},{2,10},{6,14},... | collective-permute-start | bytes 1622024 | tf_op jit(solution)/shard_map/ppermute | solution.py:19
  29.7 24.8 %collective-permute-start.6 = (bf16[66,32,128]{2,1,0:T(8,128)(2,1)}, bf16[66,32,128]{2,1,0:T(8,128)(2,1)S(1)}, u32[]{:S(2)}, u32[]{:S(2)}) collective-permute-start(bf16[66,32,128]{2,1,0:T(8,128)(2,1)} %maximum_dynamic-update-slice_fusion.refs_0_), channel_id=1, source_target_pairs={{0,4},{4,8},{8,12},{12,0},{1,5},{5,9},{9,13},{13,1},{2,6},{6,10},{... | collective-permute-start | bytes 1622024 | tf_op jit(solution)/shard_map/ppermute | solution.py:19
  35.7 0.9 copy-start
  36.7 1.0 copy-start.2
  37.7 16.8 %copy-start.1 = (f32[64,8,128]{2,1,0:T(8,128)S(1)}, f32[64,8,128]{2,1,0:T(8,128)}, u32[]{:S(2)}) copy-start(f32[64,8,128]{2,1,0:T(8,128)} %shard_map.111.refs_1_) | copy-start | bytes 786436
  41.1 13.4 %collective-permute-start.3 = (bf16[64,32,128]{2,1,0:T(8,128)(2,1)S(1)}, bf16[64,32,128]{2,1,0:T(8,128)(2,1)S(1)}, u32[]{:S(2)}, u32[]{:S(2)}) collective-permute-start(bf16[64,32,128]{2,1,0:T(8,128)(2,1)S(1)} %collective-permute-done.2.refs_4_), channel_id=1, source_target_pairs={{0,1},{1,0},{2,3},{3,2},{4,5},{5,4},{6,7},{7,6},{8,9},{9,8},{10,11... | collective-permute-start | bytes 1572872 | tf_op jit(solution)/shard_map/ppermute | solution.py:19
  43.0 11.5 %collective-permute-start.7 = (bf16[64,32,128]{2,1,0:T(8,128)(2,1)S(1)}, bf16[64,32,128]{2,1,0:T(8,128)(2,1)S(1)}, u32[]{:S(2)}, u32[]{:S(2)}) collective-permute-start(bf16[64,32,128]{2,1,0:T(8,128)(2,1)S(1)} %bitcast.35), channel_id=1, source_target_pairs={{0,1},{1,0},{2,3},{3,2},{4,5},{5,4},{6,7},{7,6},{8,9},{9,8},{10,11... | collective-permute-start | bytes 1572872 | tf_op jit(solution)/shard_map/ppermute | solution.py:19

commit v9 on v8

--- a/solution.py
+++ b/solution.py
@@ -240,7 +240,7 @@
     mass, stiff = (with_layout_constraint(v.transpose(1, 0, 2), rowwise) for v in (mass, stiff))
     f, other, terms, mass, stiff = lax.optimization_barrier((f, other, terms, mass, stiff))
     other_core = shifted(other, "c", 1)
-    other_core, panels[1:] = lax.optimization_barrier((other_core, panels[1:]))
+    other_core, panels[1], panels[3] = lax.optimization_barrier((other_core, panels[1], panels[3]))
     olds = (old, old_core, other, other_core)
     parts = panel(1, panels[1], f, olds, terms)
     for d in (3, 2):

time: 112 us -> 118 us (1.054)
  blocking collectives: 46.1 us -> 52.7 us
    all_to_all x1, blocking collectives: 18.2 us -> 24.9 us  [local(): lax.all_to_all(parts, 'y', 0, 0)]
    unnamed x11 -> x9, local copies, waits for them, and re-layouts: 4.19 us -> 3.14 us
  transfers between devices with their start and end apart: 8 -> 8, of which waited for: 2 -> 1; matrix products, arithmetic and copies ran while one was open for 3% -> 3% of each run, Pallas kernels for 4% -> 9%
where the time goes in v9:
time: 118 us; the launch traced here: 117 us
  blocking collectives  52.7 us (45%)
  starting transfers between devices  30.2 us (26%)
  Pallas kernels  15.9 us (13%)
  waiting for transfers between devices  9.66 us (8%)
  local copies, waits for them, and re-layouts  6.83 us (6%)
    all_to_all x1, blocking collectives, local(): lax.all_to_all(parts, 'y', 0, 0)  24.9 us
    ppermute x6, starting transfers between devices, shifted(): return lax.ppermute(value, axis, [(i, (i + step) % n) for i in range(n)])  24 us
    all_to_all x1, blocking collectives, local(): parts = lax.all_to_all(parts, ('x', 'zl'), 0, 0).reshape(4, 4, PIECE, 4 * M)  15.6 us
    all_to_all x1, blocking collectives, local(): lax.all_to_all(jnp.broadcast_to(parts, (8, 4 * PIECE, 4 * M)), 'y', 0, 0)  12.2 us
    ppermute x6, waiting for transfers between devices, shifted(): return lax.ppermute(value, axis, [(i, (i + step) % n) for i in range(n)])  9.65 us
    pallas_call x3, Pallas kernels, panel(): pl.pallas_call(lambda *refs: panel_kernel(d, *refs), out_shape=jax.ShapeD...  8.59 us
    ppermute x1, starting transfers between devices, local(): left = lax.ppermute(last, SPACE, [(i, i + 1) for i in range(n - 1)])  4.9 us
    unnamed x9, local copies, waits for them, and re-layouts  3.14 us
  transfers between devices with their start and end apart: 8, of which 1 were waited for; matrix products, arithmetic and copies ran while one was open for 3% of the time, Pallas kernels for 9%

profile of v9, /device:TPU:6, one launch (start us, length us, event | category | flops | bytes accessed | tf_op | source)
XLA Modules:
  0.0 117.0 jit_solution(9540042244275156274)
XLA Ops:
  0.6 2.2 %copy.64 = bf16[32,64,128]{2,0,1:T(8,128)(2,1)} copy(bf16[32,64,128]{2,1,0:T(8,128)(2,1)} %param.8) | data formatting | bytes 1048576 | tf_op args[1]
  2.8 2.3 %shard_map.110 = (bf16[40,128]{1,0:T(8,128)(2,1)}, bf16[40,128]{1,0:T(8,128)(2,1)}, bf16[66,32,128]{2,1,0:T(8,128)(2,1)}) custom-call(bf16[64,32,128]{2,1,0:T(8,128)(2,1)} %bitcast.39, s32[64,128]{1,0:T(8,128)} %mat_ref.3), custom_call_target="tpu_custom_call" | custom-call | flops 1000000 | bytes 1000000 | tf_op jit(solution)/shard_map/pallas_call | solution.py:48
  5.1 1.3 %collective-permute-start.1 = (bf16[40,128]{1,0:T(8,128)(2,1)}, bf16[40,128]{1,0:T(8,128)(2,1)S(1)}, u32[]{:S(2)}, u32[]{:S(2)}) collective-permute-start(bf16[40,128]{1,0:T(8,128)(2,1)} %get-tuple-element.26), channel_id=1, source_target_pairs={{16,0},{32,16},{48,32},{64,48},{80,64},{96,80},{112,96},{128,112},... | collective-permute-start | bytes 30728 | tf_op jit(solution)/shard_map/ppermute | solution.py:234
  6.4 4.9 %collective-permute-start = (bf16[40,128]{1,0:T(8,128)(2,1)}, bf16[40,128]{1,0:T(8,128)(2,1)S(1)}, u32[]{:S(2)}, u32[]{:S(2)}) collective-permute-start(bf16[40,128]{1,0:T(8,128)(2,1)} %get-tuple-element.25), channel_id=1, source_target_pairs={{0,16},{16,32},{32,48},{48,64},{64,80},{80,96},{96,112},{112,128},... | collective-permute-start | bytes 30728 | tf_op jit(solution)/shard_map/ppermute | solution.py:233
  11.3 1.4 %copy.63 = bf16[32,64,128]{2,0,1:T(8,128)(2,1)S(1)} copy(bf16[32,64,128]{2,1,0:T(8,128)(2,1)} %param.7) | data formatting | bytes 1048576 | tf_op jit(solution)/shard_map/optimization_barrier | solution.py:228
  12.7 10.6 %collective-permute-start.3 = (bf16[64,32,128]{2,1,0:T(8,128)(2,1)S(1)}, bf16[64,32,128]{2,1,0:T(8,128)(2,1)S(1)}, u32[]{:S(2)}, u32[]{:S(2)}) collective-permute-start(bf16[64,32,128]{2,1,0:T(8,128)(2,1)S(1)} %bitcast.34), channel_id=1, source_target_pairs={{0,2},{2,0},{1,3},{3,1},{4,6},{6,4},{5,7},{7,5},{8,10},{10,8},{9,1... | collective-permute-start | bytes 1572872 | tf_op jit(solution)/shard_map/ppermute | solution.py:19
  23.2 0.0 copy-start.2
  23.3 0.0 copy-start.3
  23.3 0.6 maximum_dynamic-update-slice_fusion.refs_0_
  23.9 2.7 %collective-permute-start.6 = (bf16[66,32,128]{2,1,0:T(8,128)(2,1)}, bf16[66,32,128]{2,1,0:T(8,128)(2,1)S(1)}, u32[]{:S(2)}, u32[]{:S(2)}) collective-permute-start(bf16[66,32,128]{2,1,0:T(8,128)(2,1)} %maximum_dynamic-update-slice_fusion.refs_0_), channel_id=1, source_target_pairs={{0,12},{4,0},{8,4},{12,8},{1,13},{5,1},{9,5},{13,9},{2,14},{6,2},{... | collective-permute-start | bytes 1622024 | tf_op jit(solution)/shard_map/ppermute | solution.py:19
  26.6 4.3 %collective-permute-start.7 = (bf16[66,32,128]{2,1,0:T(8,128)(2,1)}, bf16[66,32,128]{2,1,0:T(8,128)(2,1)S(1)}, u32[]{:S(2)}, u32[]{:S(2)}) collective-permute-start(bf16[66,32,128]{2,1,0:T(8,128)(2,1)} %maximum_dynamic-update-slice_fusion.refs_0_), channel_id=1, source_target_pairs={{0,4},{4,8},{8,12},{12,0},{1,5},{5,9},{9,13},{13,1},{2,6},{6,10},{... | collective-permute-start | bytes 1622024 | tf_op jit(solution)/shard_map/ppermute | solution.py:19
  31.0 2.0 %shard_map.111.refs_1_ = f32[64,8,128]{2,1,0:T(8,128)} custom-call(s32[64,128]{1,0:T(8,128)} %mat_ref.3, bf16[40,128]{1,0:T(8,128)(2,1)} %copy-done.3, bf16[40,128]{1,0:T(8,128)(2,1)} %copy-done.2, f32[12]{0:T(128)} %rho_ref.1, bf16[1,12]{1,0:T(2,128)(2,1)} %bitcast.42, bf16[1,12]{1,0:T(2,128)(2,1)} %bitcast.43, f32[12]{0:T(128)} %dd_ref.1), custom_call_target="tpu_custom_call" | custom-call | flops 1000000 | bytes 1000000 | tf_op jit(solution)/shard_map/pallas_call | solution.py:93
  33.0 0.9 copy-done
  34.0 3.1 %shard_map.112 = (bf16[8,192,1024]{2,1,0:T(8,128)(2,1)S(1)}, bf16[64,32,128]{2,1,0:T(8,128)(2,1)S(1)}, bf16[64,32,128]{2,1,0:T(8,128)(2,1)S(1)}) custom-call(bf16[66,32,128]{2,1,0:T(8,128)(2,1)} %maximum_dynamic-update-slice_fusion.refs_0_, f32[64,8,128]{2,1,0:T(8,128)S(1)} %copy-done), custom_call_target="tpu_custom_call" | custom-call | flops 400000000 | bytes 4000000 | tf_op jit(solution)/shard_map/pallas_call | solution.py:200
  37.0 1.4 %copy_bitcast_fusion = (bf16[32,64,128]{2,1,0:T(8,128)(2,1)}, bf16[32,64,128]{2,1,0:T(8,128)(2,1)}) fusion(bf16[64,32,128]{2,1,0:T(8,128)(2,1)S(1)} %get-tuple-element.30, bf16[64,32,128]{2,1,0:T(8,128)(2,1)S(1)} %get-tuple-element.29), kind=kLoop, calls=%fused_computation | loop fusion | bytes 2097152 | tf_op jit(solution)/shard_map/transpose | solution.py:240
  38.4 0.0 collective-permute-done.3.refs_4_
  38.4 1.9 %collective-permute-start.5 = (bf16[64,32,128]{2,1,0:T(8,128)(2,1)S(1)}, bf16[64,32,128]{2,1,0:T(8,128)(2,1)S(1)}, u32[]{:S(2)}, u32[]{:S(2)}) collective-permute-start(bf16[64,32,128]{2,1,0:T(8,128)(2,1)S(1)} %collective-permute-done.3.refs_4_), channel_id=1, source_target_pairs={{0,1},{1,0},{2,3},{3,2},{4,5},{5,4},{6,7},{7,6},{8,9},{9,8},{10,11... | collective-permute-start | bytes 1572872 | tf_op jit(solution)/shard_map/ppermute | solution.py:19
  40.3 2.4 %collective-permute-start.4 = (bf16[64,32,128]{2,1,0:T(8,128)(2,1)S(1)}, bf16[64,32,128]{2,1,0:T(8,128)(2,1)S(1)}, u32[]{:S(2)}, u32[]{:S(2)}) collective-permute-start(bf16[64,32,128]{2,1,0:T(8,128)(2,1)S(1)} %bitcast.35), channel_id=1, source_target_pairs={{0,1},{1,0},{2,3},{3,2},{4,5},{5,4},{6,7},{7,6},{8,9},{9,8},{10,11... | collective-permute-start | bytes 1572872 | tf_op jit(solution)/shard_map/ppermute | solution.py:19
  42.7 2.1 %collective-permute-start.2 = (bf16[66,32,128]{2,1,0:T(8,128)(2,1)}, bf16[66,32,128]{2,1,0:T(8,128)(2,1)S(1)}, u32[]{:S(2)}, u32[]{:S(2)}) collective-permute-start(bf16[66,32,128]{2,1,0:T(8,128)(2,1)} %maximum_dynamic-update-slice_fusion.refs_0_), channel_id=1, source_target_pairs={{0,8},{4,12},{8,0},{12,4},{1,9},{5,13},{9,1},{13,5},{2,10},{6,14},... | collective-permute-start | bytes 1622024 | tf_op jit(solution)/shard_map/ppermute | solution.py:19
  44.9 0.0 collective-permute-done.5.refs_5_
  44.9 0.0 collective-permute-done.4.refs_3_
  44.9 3.2 %shard_map.113.refs_6_ = f32[8,48,128]{2,1,0:T(8,128)S(1)} custom-call(bf16[66,32,128]{2,1,0:T(8,128)(2,1)S(1)} %collective-permute-done.6.refs_0_, f32[64,8,128]{2,1,0:T(8,128)S(1)} %copy-done.1, bf16[64,32,128]{2,1,0:T(8,128)(2,1)S(1)} %bitcast.36, bf16[64,32,128]{2,1,0:T(8,128)(2,1)S(1)} %collective-permute-done.4.refs_3_, ...), custom_call_target="tpu_custom_call" | custom-call | flops 400000000 | bytes 4000000 | tf_op jit(solution)/shard_map/pallas_call | solution.py:213
  48.1 2.8 %shard_map.114.refs_6_ = f32[8,48,128]{2,1,0:T(8,128)S(1)} custom-call(bf16[66,32,128]{2,1,0:T(8,128)(2,1)S(1)} %collective-permute-done.7.refs_0_, f32[64,8,128]{2,1,0:T(8,128)S(1)} %copy-done.1, bf16[64,32,128]{2,1,0:T(8,128)(2,1)S(1)} %bitcast.37, bf16[64,32,128]{2,1,0:T(8,128)(2,1)S(1)} %collective-permute-done.4.refs_3_, ...), custom_call_target="tpu_custom_call", output_to_operand_aliasing={{}: (6, {})} | custom-call | flops 400000000 | bytes 4000000 | tf_op jit(solution)/shard_map/pallas_call | solution.py:213
  50.9 9.6 %collective-permute-done.2.refs_0_ = bf16[66,32,128]{2,1,0:T(8,128)(2,1)S(1)} collective-permute-done((bf16[66,32,128]{2,1,0:T(8,128)(2,1)}, bf16[66,32,128]{2,1,0:T(8,128)(2,1)S(1)}, u32[]{:S(2)}, u32[]{:S(2)}) %collective-permute-start.2) | collective-permute-done | bytes 540704 | tf_op jit(solution)/shard_map/ppermute | solution.py:19
  60.5 2.6 %shard_map.115 = f32[8,48,128]{2,1,0:T(8,128)S(1)} custom-call(bf16[66,32,128]{2,1,0:T(8,128)(2,1)S(1)} %collective-permute-done.2.refs_0_, f32[64,8,128]{2,1,0:T(8,128)S(1)} %copy-done.1, bf16[64,32,128]{2,1,0:T(8,128)(2,1)S(1)} %bitcast.38, bf16[64,32,128]{2,1,0:T(8,128)(2,1)S(1)} %collective-permute-done.4.refs_3_, ...), custom_call_target="tpu_custom_call", output_to_operand_aliasing={{}: (6, {})} | custom-call | flops 400000000 | bytes 4000000 | tf_op jit(solution)/shard_map/pallas_call | solution.py:213
  63.2 24.9 %all_to_all.15 = f32[8,48,128]{2,1,0:T(8,128)S(1)} all-to-all(f32[8,48,128]{2,1,0:T(8,128)S(1)} %shard_map.115), channel_id=1, replica_groups=mesh['y'=8,'zl'=4,'x'=4,'zh'=2,'c'=2] {'y'}, dimensions={0} | all-to-all | bytes 393216 | tf_op jit(solution)/shard_map/all_to_all | solution.py:248
  88.1 15.6 %all_to_all.16 = f32[16,12,128]{2,1,0:T(8,128)S(1)} all-to-all(f32[16,12,128]{2,1,0:T(8,128)S(1)} %bitcast.41), channel_id=1, replica_groups=mesh['y'=8,'zl'=4,'x'=4,'zh'=2,'c'=2] {'x','zl'}, dimensions={0} | all-to-all | bytes 196608 | tf_op jit(solution)/shard_map/all_to_all | solution.py:250
  103.8 12.2 %all_to_all.17 = f32[8,48,128]{2,1,0:T(8,128)S(1)} all-to-all(f32[8,48,128]{2,1,0:T(8,128)S(1)} %broadcast_in_dim.25), channel_id=1, replica_groups=mesh['y'=8,'zl'=4,'x'=4,'zh'=2,'c'=2] {'y'}, dimensions={0} | all-to-all | bytes 393216 | tf_op jit(solution)/shard_map/all_to_all | solution.py:252
  116.0 0.1 copy_multiply_fusion
  116.1 0.1 copy.54
  116.2 0.1 mul.19
  116.3 0.7 slice_bitcast_fusion
  (17 shorter events, 0.1 us)
Async XLA Ops:
  5.1 18.2 %collective-permute-start.1 = (bf16[40,128]{1,0:T(8,128)(2,1)}, bf16[40,128]{1,0:T(8,128)(2,1)S(1)}, u32[]{:S(2)}, u32[]{:S(2)}) collective-permute-start(bf16[40,128]{1,0:T(8,128)(2,1)} %get-tuple-element.26), channel_id=1, source_target_pairs={{16,0},{32,16},{48,32},{64,48},{80,64},{96,80},{112,96},{128,112},... | collective-permute-start | bytes 30728 | tf_op jit(solution)/shard_map/ppermute | solution.py:234
  6.4 16.9 %collective-permute-start = (bf16[40,128]{1,0:T(8,128)(2,1)}, bf16[40,128]{1,0:T(8,128)(2,1)S(1)}, u32[]{:S(2)}, u32[]{:S(2)}) collective-permute-start(bf16[40,128]{1,0:T(8,128)(2,1)} %get-tuple-element.25), channel_id=1, source_target_pairs={{0,16},{16,32},{32,48},{48,64},{64,80},{80,96},{96,112},{112,128},... | collective-permute-start | bytes 30728 | tf_op jit(solution)/shard_map/ppermute | solution.py:233
  12.7 25.7 %collective-permute-start.3 = (bf16[64,32,128]{2,1,0:T(8,128)(2,1)S(1)}, bf16[64,32,128]{2,1,0:T(8,128)(2,1)S(1)}, u32[]{:S(2)}, u32[]{:S(2)}) collective-permute-start(bf16[64,32,128]{2,1,0:T(8,128)(2,1)S(1)} %bitcast.34), channel_id=1, source_target_pairs={{0,2},{2,0},{1,3},{3,1},{4,6},{6,4},{5,7},{7,5},{8,10},{10,8},{9,1... | collective-permute-start | bytes 1572872 | tf_op jit(solution)/shard_map/ppermute | solution.py:19
  23.2 7.7 %copy-start.2 = (bf16[40,128]{1,0:T(8,128)(2,1)}, bf16[40,128]{1,0:T(8,128)(2,1)S(1)}, u32[]{:S(2)}) copy-start(bf16[40,128]{1,0:T(8,128)(2,1)S(1)} %collective-permute-done.1.right_ref) | copy-start | bytes 30724
  23.3 7.7 %copy-start.3 = (bf16[40,128]{1,0:T(8,128)(2,1)}, bf16[40,128]{1,0:T(8,128)(2,1)S(1)}, u32[]{:S(2)}) copy-start(bf16[40,128]{1,0:T(8,128)(2,1)S(1)} %collective-permute-done.left_ref) | copy-start | bytes 30724
  23.9 20.9 %collective-permute-start.6 = (bf16[66,32,128]{2,1,0:T(8,128)(2,1)}, bf16[66,32,128]{2,1,0:T(8,128)(2,1)S(1)}, u32[]{:S(2)}, u32[]{:S(2)}) collective-permute-start(bf16[66,32,128]{2,1,0:T(8,128)(2,1)} %maximum_dynamic-update-slice_fusion.refs_0_), channel_id=1, source_target_pairs={{0,12},{4,0},{8,4},{12,8},{1,13},{5,1},{9,5},{13,9},{2,14},{6,2},{... | collective-permute-start | bytes 1622024 | tf_op jit(solution)/shard_map/ppermute | solution.py:19
  26.6 18.2 %collective-permute-start.7 = (bf16[66,32,128]{2,1,0:T(8,128)(2,1)}, bf16[66,32,128]{2,1,0:T(8,128)(2,1)S(1)}, u32[]{:S(2)}, u32[]{:S(2)}) collective-permute-start(bf16[66,32,128]{2,1,0:T(8,128)(2,1)} %maximum_dynamic-update-slice_fusion.refs_0_), channel_id=1, source_target_pairs={{0,4},{4,8},{8,12},{12,0},{1,5},{5,9},{9,13},{13,1},{2,6},{6,10},{... | collective-permute-start | bytes 1622024 | tf_op jit(solution)/shard_map/ppermute | solution.py:19
  33.0 0.9 copy-start
  34.0 10.9 %copy-start.1 = (f32[64,8,128]{2,1,0:T(8,128)S(1)}, f32[64,8,128]{2,1,0:T(8,128)}, u32[]{:S(2)}) copy-start(f32[64,8,128]{2,1,0:T(8,128)} %shard_map.111.refs_1_) | copy-start | bytes 786436
  38.4 6.5 %collective-permute-start.5 = (bf16[64,32,128]{2,1,0:T(8,128)(2,1)S(1)}, bf16[64,32,128]{2,1,0:T(8,128)(2,1)S(1)}, u32[]{:S(2)}, u32[]{:S(2)}) collective-permute-start(bf16[64,32,128]{2,1,0:T(8,128)(2,1)S(1)} %collective-permute-done.3.refs_4_), channel_id=1, source_target_pairs={{0,1},{1,0},{2,3},{3,2},{4,5},{5,4},{6,7},{7,6},{8,9},{9,8},{10,11... | collective-permute-start | bytes 1572872 | tf_op jit(solution)/shard_map/ppermute | solution.py:19
  40.3 4.6 %collective-permute-start.4 = (bf16[64,32,128]{2,1,0:T(8,128)(2,1)S(1)}, bf16[64,32,128]{2,1,0:T(8,128)(2,1)S(1)}, u32[]{:S(2)}, u32[]{:S(2)}) collective-permute-start(bf16[64,32,128]{2,1,0:T(8,128)(2,1)S(1)} %bitcast.35), channel_id=1, source_target_pairs={{0,1},{1,0},{2,3},{3,2},{4,5},{5,4},{6,7},{7,6},{8,9},{9,8},{10,11... | collective-permute-start | bytes 1572872 | tf_op jit(solution)/shard_map/ppermute | solution.py:19
  42.7 17.8 %collective-permute-start.2 = (bf16[66,32,128]{2,1,0:T(8,128)(2,1)}, bf16[66,32,128]{2,1,0:T(8,128)(2,1)S(1)}, u32[]{:S(2)}, u32[]{:S(2)}) collective-permute-start(bf16[66,32,128]{2,1,0:T(8,128)(2,1)} %maximum_dynamic-update-slice_fusion.refs_0_), channel_id=1, source_target_pairs={{0,8},{4,12},{8,0},{12,4},{1,9},{5,13},{9,1},{13,5},{2,10},{6,14},... | collective-permute-start | bytes 1622024 | tf_op jit(solution)/shard_map/ppermute | solution.py:19
